TPU v7x, 32 devices: a whole 2x2x4 slice. The times are simulated.
32 devices in a mesh: dp: 16 (over z, y, x), mp: 2 (over core).
Axes of the slice: x: 2, y: 2, z: 4, core: 2. Of those that a mesh axis runs over, the one named last changes fastest.
Arguments:
- tokens: float32 [32768, 384], P(('dp', 'mp')), may hold values from -12 to 12
- condition: float32 [128, 384], P('dp'), may hold values from -12 to 12
- cotangent: float32 [32768, 384], P(('dp', 'mp')), may hold values from -12 to 12
- routes: int32 [32768, 2], P('dp'), may hold values from 0 to 7, as said below
- w_ada: float32 [384, 2304], P('dp'), may hold values from -0.3125 to 0.3125
- ada_first: float32 [384, 2304], P('dp'), may hold values from -1 to 1
- ada_second: float32 [384, 2304], P('dp'), may hold values from 0 to 1, as said below
- w_gate: float32 [384, 8], P('dp'), may hold values from -0.15625 to 0.15625
- gate_first: float32 [384, 8], P('dp'), may hold values from -1 to 1
- gate_second: float32 [384, 8], P('dp'), may hold values from 0 to 1, as said below
- w_attn: float32 [4, 384, 384], P(None, 'dp', 'mp'), may hold values from -4 to 4
- attn_first: float32 [4, 384, 384], P(None, 'dp', 'mp'), may hold values from -1 to 1
- attn_second: float32 [4, 384, 384], P(None, 'dp', 'mp'), may hold values from 0 to 1, as said below
- w_expert: float32 [2, 10, 384, 1536], P(None, None, 'dp', 'mp'), may hold values from -4 to 4
- expert_first: float32 [2, 10, 384, 1536], P(None, None, 'dp', 'mp'), may hold values from -1 to 1
- expert_second: float32 [2, 10, 384, 1536], P(None, None, 'dp', 'mp'), may hold values from 0 to 1, as said below
Outputs:
- output: float32 [32768, 384], P(('dp', 'mp'))
- grad_tokens: float32 [32768, 384], P(('dp', 'mp'))
- grad_norm: float32 [], replicated
- ada_new: float32 [384, 2304], P('dp')
- ada_first_new: float32 [384, 2304], P('dp')
- ada_second_new: float32 [384, 2304], P('dp')
- gate_new: float32 [384, 8], P('dp')
- gate_first_new: float32 [384, 8], P('dp')
- gate_second_new: float32 [384, 8], P('dp')
- attn_new: float32 [4, 384, 384], P(None, 'dp', 'mp')
- attn_first_new: float32 [4, 384, 384], P(None, 'dp', 'mp')
- attn_second_new: float32 [4, 384, 384], P(None, 'dp', 'mp')
- expert_new: float32 [2, 10, 384, 1536], P(None, None, 'dp', 'mp')
- expert_first_new: float32 [2, 10, 384, 1536], P(None, None, 'dp', 'mp')
- expert_second_new: float32 [2, 10, 384, 1536], P(None, None, 'dp', 'mp')
Inputs may be any that keep to these rules, and one draw needn't show every extreme that they name: `routes`: each token names two different routed experts; loads differ from expert to expert and from group to group of 2048 tokens. `ada_second`: positive. `gate_second`: positive. `attn_second`: positive. `expert_second`: positive.
All inputs are finite; a program needn't handle non-finite values.
Results may differ from a plain program's by a relative error of at most 0.015.
The roundings to bfloat16 on the way count: a program that leaves them out, or rounds other values in their place, can miss the bound.
Values may be sent and summed in bfloat16 or wider, within the bound.
A program may use at most 256 MiB of HBM per device.

v0:
```python
import jax
import jax.numpy as jnp
from jax import lax
from jax.sharding import PartitionSpec as P

HD = 64
TOPK = 2
PATCH = 256
BLK = 128
STEP = 10


EPS_NORM = 1e-06
CLIP_NORM = 0.1
RATE = 0.08
BETA_ONE = 0.9
BETA_TWO = 0.95
ADAM_EPS = 1e-08
DECAY = 0.01


def layer_norm(value):
    center = value - jnp.mean(value, axis=-1, keepdims=True)
    inverse = lax.rsqrt(jnp.mean(center * center, axis=-1, keepdims=True) + EPS_NORM)
    return (center * inverse, inverse)


def norm_back(grad, normed, inverse):
    mean_grad = jnp.mean(grad, axis=-1, keepdims=True)
    mean_proj = jnp.mean(grad * normed, axis=-1, keepdims=True)
    return inverse * (grad - mean_grad - normed * mean_proj)


def gelu_back(preact, grad):
    _, pullback = jax.vjp(jax.nn.gelu, preact)
    return pullback(grad)[0]


def adam(master, first, second, grad):
    first_new = BETA_ONE * first + (1.0 - BETA_ONE) * grad
    second_new = BETA_TWO * second + (1.0 - BETA_TWO) * grad * grad
    fix_one = 1.0 - BETA_ONE**STEP
    fix_two = 1.0 - BETA_TWO**STEP
    update = first_new / fix_one / (jnp.sqrt(second_new / fix_two) + ADAM_EPS) + DECAY * master
    return (master - RATE * update, first_new, second_new)


def route_table(routes, experts, block_rows):
    tok_grp = routes.shape[0]
    flat = routes.reshape(-1)
    count_uses = flat.shape[0]
    iota = jnp.arange(experts, dtype=jnp.int32)
    onehot = (flat[:, None] == iota[None, :]).astype(jnp.int32)
    counts = jnp.sum(onehot, axis=0)
    padded = (counts + block_rows - 1) // block_rows * block_rows
    starts = jnp.cumsum(padded) - padded
    ranks = jnp.cumsum(onehot, axis=0) - 1
    slot = jnp.sum(onehot * (starts[None, :] + ranks), axis=1)
    slot_count = tok_grp * TOPK + experts * block_rows
    uses = jnp.arange(count_uses, dtype=jnp.int32)
    owner = jnp.zeros((slot_count,), jnp.int32).at[slot].set(uses)
    filled = jnp.zeros((slot_count,), jnp.int32).at[slot].set(1)
    block_first = jnp.arange(slot_count // block_rows, dtype=jnp.int32) * block_rows
    block_expert = jnp.sum((starts[None, :] <= block_first[:, None]).astype(jnp.int32), axis=1) - 1
    return (slot, owner, filled, block_expert)


def per_device(
    tokens,
    condition,
    cotangent,
    routes,
    w_ada,
    ada_first,
    ada_second,
    w_gate,
    gate_first,
    gate_second,
    w_attn,
    attn_first,
    attn_second,
    w_expert,
    expert_first,
    expert_second,
):
    bf16 = jnp.bfloat16
    f32 = jnp.float32
    tok_dev, width = tokens.shape
    img_grp = condition.shape[0]
    img_own = tok_dev // PATCH
    mp_index = lax.axis_index("mp")
    ada_low, gate_low, attn_low, expert_low = (
        lax.all_gather(w_ada.astype(bf16), "dp", axis=0, tiled=True),
        lax.all_gather(w_gate.astype(bf16), "dp", axis=0, tiled=True),
        lax.all_gather(w_attn.astype(bf16), "dp", axis=1, tiled=True),
        lax.all_gather(w_expert.astype(bf16), "dp", axis=2, tiled=True),
    )
    cond_low = jax.nn.silu(condition).astype(bf16)
    cond_own = lax.dynamic_slice_in_dim(cond_low, mp_index * img_own, img_own, 0)
    modulation = jnp.dot(cond_own, ada_low, preferred_element_type=f32).reshape(
        img_own, 6, 1, width
    )
    shift_one = modulation[:, 0]
    scale_one = modulation[:, 1]
    gate_one = modulation[:, 2]
    shift_two = modulation[:, 3]
    scale_two = modulation[:, 4]
    gate_two = modulation[:, 5]
    x_img = tokens.reshape(img_own, PATCH, width)
    normed_one, inverse_one = layer_norm(x_img)
    h_one = (normed_one * (1.0 + scale_one) + shift_one).astype(bf16).reshape(tok_dev, width)
    h_one_all = lax.all_gather(h_one, "mp", axis=0, tiled=True)
    tok_grp = h_one_all.shape[0]
    local = attn_low.shape[2]
    heads_local = local // HD
    triple = jnp.einsum("td,jdc->jtc", h_one_all, attn_low[:3], preferred_element_type=f32).astype(
        bf16
    )
    head_shape = (img_grp, PATCH, heads_local, HD)
    query = triple[0].reshape(head_shape)
    keys = triple[1].reshape(head_shape)
    values = triple[2].reshape(head_shape)
    scale = HD ** (-0.5)
    scores = jnp.einsum("iqhc,ikhc->ihqk", query, keys, preferred_element_type=f32) * scale
    top = jax.nn.logsumexp(scores, axis=-1, keepdims=True)
    soft_low = jnp.exp(scores - top).astype(bf16)
    mixed = (
        jnp.einsum("ihqk,ikhc->iqhc", soft_low, values, preferred_element_type=f32)
        .astype(bf16)
        .reshape(tok_grp, local)
    )
    out_weight = attn_low[3]
    block = mixed
    attention = lax.psum_scatter(
        jnp.einsum("tc,jc->tj", block, out_weight, preferred_element_type=f32),
        "mp",
        scatter_dimension=0,
        tiled=True,
    )
    attention_img = attention.reshape(img_own, PATCH, width)
    x_one = x_img + gate_one * attention_img
    normed_two, inverse_two = layer_norm(x_one)
    h_two = (normed_two * (1.0 + scale_two) + shift_two).astype(bf16).reshape(tok_dev, width)
    h_two_all = lax.all_gather(h_two, "mp", axis=0, tiled=True)
    experts = gate_low.shape[1]
    logits = jnp.dot(h_two_all, gate_low, preferred_element_type=f32)
    router = jax.nn.softmax(logits, axis=-1)
    iota = jnp.arange(experts, dtype=jnp.int32)
    picks = (routes[:, :, None] == iota[None, None, :]).astype(f32)
    gates = jnp.sum(picks * router[:, None, :], axis=-1)
    slot, owner, filled, block_expert = route_table(routes, experts, BLK)
    block_count = block_expert.shape[0]
    block_up = expert_low[0, :experts][block_expert]
    block_down = expert_low[1, :experts][block_expert]
    shared_up = expert_low[0, experts:]
    shared_down = expert_low[1, experts:]
    filled_low = filled[:, None].astype(bf16)
    slot_rows = (h_two_all[owner // TOPK] * filled_low).reshape(block_count, BLK, width)
    routed_pre = jnp.einsum("bsd,bdf->bsf", slot_rows, block_up, preferred_element_type=f32)
    routed_act = jax.nn.gelu(routed_pre).astype(bf16)
    slot_out = jnp.einsum(
        "bsf,bdf->bsd", routed_act, block_down, preferred_element_type=f32
    ).reshape(-1, width)
    picked = slot_out[slot].reshape(tok_grp, TOPK, width)
    shared_pre = jnp.einsum("td,sdf->stf", h_two_all, shared_up, preferred_element_type=f32)
    shared_act = jax.nn.gelu(shared_pre).astype(bf16)
    shared_out = jnp.einsum("stf,sdf->td", shared_act, shared_down, preferred_element_type=f32)
    branch_part = jnp.sum(gates[:, :, None] * picked, axis=1) + shared_out
    branch = lax.psum_scatter(
        branch_part.astype(jnp.bfloat16), "mp", scatter_dimension=0, tiled=True
    ).astype(jnp.float32)
    branch_img = branch.reshape(img_own, PATCH, width)
    output = (x_one + gate_two * branch_img).reshape(tok_dev, width)
    grad_out = cotangent.reshape(img_own, PATCH, width)
    grad_gate_two = jnp.sum(grad_out * branch_img, axis=1, keepdims=True)
    grad_branch = (grad_out * gate_two).astype(bf16).reshape(tok_dev, width)
    grad_branch_all = lax.all_gather(grad_branch, "mp", axis=0, tiled=True)
    grad_wide = grad_branch_all.astype(f32)
    gate_part = jnp.sum(grad_wide[:, None, :] * picked, axis=-1)
    grad_gates = lax.psum(gate_part, "mp")
    grad_picked = (gates[:, :, None] * grad_wide[:, None, :]).astype(bf16).reshape(-1, width)
    grad_slots = (grad_picked[owner] * filled_low).reshape(block_count, BLK, width)
    grad_act = jnp.einsum("bsd,bdf->bsf", grad_slots, block_down, preferred_element_type=f32)
    grad_pre = gelu_back(routed_pre, grad_act).astype(bf16)
    block_grad_up = jnp.einsum("bsd,bsf->bdf", slot_rows, grad_pre, preferred_element_type=f32)
    routed_grad_up = jax.ops.segment_sum(
        block_grad_up, block_expert, experts, indices_are_sorted=True
    )
    block_grad_down = jnp.einsum("bsd,bsf->bdf", grad_slots, routed_act, preferred_element_type=f32)
    routed_grad_down = jax.ops.segment_sum(
        block_grad_down, block_expert, experts, indices_are_sorted=True
    )
    slot_back = jnp.einsum("bsf,bdf->bsd", grad_pre, block_up, preferred_element_type=f32).reshape(
        -1, width
    )
    grad_h_part = jnp.sum(slot_back[slot].reshape(tok_grp, TOPK, width), axis=1)
    grad_shared_act = jnp.einsum(
        "td,sdf->stf", grad_branch_all, shared_down, preferred_element_type=f32
    )
    grad_shared_pre = gelu_back(shared_pre, grad_shared_act).astype(bf16)
    shared_grad_up = jnp.einsum(
        "td,stf->sdf", h_two_all, grad_shared_pre, preferred_element_type=f32
    )
    shared_grad_down = jnp.einsum(
        "td,stf->sdf", grad_branch_all, shared_act, preferred_element_type=f32
    )
    grad_h_part = grad_h_part + jnp.einsum(
        "stf,sdf->td", grad_shared_pre, shared_up, preferred_element_type=f32
    )
    grad_expert = jnp.stack(
        [
            jnp.concatenate([routed_grad_up, shared_grad_up], axis=0),
            jnp.concatenate([routed_grad_down, shared_grad_down], axis=0),
        ]
    )
    grad_h_own = lax.psum_scatter(
        grad_h_part.astype(jnp.bfloat16), "mp", scatter_dimension=0, tiled=True
    ).astype(jnp.float32)
    grad_router = jnp.sum(grad_gates[:, :, None] * picks, axis=1)
    grad_logits = (
        router * (grad_router - jnp.sum(router * grad_router, axis=-1, keepdims=True))
    ).astype(bf16)
    grad_gate_w = jnp.einsum("td,te->de", h_two_all, grad_logits, preferred_element_type=f32)
    own_logits = lax.dynamic_slice_in_dim(grad_logits, mp_index * tok_dev, tok_dev, 0)
    grad_h_two = grad_h_own + jnp.einsum(
        "te,de->td", own_logits, gate_low, preferred_element_type=f32
    )
    grad_h_two = grad_h_two.reshape(img_own, PATCH, width)
    grad_shift_two = jnp.sum(grad_h_two, axis=1, keepdims=True)
    grad_scale_two = jnp.sum(grad_h_two * normed_two, axis=1, keepdims=True)
    grad_x_one = grad_out + norm_back(grad_h_two * (1.0 + scale_two), normed_two, inverse_two)
    grad_gate_one = jnp.sum(grad_x_one * attention_img, axis=1, keepdims=True)
    grad_attention = (grad_x_one * gate_one).astype(bf16).reshape(tok_dev, width)
    grad_attention_all = lax.all_gather(grad_attention, "mp", axis=0, tiled=True)
    grad_mixed = jnp.einsum(
        "tj,jc->tc", grad_attention_all, out_weight, preferred_element_type=f32
    ).astype(bf16)
    grad_out_weight = jnp.einsum("tj,tc->jc", grad_attention_all, mixed, preferred_element_type=f32)
    grad_mixed_heads = grad_mixed.reshape(head_shape)
    scores_back = jnp.einsum("iqhc,ikhc->ihqk", query, keys, preferred_element_type=f32) * scale
    soft_back = jnp.exp(scores_back - top)
    grad_soft = jnp.einsum("iqhc,ikhc->ihqk", grad_mixed_heads, values, preferred_element_type=f32)
    delta = jnp.sum(soft_back * grad_soft, axis=-1, keepdims=True)
    grad_scores = (soft_back * (grad_soft - delta)).astype(bf16)
    grad_query = (
        jnp.einsum("ihqk,ikhc->iqhc", grad_scores, keys, preferred_element_type=f32) * scale
    )
    grad_keys = (
        jnp.einsum("ihqk,iqhc->ikhc", grad_scores, query, preferred_element_type=f32) * scale
    )
    grad_values = jnp.einsum(
        "ihqk,iqhc->ikhc", soft_low, grad_mixed_heads, preferred_element_type=f32
    )
    grad_triple = (
        jnp.stack([grad_query, grad_keys, grad_values]).reshape(3, tok_grp, local).astype(bf16)
    )
    grad_triple_w = jnp.einsum("td,jtc->jdc", h_one_all, grad_triple, preferred_element_type=f32)
    triple_weight = attn_low[:3]
    block = grad_triple
    grad_h_one = (
        lax.psum_scatter(
            jnp.einsum("jtc,jdc->td", block, triple_weight, preferred_element_type=f32).astype(
                jnp.bfloat16
            ),
            "mp",
            scatter_dimension=0,
            tiled=True,
        )
        .astype(jnp.float32)
        .reshape(img_own, PATCH, width)
    )
    grad_shift_one = jnp.sum(grad_h_one, axis=1, keepdims=True)
    grad_scale_one = jnp.sum(grad_h_one * normed_one, axis=1, keepdims=True)
    grad_tokens = (
        grad_x_one + norm_back(grad_h_one * (1.0 + scale_one), normed_one, inverse_one)
    ).reshape(tok_dev, width)
    grad_modulation = jnp.concatenate(
        [
            grad_shift_one,
            grad_scale_one,
            grad_gate_one,
            grad_shift_two,
            grad_scale_two,
            grad_gate_two,
        ],
        axis=1,
    )
    grad_modulation = grad_modulation.reshape(img_own, 6 * width).astype(bf16)
    grad_modulation_all = lax.all_gather(grad_modulation, "mp", axis=0, tiled=True)
    grad_ada_w = jnp.einsum("id,ie->de", cond_low, grad_modulation_all, preferred_element_type=f32)
    grad_attn_w = jnp.concatenate([grad_triple_w, grad_out_weight[None]], axis=0)
    ada_total, gate_total, attn_total, expert_total = (
        lax.psum_scatter(grad_ada_w, "dp", scatter_dimension=0, tiled=True),
        lax.psum_scatter(grad_gate_w, "dp", scatter_dimension=0, tiled=True),
        lax.psum_scatter(grad_attn_w, "dp", scatter_dimension=1, tiled=True),
        lax.psum_scatter(grad_expert, "dp", scatter_dimension=2, tiled=True),
    )
    squares = 0.5 * (jnp.sum(ada_total * ada_total) + jnp.sum(gate_total * gate_total))
    squares = squares + jnp.sum(attn_total * attn_total) + jnp.sum(expert_total * expert_total)
    grad_norm = jnp.sqrt(lax.psum(squares, ("dp", "mp")))
    factor = jnp.minimum(1.0, CLIP_NORM / (grad_norm + 1e-06))
    ada_new, ada_first_new, ada_second_new = adam(w_ada, ada_first, ada_second, ada_total * factor)
    gate_new, gate_first_new, gate_second_new = adam(
        w_gate, gate_first, gate_second, gate_total * factor
    )
    attn_new, attn_first_new, attn_second_new = adam(
        w_attn, attn_first, attn_second, attn_total * factor
    )
    expert_new, expert_first_new, expert_second_new = adam(
        w_expert, expert_first, expert_second, expert_total * factor
    )
    return (
        output,
        grad_tokens,
        grad_norm,
        ada_new,
        ada_first_new,
        ada_second_new,
        gate_new,
        gate_first_new,
        gate_second_new,
        attn_new,
        attn_first_new,
        attn_second_new,
        expert_new,
        expert_first_new,
        expert_second_new,
    )


def solution(mesh):
    placed = (
        P(("dp", "mp"), None),
        P("dp", None),
        P(("dp", "mp"), None),
        P("dp", None),
        P("dp", None),
        P("dp", None),
        P("dp", None),
        P("dp", None),
        P("dp", None),
        P("dp", None),
        P(None, "dp", "mp"),
        P(None, "dp", "mp"),
        P(None, "dp", "mp"),
        P(None, None, "dp", "mp"),
        P(None, None, "dp", "mp"),
        P(None, None, "dp", "mp"),
    )
    return jax.shard_map(
        per_device,
        mesh=mesh,
        in_specs=placed,
        out_specs=(
            P(("dp", "mp"), None),
            P(("dp", "mp"), None),
            P(),
            P("dp", None),
            P("dp", None),
            P("dp", None),
            P("dp", None),
            P("dp", None),
            P("dp", None),
            P(None, "dp", "mp"),
            P(None, "dp", "mp"),
            P(None, "dp", "mp"),
            P(None, None, "dp", "mp"),
            P(None, None, "dp", "mp"),
            P(None, None, "dp", "mp"),
        ),
        check_vma=False,
    )
```

profile of v0, /device:TPU:0, one launch (start us, length us, event | category | flops | bytes accessed | tf_op | source)
XLA Modules:
  0.0 1325.9 jit_solution(13753471029853119025)
XLA Ops:
  13.2 59.8 %all-gather.9.cloned.1.call-done = bf16[384,2304]{1,0:T(8,128)(2,1)} async-done(((bf16[24,2304]{1,0:T(8,128)(2,1)}), bf16[384,2304]{1,0:T(8,128)(2,1)}) %all-gather.9.cloned.1.call-update) | async-done | bytes 1769488 | tf_op jit(solution)/shard_map/all_gather | solution.py:93
  76.4 43.2 %all_gather.29 = bf16[4,384,192]{2,0,1:T(4,128)(2,1)S(1)} all-gather(bf16[4,24,192]{2,0,1:T(4,128)(2,1)S(1)} %copy.346), channel_id=1, replica_groups=mesh['dp'=16,'mp'=2] {'dp'}, dimensions={1}, use_global_device_ids=true | all-gather | bytes 626688 | tf_op jit(solution)/shard_map/all_gather | solution.py:95
  121.7 2.9 fusion.120
  131.0 2.4 fusion.82
  135.3 5.2 reduce-scatter.8.cloned.1.call-done
  147.2 41.1 %all-gather = bf16[16,24,8]{1,2,0:T(8,128)(2,1)S(1)} all-gather(bf16[1,24,8]{1,2,0:T(8,128)(2,1)S(1)} %convert_bitcast_fusion.2), channel_id=1, replica_groups=mesh['dp'=16,'mp'=2] {'dp'}, dimensions={0}, use_global_device_ids=true | all-gather | bytes 6528 | tf_op jit(solution)/shard_map/all_gather | solution.py:94
  191.9 15.5 %scatter_custom_fusion = s32[5120]{0:T(1024)S(1)} fusion(s32[4096]{0:T(1024)S(1)} %bitcast.343, s32[4096]{0:T(1024)S(1)} %iota.20, s32[]{:T(128)} %constant.52.clone.1), kind=kCustom, calls=%fused_computation.207 | custom fusion | bytes 20484 | tf_op jit(solution)/shard_map/scatter | solution.py:61
  207.5 15.5 %scatter_custom_fusion.1 = s32[5120]{0:T(1024)S(1)} fusion(s32[4096]{0:T(1024)S(1)} %bitcast.344, s32[4096]{0:T(1024)S(1)} %broadcast.480, s32[]{:T(128)} %constant.52.clone.1), kind=kCustom, calls=%fused_computation.205 | custom fusion | bytes 20484 | tf_op jit(solution)/shard_map/scatter | solution.py:62
  223.7 6.1 mul.664
  229.8 8.7 mul.665
  240.4 22.2 %gather_fusion = bf16[5120,384]{1,0:T(8,128)(2,1)} fusion(bf16[2048,384]{1,0:T(8,128)(2,1)} %all-gather.13.cloned.1.call-done, s32[5120]{0:T(1024)S(1)} %get-tuple-element.148), kind=kCustom, calls=%fused_computation | custom fusion | bytes 7884800 | tf_op jit(solution)/shard_map/gather | solution.py:158
  262.6 6.3 copy.270
  271.0 4.4 multiply_convert_fusion.2
  275.4 22.9 %gather_fusion.4 = bf16[5120,384]{1,0:T(8,128)(2,1)} fusion(bf16[4096,384]{1,0:T(8,128)(2,1)} %multiply_convert_fusion.2, s32[5120]{0:T(1024)S(1)} %get-tuple-element.147), kind=kCustom, calls=%fused_computation.4 | custom fusion | bytes 7884800 | tf_op jit(solution)/shard_map/gather | solution.py:182
  298.3 6.3 copy.273
  304.6 11.2 all-gather.15.cloned.1.call-done
  315.8 8.1 slice_bitcast_fusion.1
  323.9 11.9 gather_fusion.2
  335.8 11.9 gather_fusion.1
  347.8 18.6 %fusion.27 = f32[40,128,768]{2,1,0:T(8,128)} fusion(bf16[40,384,768]{2,1,0:T(8,128)(2,1)} %gather_fusion.1, bf16[40,128,384]{1,2,0:T(8,128)(2,1)} %copy.270, bf16[40,128]{1,0:T(8,128)(2,1)S(1)} %convert_bitcast_fusion.1), kind=kOutput, calls=%fused_computation.56 | convolution fusion | flops 3021864960 | bytes 43264000 | tf_op jit(solution)/shard_map/bsd,bdf->bsf/dot_general | solution.py:159
  366.4 23.2 %fusion.6 = bf16[40,128,768]{2,1,0:T(8,128)(2,1)} fusion(f32[40,128,768]{2,1,0:T(8,128)} %fusion.27, bf16[40,384,768]{2,1,0:T(8,128)(2,1)} %gather_fusion.2, bf16[40,128,384]{1,2,0:T(8,128)(2,1)} %copy.273, bf16[40,128]{1,0:T(8,128)(2,1)S(1)} %convert_bitcast_fusion.1), kind=kOutput, calls=%fused_computation.21 | convolution fusion | flops 3100508160 | bytes 51128320 | tf_op jit(solution)/shard_map/bsd,bdf->bsf/dot_general | solution.py:183
  389.6 16.7 %fusion.121 = f32[40,128,384]{2,1,0:T(8,128)} fusion(bf16[40,128,768]{2,1,0:T(8,128)(2,1)} %fusion.6, bf16[40,384,768]{2,1,0:T(8,128)(2,1)} %gather_fusion.1), kind=kOutput, calls=%fused_computation.261 | convolution fusion | flops 3019898880 | bytes 39321600 | tf_op jit(solution)/shard_map/bsf,bdf->bsd/dot_general | solution.py:193
  406.3 20.3 %gather_fusion.5 = f32[4096,384]{1,0:T(8,128)} fusion(f32[5120,384]{1,0:T(8,128)} %bitcast.318, s32[4096]{0:T(1024)S(1)} %broadcast_clamp_fusion), kind=kCustom, calls=%fused_computation.5 | custom fusion | bytes 12599296 | tf_op jit(solution)/shard_map/gather | solution.py:196
  426.6 8.1 reshape.487
  434.7 35.5 %reduce_sum.284 = f32[2048,384]{1,0:T(8,128)} reduce(f32[2048,2,384]{2,1,0:T(2,128)} %reshape.487, f32[]{:T(128)} %constant.54.clone.1), dimensions={1}, to_apply=%region_20.21 | reduce | flops 786432 | bytes 9437188 | tf_op jit(solution)/shard_map/reduce_sum | solution.py:196
  470.3 4.8 fusion.57
  475.1 12.4 fusion.13
  487.5 2.6 copy-done.81
  490.2 6.0 fusion.29
  496.2 19.3 %fusion.111 = f32[40,128,384]{2,1,0:T(8,128)} fusion(bf16[40,384,768]{2,1,0:T(8,128)(2,1)} %gather_fusion.2, f32[40,128,768]{2,1,0:T(8,128)} %fusion.27), kind=kOutput, calls=%fused_computation.256 | convolution fusion | flops 3055288320 | bytes 47185920 | tf_op jit(solution)/shard_map/bsf,bdf->bsd/dot_general | solution.py:161
  515.5 20.3 %gather_fusion.3 = f32[4096,384]{1,0:T(8,128)} fusion(f32[5120,384]{1,0:T(8,128)} %bitcast.319, s32[4096]{0:T(1024)S(1)} %broadcast_clamp_fusion), kind=kCustom, calls=%fused_computation.3 | custom fusion | bytes 12599296 | tf_op jit(solution)/shard_map/gather | solution.py:164
  535.9 8.3 reshape.485
  544.2 18.0 %multiply_reduce_fusion.1 = (f32[2048,2]{1,0:T(8,128)}, f32[2048,384]{1,0:T(8,128)S(1)}) fusion(f32[2048,2,384]{2,1,0:T(2,128)} %reshape.485, f32[2048,384]{1,0:T(8,128)} %convert_element_type.133, f32[2048,2]{1,0:T(8,128)S(1)} %copy-done.12), kind=kLoop, calls=%fused_computation.41 | loop fusion | flops 5500928 | bytes 12615680 | tf_op jit(solution)/shard_map/reduce_sum | solution.py:179
  562.2 8.5 fusion.30
  570.8 8.1 psum.14
  580.7 3.1 fusion.60
  583.8 3.9 fusion.36
  587.8 8.2 all-gather.19.cloned.1.call-done
  598.3 7.2 multiply_reduce_fusion
  605.6 4.6 multiply_convert_fusion.1
  619.2 2.5 copy.286
  625.2 4.7 bitcast_convert_fusion
  630.1 11.0 convolution_bitcast_fusion
  641.0 3.1 copy.291
  646.2 3.5 fusion.61
  650.8 2.6 copy.287
  653.5 3.6 fusion.53
  659.0 2.4 fusion.122
  661.7 7.7 convolution_bitcast_fusion.1
  669.4 3.1 copy.289
  672.5 22.8 %fusion.19 = f32[40,384,768]{2,1,0:T(8,128)} fusion(bf16[40,128,384]{1,2,0:T(8,128)(2,1)} %copy.273, bf16[40,128]{1,0:T(8,128)(2,1)S(1)} %copy-done.38, f32[40,128,768]{2,1,0:T(8,128)} %fusion.27), kind=kOutput, calls=%fused_computation.50 | convolution fusion | flops 3057254400 | bytes 66856960 | tf_op jit(solution)/shard_map/bsd,bsf->bdf/dot_general | solution.py:189
  695.4 4.3 broadcast.479.clone
  699.7 84.9 %scatter_fusion.1 = f32[8,384,768]{2,1,0:T(8,128)} fusion(f32[8,384,768]{2,1,0:T(8,128)} %broadcast.479.clone, s32[40]{0:T(128)S(1)} %broadcast_add_fusion, f32[40,384,768]{2,1,0:T(8,128)} %fusion.19), kind=kCustom, calls=%fused_computation.9 | custom fusion | flops 11796480 | bytes 141557920 | tf_op jit(solution)/shard_map/scatter-add | solution.py:190
  784.6 22.4 %fusion.25 = f32[40,384,768]{2,1,0:T(8,128)} fusion(bf16[40,128,768]{2,1,0:T(8,128)(2,1)} %fusion.6, bf16[40,128,384]{1,2,0:T(8,128)(2,1)} %copy.270, bf16[40,128]{1,0:T(8,128)(2,1)S(1)} %copy-done.38), kind=kOutput, calls=%fused_computation.54 | convolution fusion | flops 3021864960 | bytes 58992640 | tf_op jit(solution)/shard_map/bsd,bsf->bdf/dot_general | solution.py:185
  807.0 4.4 broadcast.479.clone.1
  811.4 85.4 %scatter_fusion = f32[8,384,768]{2,1,0:T(8,128)} fusion(f32[8,384,768]{2,1,0:T(8,128)} %broadcast.479.clone.1, s32[40]{0:T(128)S(1)} %broadcast_add_fusion, f32[40,384,768]{2,1,0:T(8,128)} %fusion.25), kind=kCustom, calls=%fused_computation.8 | custom fusion | flops 11796480 | bytes 141557920 | tf_op jit(solution)/shard_map/scatter-add | solution.py:186
  896.9 4.9 maximum_bitcast_fusion.1
  903.4 2.9 maximum_bitcast_fusion
  906.4 8.2 pad_maximum_fusion
  916.8 85.2 %all-reduce = f32[384,8]{0,1:T(8,128)S(1)} all-reduce(f32[384,8]{0,1:T(8,128)S(1)} %fusion.123), channel_id=7, replica_groups=mesh['dp'=16,'mp'=2] {'dp'}, use_global_device_ids=true, to_apply=%region_40.41.clone | all-reduce | flops 3072 | bytes 24576
  1009.9 252.9 %reduce-scatter.18.cloned.1.call-done = f32[2,10,24,768]{3,2,1,0:T(8,128)} async-done(((f32[2,10,384,768]{3,2,1,0:T(8,128)}), f32[2,10,24,768]{3,2,1,0:T(8,128)}) %reduce-scatter.18.cloned.1.call-update) | async-done | bytes 1474576 | tf_op jit(solution)/shard_map/reduce_scatter | solution.py:296
  1265.9 2.9 fusion.50
  1268.8 39.3 %psum.15 = f32[]{:T(128)} all-reduce(f32[]{:T(128)S(6)} %add.389), channel_id=1, replica_groups=mesh['dp'=16,'mp'=2] {'dp','mp'}, use_global_device_ids=true, to_apply=%region_48.49 | all-reduce | flops 1 | bytes 8 | tf_op jit(solution)/shard_map/psum | solution.py:300
  1312.2 5.5 multiply_subtract_fusion
  (320 shorter events, 71.0 us)
Async XLA Ops:
  7.2 67.8 %copy-start.4 = (f32[1024,384]{1,0:T(8,128)S(1)}, f32[1024,384]{1,0:T(8,128)}, u32[]{:S(2)}) copy-start(f32[1024,384]{1,0:T(8,128)} %param.16) | copy-start | bytes 4718596
  7.2 65.9 %all-gather.9.cloned.1.call-start = ((), (), s32[]{:S(2)}) async-start(), calls=%async_computation.6 | async-start | bytes 1880064 | tf_op jit(solution)/shard_map/all_gather | solution.py:93
  9.0 112.7 %all-gather.11.cloned.1.call-start = ((), (), s32[]{:S(2)}) async-start(), calls=%async_computation.7 | async-start | bytes 2359296 | tf_op jit(solution)/shard_map/all_gather | solution.py:112
  9.0 67.3 %copy-start.39 = (f32[4,24,192]{2,1,0:T(8,128)S(1)}, f32[4,24,192]{2,1,0:T(8,128)}, u32[]{:S(2)}) copy-start(f32[4,24,192]{2,1,0:T(8,128)} %param.26) | copy-start | bytes 221188
  10.7 65.6 %copy-start.52 = (f32[1024]{0:T(1024)}, f32[1024]{0:T(1024)S(1)}, u32[]{:S(2)}) copy-start(f32[1024]{0:T(1024)S(1)} %broadcast_multiply_fusion.5) | copy-start | bytes 12292
  12.5 63.8 %copy-start.59 = (f32[1024]{0:T(1024)}, f32[1024]{0:T(1024)S(1)}, u32[]{:S(2)}) copy-start(f32[1024]{0:T(1024)S(1)} %add_rsqrt_fusion.1) | copy-start | bytes 12292
  13.2 59.8 %copy-start.72 = (bf16[8,384]{1,0:T(8,128)(2,1)}, bf16[8,384]{1,0:T(8,128)(2,1)S(1)}, u32[]{:S(2)}) copy-start(bf16[8,384]{1,0:T(8,128)(2,1)S(1)} %multiply_convert_fusion.6) | copy-start | bytes 18436
  76.2 64.2 %reduce-scatter.8.cloned.1.call-start = ((), (), s32[]{:S(2)}) async-start(), calls=%async_computation.8 | async-start | bytes 4718592 | tf_op jit(solution)/shard_map/reduce_scatter | solution.py:134
  121.6 8.6 copy-start.31
  133.5 90.2 %all-gather.17.cloned.1.call-start = ((), (), s32[]{:S(2)}) async-start(), calls=%async_computation.12 | async-start | bytes 2359296 | tf_op jit(solution)/shard_map/all_gather | solution.py:177
  135.2 105.2 %all-gather.13.cloned.1.call-start = ((), (), s32[]{:S(2)}) async-start(), calls=%async_computation.9 | async-start | bytes 2359296 | tf_op jit(solution)/shard_map/all_gather | solution.py:144
  135.2 5.2 copy-start.66
  135.2 9.3 copy-start.46
  144.6 171.2 %all-gather.15.cloned.1.call-start = ((), (), s32[]{:S(2)}) async-start(), calls=%async_computation.10 | async-start | bytes 12533760 | tf_op jit(solution)/shard_map/all_gather | solution.py:96
  145.6 435.0 %reduce-scatter.12.cloned.1.call-start = ((), (), s32[]{:S(2)}) async-start(), calls=%async_computation.13 | async-start | bytes 2359296 | tf_op jit(solution)/shard_map/reduce_scatter | solution.py:216
  188.4 80.5 %copy-start.68 = (bf16[384,8]{0,1:T(8,128)(2,1)}, bf16[384,8]{0,1:T(8,128)(2,1)S(1)}, u32[]{:S(2)}) copy-start(bf16[384,8]{0,1:T(8,128)(2,1)S(1)} %reshape.580) | copy-start | bytes 18436
  223.6 142.8 %copy-start.37 = (bf16[40,128]{1,0:T(8,128)(2,1)}, bf16[40,128]{1,0:T(8,128)(2,1)S(1)}, u32[]{:S(2)}) copy-start(bf16[40,128]{1,0:T(8,128)(2,1)S(1)} %convert_bitcast_fusion.1) | copy-start | bytes 30724
  229.8 8.7 copy-start.23
  262.6 6.3 copy-start
  269.5 5.8 copy-start.55
  270.5 4.8 copy-start.11
  475.1 12.4 copy-start.7
  475.1 15.1 %copy-start.27 = (f32[2048,384]{1,0:T(8,128)S(1)}, f32[2048,384]{1,0:T(8,128)}, u32[]{:S(2)}) copy-start(f32[2048,384]{1,0:T(8,128)} %reduce_sum.284) | copy-start | bytes 9437188
  496.2 87.6 %reduce-scatter.10.cloned.1.call-start = ((), (), s32[]{:S(2)}) async-start(), calls=%async_computation.11 | async-start | bytes 2359296 | tf_op jit(solution)/shard_map/reduce_scatter | solution.py:169
  535.9 8.3 copy-start.12
  570.6 9.8 copy-start.51
  570.6 9.9 copy-start.30
  570.6 9.9 copy-start.43
  570.6 9.9 copy-start.56
  570.7 10.0 copy-start.9
  570.7 10.0 copy-start.47
  570.7 10.0 copy-start.49
  570.7 10.0 copy-start.58
  570.7 10.0 copy-start.69
  570.7 13.1 copy-start.67
  570.7 13.1 copy-start.71
  570.8 25.2 %all-gather.19.cloned.1.call-start = ((), (), s32[]{:S(2)}) async-start(), calls=%async_computation.14 | async-start | bytes 2359296 | tf_op jit(solution)/shard_map/all_gather | solution.py:234
  583.8 12.2 copy-start.32
  587.7 10.6 copy-start.21
  587.7 10.6 copy-start.36
  587.8 65.7 %reduce-scatter.14.cloned.1.call-start = ((), (), s32[]{:S(2)}) async-start(), calls=%async_computation.15 | async-start | bytes 2359296 | tf_op jit(solution)/shard_map/reduce_scatter | solution.py:261
  598.3 7.3 slice-start
  598.3 7.2 slice-start.1
  625.2 4.9 copy-start.25
  629.9 372.7 %all-reduce.4.cloned.1.call-start = ((), (), s32[]{:S(2)}) async-start(), calls=%async_computation.18 | async-start | bytes 3145728
  653.4 5.6 copy-start.73
  653.4 352.8 %reduce-scatter.16.cloned.1.call-start = ((), (), s32[]{:S(2)}) async-start(), calls=%async_computation.16 | async-start | bytes 3760128 | tf_op jit(solution)/shard_map/reduce_scatter | solution.py:293
  661.5 601.4 %reduce-scatter.18.cloned.1.call-start = ((), (), s32[]{:S(2)}) async-start(), calls=%async_computation.17 | async-start | bytes 25067520 | tf_op jit(solution)/shard_map/reduce_scatter | solution.py:296
  811.4 85.4 %copy-start.13 = (f32[2,384,768]{2,1,0:T(8,128)S(1)}, f32[2,384,768]{2,1,0:T(8,128)}, u32[]{:S(2)}) copy-start(f32[2,384,768]{2,1,0:T(8,128)} %copy.291) | copy-start | bytes 7077892
  896.9 6.6 copy-start.2
  914.5 89.7 %copy-start.6 = (f32[1024,384]{1,0:T(8,128)S(1)}, f32[1024,384]{1,0:T(8,128)}, u32[]{:S(2)}) copy-start(f32[1024,384]{1,0:T(8,128)} %param.16) | copy-start | bytes 4718596
  914.5 89.7 %copy-start.54 = (f32[1024]{0:T(1024)S(1)}, f32[1024]{0:T(1024)}, u32[]{:S(2)}) copy-start(f32[1024]{0:T(1024)} %copy-done.52) | copy-start | bytes 12292
  914.6 89.7 %copy-start.61 = (f32[1024]{0:T(1024)S(1)}, f32[1024]{0:T(1024)}, u32[]{:S(2)}) copy-start(f32[1024]{0:T(1024)} %copy-done.59) | copy-start | bytes 12292
  914.6 89.7 %copy-start.65 = (f32[4,384]{1,0:T(4,128)S(1)}, f32[4,384]{1,0:T(4,128)}, u32[]{:S(2)}) copy-start(f32[4,384]{1,0:T(4,128)} %copy-done.64) | copy-start | bytes 18436
  916.8 349.2 %copy-start.22 = (bf16[1024,384]{1,0:T(8,128)(2,1)S(1)}, bf16[1024,384]{1,0:T(8,128)(2,1)}, u32[]{:S(2)}) copy-start(bf16[1024,384]{1,0:T(8,128)(2,1)} %reduce-scatter.14.cloned.1.call-done) | copy-start | bytes 2359300
  1006.1 302.8 %copy-start.75 = (f32[24,8]{0,1:T(8,128)S(1)}, f32[24,8]{0,1:T(8,128)}, u32[]{:S(2)}) copy-start(f32[24,8]{0,1:T(8,128)} %param.23) | copy-start | bytes 2308
  1006.1 302.8 %copy-start.76 = (f32[24,8]{0,1:T(8,128)S(1)}, f32[24,8]{0,1:T(8,128)}, u32[]{:S(2)}) copy-start(f32[24,8]{0,1:T(8,128)} %param.24) | copy-start | bytes 2308
  1006.1 302.8 %copy-start.77 = (f32[24,8]{0,1:T(8,128)S(1)}, f32[24,8]{0,1:T(8,128)}, u32[]{:S(2)}) copy-start(f32[24,8]{0,1:T(8,128)} %param.25) | copy-start | bytes 2308
  1006.1 303.5 %copy-start.40 = (f32[4,24,192]{2,1,0:T(8,128)S(1)}, f32[4,24,192]{2,1,0:T(8,128)}, u32[]{:S(2)}) copy-start(f32[4,24,192]{2,1,0:T(8,128)} %param.26) | copy-start | bytes 221188
  1006.1 303.5 %copy-start.62 = (f32[4,24,192]{2,1,0:T(8,128)S(1)}, f32[4,24,192]{2,1,0:T(8,128)}, u32[]{:S(2)}) copy-start(f32[4,24,192]{2,1,0:T(8,128)} %param.27) | copy-start | bytes 221188
  1006.1 303.4 %copy-start.63 = (f32[4,24,192]{2,1,0:T(8,128)S(1)}, f32[4,24,192]{2,1,0:T(8,128)}, u32[]{:S(2)}) copy-start(f32[4,24,192]{2,1,0:T(8,128)} %param.28) | copy-start | bytes 221188
  1006.2 304.2 %copy-start.34 = (f32[24,2304]{1,0:T(8,128)S(1)}, f32[24,2304]{1,0:T(8,128)}, u32[]{:S(2)}) copy-start(f32[24,2304]{1,0:T(8,128)} %param.20) | copy-start | bytes 663556
  1006.2 304.2 %copy-start.41 = (f32[24,2304]{1,0:T(8,128)S(1)}, f32[24,2304]{1,0:T(8,128)}, u32[]{:S(2)}) copy-start(f32[24,2304]{1,0:T(8,128)} %param.21) | copy-start | bytes 663556
  1006.2 304.1 %copy-start.33 = (f32[24,2304]{1,0:T(8,128)S(1)}, f32[24,2304]{1,0:T(8,128)}, u32[]{:S(2)}) copy-start(f32[24,2304]{1,0:T(8,128)} %reduce-scatter.16.cloned.1.call-done) | copy-start | bytes 663556
  (33 other events, 80.4 us)
Sparse Core Ops, SparseCore 0:
  11.4 61.6 all-gather.8
  76.4 8.5 all-gather.10
  133.6 6.7 reduce-scatter.7
  142.5 10.9 all-gather.16
  155.5 10.9 all-gather.12
  170.0 145.7 all-gather.14
  496.3 7.1 reduce-scatter.11
  570.9 7.5 reduce-scatter.9
  587.9 8.0 all-gather.18
  630.0 10.2 reduce-scatter.13
  653.5 118.5 all-reduce.3
  777.9 133.4 reduce-scatter.15
  918.3 344.5 reduce-scatter.17
where the time goes:
time: 1340 us; the launch traced here: 1330 us
  waiting for transfers between devices  338 us (25%)
  other arithmetic  297 us (22%)
  local copies, waits for them, and re-layouts  238 us (18%)
  blocking collectives  219 us (16%)
  matrix products  213 us (16%)
  between operations  20.9 us (2%)
    reduce_scatter x1, waiting for transfers between devices, per_device(): lax.psum_scatter(grad_expert, 'dp', scatter_dimension=2, tiled=True)  253 us
    scatter-add x1, other arithmetic, per_device(): jax.ops.segment_sum(block_grad_up, block_expert, experts, indices_are_sor...  85.4 us
    unnamed x1, blocking collectives  85.2 us
    scatter-add x1, other arithmetic, per_device(): jax.ops.segment_sum(block_grad_down, block_expert, experts, indices_are_s...  84.9 us
    all_gather x1, waiting for transfers between devices, per_device(): lax.all_gather(w_ada.astype(bf16), 'dp', axis=0, tiled=True)  59.8 us
    all_gather x1, blocking collectives, per_device(): lax.all_gather(w_attn.astype(bf16), 'dp', axis=1, tiled=True)  43.2 us
    all_gather x1, blocking collectives, per_device(): lax.all_gather(w_gate.astype(bf16), 'dp', axis=0, tiled=True)  41.1 us
    psum x1, blocking collectives, per_device(): grad_norm = jnp.sqrt(lax.psum(squares, ('dp', 'mp')))  39.3 us
  transfers between devices with their start and end apart: 13, of which 5 were waited for; matrix products, arithmetic and copies ran while one was open for 37% of the time, Pallas kernels for 0%

commit v1 on v0

v1 whole, which is shorter than its diff:
```python
import functools

import jax
import jax.numpy as jnp
from jax import lax
from jax.experimental import pallas as pl
from jax.experimental.pallas import tpu as pltpu
from jax.sharding import PartitionSpec as P

HD = 64
PATCH = 256
STEP = 10
LANES = 128
SUB = 16
TILE = 512

EPS_NORM = 1e-06
CLIP_NORM = 0.1
RATE = 0.08
BETA_ONE = 0.9
BETA_TWO = 0.95
ADAM_EPS = 1e-08
DECAY = 0.01
GELU_LIN = 0.7978845608
GELU_CUBE = 0.7978845608 * 0.044715

MESH = pl.DeviceIdType.MESH
VMEM_BYTES = 62 * 1024 * 1024
bf16 = jnp.bfloat16
f32 = jnp.float32
NN = (((1,), (0,)), ((), ()))
NT = (((1,), (1,)), ((), ()))
TN = (((0,), (0,)), ((), ()))


def mxu(left, right, dims=NN):
    return lax.dot_general(left, right, dims, preferred_element_type=f32)


def layer_norm(value):
    center = value - jnp.mean(value, axis=-1, keepdims=True)
    inverse = lax.rsqrt(jnp.mean(center * center, axis=-1, keepdims=True) + EPS_NORM)
    return (center * inverse, inverse)


def norm_back(grad, normed, inverse):
    mean_grad = jnp.mean(grad, axis=-1, keepdims=True)
    mean_proj = jnp.mean(grad * normed, axis=-1, keepdims=True)
    return inverse * (grad - mean_grad - normed * mean_proj)


def adam(master, first, second, grad):
    first_new = BETA_ONE * first + (1.0 - BETA_ONE) * grad
    second_new = BETA_TWO * second + (1.0 - BETA_TWO) * grad * grad
    fix_one = 1.0 - BETA_ONE**STEP
    fix_two = 1.0 - BETA_TWO**STEP
    update = first_new / fix_one / (jnp.sqrt(second_new / fix_two) + ADAM_EPS) + DECAY * master
    return (master - RATE * update, first_new, second_new)


def gelu_both(value):
    square = value * value
    tanh = jnp.tanh(value * (GELU_CUBE * square + GELU_LIN))
    half = 0.5 * tanh + 0.5
    act = value * half
    slope = half + act * (1.0 - tanh) * (3.0 * GELU_CUBE * square + GELU_LIN)
    return act, slope


def dp_sizes(count):
    side = 4 if count >= 64 else 2
    return count // (side * side), side


class Place:
    def __init__(self, count):
        self.count = count
        self.depth, self.side = dp_sizes(count)
        self.dp = lax.axis_index("dp")
        self.mp = lax.axis_index("mp")
        side = self.side
        self.z = self.dp // (side * side)
        y = (self.dp // side) % side
        x = self.dp % side
        self.a = jnp.where(self.mp == 0, y, x)
        self.b = jnp.where(self.mp == 0, x, y)
        self.slot = self.slot_at(self.a, self.b, self.z)

    def slot_at(self, a, b, z):
        return (a * self.side + b) * self.depth + z

    def device(self, a, b, z):
        side = self.side
        dp = jnp.where(self.mp == 0, (z * side + a) * side + b, (z * side + b) * side + a)
        return (dp, self.mp)

    def slot_of(self, dp):
        side = self.side
        z, y, x = dp // (side * side), (dp // side) % side, dp % side
        return jnp.where(self.mp == 0, self.slot_at(y, x, z), self.slot_at(x, y, z))

    def peers_z(self):
        return [self.device(self.a, self.b, (self.z + k) % self.depth) for k in range(1, self.depth)]

    def peers_b(self):
        return [self.device(self.a, (self.b + k) % self.side, self.z) for k in range(1, self.side)]

    def peers_a(self):
        return [self.device((self.a + k) % self.side, self.b, self.z) for k in range(1, self.side)]

    def other_core(self):
        return (self.dp, 1 - self.mp)

    def greet(self):
        peers = self.peers_z() + self.peers_b() + self.peers_a() + [self.other_core()]
        barrier = pltpu.get_barrier_semaphore()
        for peer in peers:
            pl.semaphore_signal(barrier, inc=1, device_id=peer, device_id_type=MESH)
        pl.semaphore_wait(barrier, len(peers))


def remote(src, dst, send, recv, peer):
    return pltpu.make_async_remote_copy(
        src_ref=src, dst_ref=dst, send_sem=send, recv_sem=recv, device_id=peer, device_id_type=MESH
    )


class Gather:
    def __init__(self, place, buf, send, recv):
        self.p, self.buf, self.send, self.recv = place, buf, send, recv

    def copies(self, stage, e):
        p = self.p
        if stage == 0:
            src = self.buf.at[e, pl.ds(p.slot, 1)]
            peers, base = p.peers_z(), 0
        elif stage == 1:
            src = self.buf.at[e, pl.ds(p.slot_at(p.a, p.b, 0), p.depth)]
            peers, base = p.peers_b(), p.depth - 1
        else:
            src = self.buf.at[e, pl.ds(p.slot_at(p.a, 0, 0), p.depth * p.side)]
            peers, base = p.peers_a(), p.depth - 1 + p.side - 1
        return [
            remote(src, src, self.send.at[e, base + k], self.recv.at[e, base + k], peer)
            for k, peer in enumerate(peers)
        ]

    def start(self, stage, e):
        for copy in self.copies(stage, e):
            copy.start()

    def arrive(self, stage, e):
        for copy in self.copies(stage, e):
            copy.wait_recv()

    def sent(self, e):
        for stage in range(3):
            for copy in self.copies(stage, e):
                copy.wait_send()


class Scatter:
    def __init__(self, place, buf, boxes, send, recv):
        self.p, self.buf, self.boxes, self.send, self.recv = place, buf, boxes, send, recv

    def copies(self, stage, e):
        p = self.p
        made = []
        for k in range(1, p.side if stage < 2 else p.depth):
            if stage == 0:
                a = (p.a + k) % p.side
                src = self.buf.at[e, pl.ds(p.slot_at(a, 0, 0), p.depth * p.side)]
                peer, base = p.device(a, p.b, p.z), 0
            elif stage == 1:
                b = (p.b + k) % p.side
                src = self.buf.at[e, pl.ds(p.slot_at(p.a, b, 0), p.depth)]
                peer, base = p.device(p.a, b, p.z), p.side - 1
            else:
                z = (p.z + k) % p.depth
                src = self.buf.at[e, pl.ds(p.slot_at(p.a, p.b, z), 1)]
                peer, base = p.device(p.a, p.b, z), 2 * (p.side - 1)
            at = base + k - 1
            made.append(remote(src, self.boxes[stage].at[e, k - 1], self.send.at[e, at], self.recv.at[e, at], peer))
        return made

    def start(self, stage, e):
        for copy in self.copies(stage, e):
            copy.start()

    def arrive(self, stage, e):
        for copy in self.copies(stage, e):
            copy.wait()

    def add(self, stage, e):
        p = self.p
        if stage == 0:
            first, many = p.slot_at(p.a, 0, 0), p.depth * p.side
        else:
            first, many = p.slot_at(p.a, p.b, 0), p.depth
        box = self.boxes[stage]

        def one(i, carry):
            total = self.buf[e, first + i].astype(f32)
            for k in range(p.side - 1):
                total = total + box[e, k, i].astype(f32)
            self.buf[e, first + i] = total.astype(bf16)
            return carry

        lax.fori_loop(0, many, one, 0)

    def last(self, e):
        p = self.p
        total = self.buf[e, p.slot].astype(f32)
        for k in range(p.depth - 1):
            total = total + self.boxes[2][e, k, 0].astype(f32)
        return total


def block_rows(rows):
    return (2 * rows + SUB - 1) // SUB * SUB


def pick_matrix(place, rows, lower):
    block = block_rows(rows)
    shape = (place.count * rows, place.count * block)
    feature = lax.broadcasted_iota(jnp.int32, shape, 0)
    column = lax.broadcasted_iota(jnp.int32, shape, 1)
    slot, inner = column // block, column % block - (rows if lower else 0)
    z, b, a = slot % place.depth, slot // place.depth % place.side, slot // (place.depth * place.side)
    first = jnp.where(place.mp == 0, (z * place.side + a) * place.side + b, (z * place.side + b) * place.side + a)
    hit = (inner >= 0) & (inner < rows) & (first * rows + inner == feature)
    return hit.astype(f32).astype(bf16)


def blocks_to_weights(place, rows, buf, e, up_ref, down_ref):
    if rows % 8 == 0:
        for pair in range(place.count // 2):
            one = buf[e, place.slot_of(2 * pair)].astype(f32)
            two = buf[e, place.slot_of(2 * pair + 1)].astype(f32)
            at = pl.ds(2 * pair * rows, 2 * rows)
            up_ref[at, :] = jnp.concatenate([one[:rows], two[:rows]], axis=0).astype(bf16)
            down_ref[at, :] = jnp.concatenate([one[rows : 2 * rows], two[rows : 2 * rows]], axis=0).astype(bf16)
    else:
        flat = buf[e].reshape(place.count * block_rows(rows), buf.shape[-1])
        up_ref[...] = mxu(pick_matrix(place, rows, False), flat).astype(bf16)
        down_ref[...] = mxu(pick_matrix(place, rows, True), flat).astype(bf16)


def grads_to_blocks(place, rows, up_ref, down_ref, buf, e):
    if rows % 8 == 0:
        for dp in range(place.count):
            at = pl.ds(dp * rows, rows)
            both = jnp.concatenate([up_ref[at, :], down_ref[at, :]], axis=0)
            buf[e, place.slot_of(dp)] = both.astype(bf16)
    else:
        flat = mxu(pick_matrix(place, rows, False), up_ref[...].astype(bf16), TN)
        flat = flat + mxu(pick_matrix(place, rows, True), down_ref[...].astype(bf16), TN)
        buf[e] = flat.astype(bf16).reshape(buf.shape[1:])


def expert_kernel(
    count,
    rows,
    w_ref,
    h_ref,
    d_ref,
    gate_ref,
    branch_ref,
    grad_h_ref,
    grad_gate_ref,
    total_ref,
    buf,
    box_a,
    box_b,
    box_z,
    h_all,
    d_all,
    gate_all,
    branch_acc,
    grad_h_acc,
    grad_gate_acc,
    up_w,
    down_w,
    up_grad,
    down_grad,
    share_out,
    share_in,
    gate_in,
    gather_send,
    gather_recv,
    scatter_send,
    scatter_recv,
    core_send,
    core_recv,
):
    place = Place(count)
    experts = w_ref.shape[1]
    own_tok = h_ref.shape[0]
    gather = Gather(place, buf, gather_send, gather_recv)
    scatter = Scatter(place, buf, (box_a, box_b, box_z), scatter_send, scatter_recv)
    own = pl.ds(pl.multiple_of(place.mp * own_tok, own_tok), own_tok)
    theirs = pl.ds(pl.multiple_of((1 - place.mp) * own_tok, own_tok), own_tok)

    def fill(e, carry):
        both = jnp.concatenate([w_ref[0, e], w_ref[1, e]], axis=0).astype(bf16)
        if both.shape[0] != buf.shape[2]:
            buf[e, place.slot] = jnp.zeros(buf.shape[2:], bf16)
        buf[e, place.slot, pl.ds(0, both.shape[0])] = both
        return carry

    lax.fori_loop(0, experts, fill, 0)
    loads = [
        pltpu.make_async_copy(src, dst.at[own], core_send.at[5 + i])
        for i, (src, dst) in enumerate(((h_ref, h_all), (d_ref, d_all), (gate_ref, gate_all)))
    ]
    for load in loads:
        load.start()
    place.greet()
    for e in range(3):
        gather.start(0, e)
    shared = [
        remote(ref.at[own], ref.at[own], core_send.at[i], core_recv.at[i], place.other_core())
        for i, ref in enumerate((h_all, d_all, gate_all))
    ]
    for load, copy in zip(loads, shared):
        load.wait()
        copy.start()
    gather.start(0, 3)
    branch_acc[...] = jnp.zeros_like(branch_acc)
    grad_h_acc[...] = jnp.zeros_like(grad_h_acc)
    grad_gate_acc[...] = jnp.zeros_like(grad_gate_acc)
    for e in range(2):
        gather.arrive(0, e)
        gather.start(1, e)
    gather.arrive(1, 0)
    gather.start(2, 0)
    for copy in shared:
        copy.wait()

    def compute(e):
        blocks_to_weights(place, rows, buf, e, up_w, down_w)
        up_grad[...] = jnp.zeros_like(up_grad)
        down_grad[...] = jnp.zeros_like(down_grad)

        def tile(t, carry):
            at = pl.ds(pl.multiple_of(t * TILE, TILE), TILE)
            h = h_all[at, :]
            d = d_all[at, :]
            lane = lax.broadcasted_iota(jnp.int32, (TILE, LANES), 1)
            gate = jnp.sum(jnp.where(lane == e, gate_all[at, :], 0.0), axis=1, keepdims=True)
            pre = mxu(h, up_w[...])
            back = mxu(d, down_w[...])
            act, slope = gelu_both(pre)
            inner = jnp.sum(act * back, axis=1, keepdims=True)
            grad_gate_acc[at, :] += jnp.where(lane == e, inner, 0.0)
            act_low = (gate * act).astype(bf16)
            pre_low = (gate * back * slope).astype(bf16)
            branch_acc[at, :] += mxu(act_low, down_w[...], NT)
            grad_h_acc[at, :] += mxu(pre_low, up_w[...], NT)
            up_grad[...] += mxu(h, pre_low, TN)
            down_grad[...] += mxu(d, act_low, TN)
            return carry

        lax.fori_loop(0, h_all.shape[0] // TILE, tile, 0)

    def step(e, carry):
        @pl.when(e + 4 < experts)
        def _():
            gather.start(0, e + 4)

        @pl.when(e + 2 < experts)
        def _():
            gather.arrive(0, e + 2)
            gather.start(1, e + 2)

        @pl.when(e + 1 < experts)
        def _():
            gather.arrive(1, e + 1)
            gather.start(2, e + 1)

        gather.arrive(2, e)
        compute(e)
        gather.sent(e)
        grads_to_blocks(place, rows, up_grad, down_grad, buf, e)
        scatter.start(0, e)

        @pl.when(e >= 1)
        def _():
            scatter.arrive(0, e - 1)
            scatter.add(0, e - 1)
            scatter.start(1, e - 1)

        @pl.when(e >= 2)
        def _():
            scatter.arrive(1, e - 2)
            scatter.add(1, e - 2)
            scatter.start(2, e - 2)

        @pl.when(e >= 3)
        def _():
            scatter.arrive(2, e - 3)
            total_ref[e - 3] = scatter.last(e - 3)

        return carry

    lax.fori_loop(0, experts, step, 0)
    share_out[0] = branch_acc[theirs, :].astype(bf16)
    share_out[1] = grad_h_acc[theirs, :].astype(bf16)
    shares = [
        remote(share_out, share_in, core_send.at[3], core_recv.at[3], place.other_core()),
        remote(grad_gate_acc.at[theirs], gate_in, core_send.at[4], core_recv.at[4], place.other_core()),
    ]
    shares[0].start()
    shares[1].start()
    scatter.arrive(0, experts - 1)
    scatter.add(0, experts - 1)
    scatter.start(1, experts - 1)
    scatter.arrive(1, experts - 2)
    scatter.add(1, experts - 2)
    scatter.start(2, experts - 2)
    shares[0].wait()
    shares[1].wait()
    branch_ref[...] = branch_acc[own, :] + share_in[0].astype(f32)
    grad_h_ref[...] = grad_h_acc[own, :] + share_in[1].astype(f32)
    grad_gate_ref[...] = grad_gate_acc[own, :] + gate_in[...]
    scatter.arrive(1, experts - 1)
    scatter.add(1, experts - 1)
    scatter.start(2, experts - 1)
    for e in range(experts - 3, experts):
        scatter.arrive(2, e)
        total_ref[e] = scatter.last(e)


def expert_call(count, w_expert, h_own, d_own, gates):
    _, experts, rows, hidden = w_expert.shape
    own_tok, width = h_own.shape
    depth, side = dp_sizes(count)
    block = block_rows(rows)
    tok = 2 * own_tok
    vmem = pl.BlockSpec(memory_space=pltpu.VMEM)
    gather_sems = depth + 2 * side - 3
    return pl.pallas_call(
        functools.partial(expert_kernel, count, rows),
        out_shape=(
            jax.ShapeDtypeStruct((own_tok, width), f32),
            jax.ShapeDtypeStruct((own_tok, width), f32),
            jax.ShapeDtypeStruct((own_tok, LANES), f32),
            jax.ShapeDtypeStruct((experts, block, hidden), f32),
        ),
        in_specs=[vmem] + [pl.BlockSpec(memory_space=pl.ANY)] * 3,
        out_specs=(vmem,) * 4,
        scratch_shapes=[
            pltpu.VMEM((experts, count, block, hidden), bf16),
            pltpu.VMEM((experts, side - 1, side * depth, block, hidden), bf16),
            pltpu.VMEM((experts, side - 1, depth, block, hidden), bf16),
            pltpu.VMEM((experts, depth - 1, 1, block, hidden), bf16),
            pltpu.VMEM((tok, width), bf16),
            pltpu.VMEM((tok, width), bf16),
            pltpu.VMEM((tok, LANES), f32),
            pltpu.VMEM((tok, width), f32),
            pltpu.VMEM((tok, width), f32),
            pltpu.VMEM((tok, LANES), f32),
            pltpu.VMEM((width, hidden), bf16),
            pltpu.VMEM((width, hidden), bf16),
            pltpu.VMEM((width, hidden), f32),
            pltpu.VMEM((width, hidden), f32),
            pltpu.VMEM((2, own_tok, width), bf16),
            pltpu.VMEM((2, own_tok, width), bf16),
            pltpu.VMEM((own_tok, LANES), f32),
            pltpu.SemaphoreType.DMA((experts, gather_sems)),
            pltpu.SemaphoreType.DMA((experts, gather_sems)),
            pltpu.SemaphoreType.DMA((experts, gather_sems)),
            pltpu.SemaphoreType.DMA((experts, gather_sems)),
            pltpu.SemaphoreType.DMA((8,)),
            pltpu.SemaphoreType.DMA((5,)),
        ],
        compiler_params=pltpu.CompilerParams(
            collective_id=1, has_side_effects=True, vmem_limit_bytes=VMEM_BYTES
        ),
        cost_estimate=pl.CostEstimate(
            flops=12 * tok * width * hidden * experts, bytes_accessed=8 * w_expert.size, transcendentals=0
        ),
        name="experts",
    )(w_expert, h_own, d_own, gates)


def per_device(
    tokens,
    condition,
    cotangent,
    routes,
    w_ada,
    ada_first,
    ada_second,
    w_gate,
    gate_first,
    gate_second,
    w_attn,
    attn_first,
    attn_second,
    w_expert,
    expert_first,
    expert_second,
):
    tok_dev, width = tokens.shape
    img_own = tok_dev // PATCH
    heads = width // HD
    experts = w_gate.shape[1]
    rows = w_expert.shape[2]
    count = lax.axis_size("dp")
    mp_index = lax.axis_index("mp")
    ada_low = lax.all_gather(w_ada.astype(bf16), "dp", axis=0, tiled=True)
    gate_low = lax.all_gather(w_gate.astype(bf16), "dp", axis=0, tiled=True)
    attn_low = lax.all_gather(w_attn.astype(bf16), "dp", axis=1, tiled=True)
    attn_low = lax.all_gather(attn_low, "mp", axis=2, tiled=True)
    cond_low = jax.nn.silu(condition).astype(bf16)
    cond_own = lax.dynamic_slice_in_dim(cond_low, mp_index * img_own, img_own, 0)
    modulation = jnp.dot(cond_own, ada_low, preferred_element_type=f32).reshape(img_own, 6, 1, width)
    shift_one = modulation[:, 0]
    scale_one = modulation[:, 1]
    gate_one = modulation[:, 2]
    shift_two = modulation[:, 3]
    scale_two = modulation[:, 4]
    gate_two = modulation[:, 5]
    x_img = tokens.reshape(img_own, PATCH, width)
    normed_one, inverse_one = layer_norm(x_img)
    h_one = (normed_one * (1.0 + scale_one) + shift_one).astype(bf16).reshape(tok_dev, width)
    triple = jnp.einsum("td,jdc->jtc", h_one, attn_low[:3], preferred_element_type=f32).astype(bf16)
    head_shape = (img_own, PATCH, heads, HD)
    query = triple[0].reshape(head_shape)
    keys = triple[1].reshape(head_shape)
    values = triple[2].reshape(head_shape)
    scale = HD ** (-0.5)
    scores = jnp.einsum("iqhc,ikhc->ihqk", query, keys, preferred_element_type=f32) * scale
    top = jax.nn.logsumexp(scores, axis=-1, keepdims=True)
    soft_low = jnp.exp(scores - top).astype(bf16)
    mixed = (
        jnp.einsum("ihqk,ikhc->iqhc", soft_low, values, preferred_element_type=f32)
        .astype(bf16)
        .reshape(tok_dev, width)
    )
    out_weight = attn_low[3]
    attention = jnp.einsum("tc,jc->tj", mixed, out_weight, preferred_element_type=f32)
    attention_img = attention.reshape(img_own, PATCH, width)
    x_one = x_img + gate_one * attention_img
    normed_two, inverse_two = layer_norm(x_one)
    h_two = (normed_two * (1.0 + scale_two) + shift_two).astype(bf16).reshape(tok_dev, width)
    grad_out = cotangent.reshape(img_own, PATCH, width)
    grad_branch = (grad_out * gate_two).astype(bf16).reshape(tok_dev, width)
    logits = jnp.dot(h_two, gate_low, preferred_element_type=f32)
    router = jax.nn.softmax(logits, axis=-1)
    own_routes = lax.dynamic_slice_in_dim(routes, mp_index * tok_dev, tok_dev, 0)
    iota = jnp.arange(experts, dtype=jnp.int32)
    chosen = jnp.sum((own_routes[:, :, None] == iota[None, None, :]).astype(f32), axis=1)
    gate_table = router * chosen
    shared = w_expert.shape[1] - experts
    gate_table = jnp.concatenate(
        [gate_table, jnp.ones((tok_dev, shared), f32), jnp.zeros((tok_dev, LANES - experts - shared), f32)],
        axis=1,
    )
    branch, grad_h_own, grad_gates, expert_blocks = expert_call(count, w_expert, h_two, grad_branch, gate_table)
    branch_img = branch.reshape(img_own, PATCH, width)
    output = (x_one + gate_two * branch_img).reshape(tok_dev, width)
    grad_gate_two = jnp.sum(grad_out * branch_img, axis=1, keepdims=True)
    grad_router = grad_gates[:, :experts] * chosen
    grad_logits = (
        router * (grad_router - jnp.sum(router * grad_router, axis=-1, keepdims=True))
    ).astype(bf16)
    grad_gate_w = jnp.einsum("td,te->de", h_two, grad_logits, preferred_element_type=f32)
    grad_h_two = grad_h_own + jnp.einsum("te,de->td", grad_logits, gate_low, preferred_element_type=f32)
    grad_h_two = grad_h_two.reshape(img_own, PATCH, width)
    grad_shift_two = jnp.sum(grad_h_two, axis=1, keepdims=True)
    grad_scale_two = jnp.sum(grad_h_two * normed_two, axis=1, keepdims=True)
    grad_x_one = grad_out + norm_back(grad_h_two * (1.0 + scale_two), normed_two, inverse_two)
    grad_gate_one = jnp.sum(grad_x_one * attention_img, axis=1, keepdims=True)
    grad_attention = (grad_x_one * gate_one).astype(bf16).reshape(tok_dev, width)
    grad_mixed = jnp.einsum("tj,jc->tc", grad_attention, out_weight, preferred_element_type=f32).astype(bf16)
    grad_out_weight = jnp.einsum("tj,tc->jc", grad_attention, mixed, preferred_element_type=f32)
    grad_mixed_heads = grad_mixed.reshape(head_shape)
    scores_back = jnp.einsum("iqhc,ikhc->ihqk", query, keys, preferred_element_type=f32) * scale
    soft_back = jnp.exp(scores_back - top)
    grad_soft = jnp.einsum("iqhc,ikhc->ihqk", grad_mixed_heads, values, preferred_element_type=f32)
    delta = jnp.sum(soft_back * grad_soft, axis=-1, keepdims=True)
    grad_scores = (soft_back * (grad_soft - delta)).astype(bf16)
    grad_query = jnp.einsum("ihqk,ikhc->iqhc", grad_scores, keys, preferred_element_type=f32) * scale
    grad_keys = jnp.einsum("ihqk,iqhc->ikhc", grad_scores, query, preferred_element_type=f32) * scale
    grad_values = jnp.einsum("ihqk,iqhc->ikhc", soft_low, grad_mixed_heads, preferred_element_type=f32)
    grad_triple = jnp.stack([grad_query, grad_keys, grad_values]).reshape(3, tok_dev, width).astype(bf16)
    grad_triple_w = jnp.einsum("td,jtc->jdc", h_one, grad_triple, preferred_element_type=f32)
    grad_h_one = jnp.einsum(
        "jtc,jdc->td", grad_triple, attn_low[:3], preferred_element_type=f32
    ).reshape(img_own, PATCH, width)
    grad_shift_one = jnp.sum(grad_h_one, axis=1, keepdims=True)
    grad_scale_one = jnp.sum(grad_h_one * normed_one, axis=1, keepdims=True)
    grad_tokens = (
        grad_x_one + norm_back(grad_h_one * (1.0 + scale_one), normed_one, inverse_one)
    ).reshape(tok_dev, width)
    grad_modulation = jnp.concatenate(
        [grad_shift_one, grad_scale_one, grad_gate_one, grad_shift_two, grad_scale_two, grad_gate_two],
        axis=1,
    )
    grad_modulation = grad_modulation.reshape(img_own, 6 * width).astype(bf16)
    grad_ada_w = jnp.einsum("id,ie->de", cond_own, grad_modulation, preferred_element_type=f32)
    grad_attn_w = jnp.concatenate([grad_triple_w, grad_out_weight[None]], axis=0)
    half = width // 2
    small = jnp.concatenate(
        [
            grad_ada_w.reshape(width, 2, 3 * width).transpose(1, 0, 2),
            grad_attn_w.reshape(4, width, 2, half).transpose(2, 1, 0, 3).reshape(2, width, 2 * width),
        ],
        axis=2,
    ).astype(bf16)
    small = lax.psum_scatter(small, "mp", scatter_dimension=0, tiled=False)
    small = lax.psum_scatter(small, "dp", scatter_dimension=0, tiled=True).astype(f32)
    ada_half = small[:, : 3 * width]
    attn_total = small[:, 3 * width :].reshape(-1, 4, half).transpose(1, 0, 2)
    ada_total = lax.all_gather(ada_half, "mp", axis=1, tiled=True)
    gate_total = lax.psum(grad_gate_w, ("dp", "mp"))
    gate_total = lax.dynamic_slice_in_dim(gate_total, lax.axis_index("dp") * rows, rows, 0)
    expert_total = expert_blocks[:, : 2 * rows].reshape(-1, 2, rows, w_expert.shape[3]).transpose(1, 0, 2, 3)
    squares = 0.5 * (jnp.sum(ada_total * ada_total) + jnp.sum(gate_total * gate_total))
    squares = squares + jnp.sum(attn_total * attn_total) + jnp.sum(expert_total * expert_total)
    grad_norm = jnp.sqrt(lax.psum(squares, ("dp", "mp")))
    factor = jnp.minimum(1.0, CLIP_NORM / (grad_norm + 1e-06))
    ada_new, ada_first_new, ada_second_new = adam(w_ada, ada_first, ada_second, ada_total * factor)
    gate_new, gate_first_new, gate_second_new = adam(
        w_gate, gate_first, gate_second, gate_total * factor
    )
    attn_new, attn_first_new, attn_second_new = adam(
        w_attn, attn_first, attn_second, attn_total * factor
    )
    expert_new, expert_first_new, expert_second_new = adam(
        w_expert, expert_first, expert_second, expert_total * factor
    )
    return (
        output,
        grad_tokens,
        grad_norm,
        ada_new,
        ada_first_new,
        ada_second_new,
        gate_new,
        gate_first_new,
        gate_second_new,
        attn_new,
        attn_first_new,
        attn_second_new,
        expert_new,
        expert_first_new,
        expert_second_new,
    )


def solution(mesh):
    placed = (
        P(("dp", "mp"), None),
        P("dp", None),
        P(("dp", "mp"), None),
        P("dp", None),
        P("dp", None),
        P("dp", None),
        P("dp", None),
        P("dp", None),
        P("dp", None),
        P("dp", None),
        P(None, "dp", "mp"),
        P(None, "dp", "mp"),
        P(None, "dp", "mp"),
        P(None, None, "dp", "mp"),
        P(None, None, "dp", "mp"),
        P(None, None, "dp", "mp"),
    )
    return jax.shard_map(
        per_device,
        mesh=mesh,
        in_specs=placed,
        out_specs=(
            P(("dp", "mp"), None),
            P(("dp", "mp"), None),
            P(),
            P("dp", None),
            P("dp", None),
            P("dp", None),
            P("dp", None),
            P("dp", None),
            P("dp", None),
            P(None, "dp", "mp"),
            P(None, "dp", "mp"),
            P(None, "dp", "mp"),
            P(None, None, "dp", "mp"),
            P(None, None, "dp", "mp"),
            P(None, None, "dp", "mp"),
        ),
        check_vma=False,
    )
```

time: 1340 us -> 639 us (0.48)
  other arithmetic: 297 us -> 40.7 us
  Pallas kernels: 0 us -> 232 us
  waiting for transfers between devices: 338 us -> 113 us
  local copies, waits for them, and re-layouts: 238 us -> 37.9 us
  matrix products: 213 us -> 26.4 us
  blocking collectives: 219 us -> 166 us
    reduce_scatter x6 -> x1, waiting for transfers between devices: 258 us -> 10.6 us  [per_device(): small = lax.psum_scatter(small, 'mp', scatter_dimension=0, tiled=False)]
    pallas_call x0 -> x1, Pallas kernels: none -> 232 us  [expert_call(): pl.pallas_call(functools.partial(expert_kernel, count, rows), out_shape=(...]
    dot_general x21 -> x10, matrix products: 194 us -> 13.5 us  [the longest x1 4.9 us: per_device(): jnp.einsum('jtc,jdc->td', grad_triple, attn_low[:3], preferred_element_ty...]
    scatter-add x2 -> x0, other arithmetic: 170 us -> none  [the longest x1 85.4 us: per_device(): jax.ops.segment_sum(block_grad_up, block_expert, experts, indices_are_sor...]
    gather x8 -> x0, local copies, waits for them, and re-layouts: 122 us -> none  [the longest x2 29.2 us: per_device(): grad_picked[owner] * filled_low]
    unnamed x1 -> x0, blocking collectives: 85.2 us -> none
    unnamed x14 -> x5, waiting for transfers between devices: 0.22 us -> 80.3 us
    all_gather x6 -> x2, waiting for transfers between devices: 79.3 us -> 22.6 us  [the longest x1 22.6 us: per_device(): ada_low = lax.all_gather(w_ada.astype(bf16), 'dp', axis=0, tiled=True)]
  transfers between devices with their start and end apart: 13 -> 4, of which waited for: 5 -> 3; matrix products, arithmetic and copies ran while one was open for 37% -> 2% of each run, Pallas kernels for 0% -> 0%
where the time goes in v1:
time: 639 us; the launch traced here: 636 us
  Pallas kernels  232 us (36%)
  blocking collectives  166 us (26%)
  waiting for transfers between devices  113 us (18%)
  other arithmetic  40.7 us (6%)
  local copies, waits for them, and re-layouts  37.9 us (6%)
  matrix products  26.4 us (4%)
  between operations  19.4 us (3%)
    pallas_call x1, Pallas kernels, expert_call(): pl.pallas_call(functools.partial(expert_kernel, count, rows), out_shape=(...  232 us
    unnamed x5, waiting for transfers between devices  80.3 us
    all_gather x1, blocking collectives, per_device(): attn_low = lax.all_gather(w_attn.astype(bf16), 'dp', axis=1, tiled=True)  47.2 us
    psum x1, blocking collectives, per_device(): gate_total = lax.psum(grad_gate_w, ('dp', 'mp'))  41 us
    psum x1, blocking collectives, per_device(): grad_norm = jnp.sqrt(lax.psum(squares, ('dp', 'mp')))  40 us
    all_gather x1, blocking collectives, per_device(): gate_low = lax.all_gather(w_gate.astype(bf16), 'dp', axis=0, tiled=True)  35.7 us
    all_gather x1, waiting for transfers between devices, per_device(): ada_low = lax.all_gather(w_ada.astype(bf16), 'dp', axis=0, tiled=True)  22.6 us
    unnamed x118, local copies, waits for them, and re-layouts  15.9 us
  transfers between devices with their start and end apart: 4, of which 3 were waited for; matrix products, arithmetic and copies ran while one was open for 2% of the time, Pallas kernels for 0%

profile of v1, /device:TPU:0, one launch (start us, length us, event | category | flops | bytes accessed | tf_op | source)
XLA Modules:
  0.0 635.7 jit_solution(4783655340150343951)
XLA Ops:
  7.3 1.0 copy.261
  8.3 47.2 %all_gather.16 = bf16[4,384,192]{2,0,1:T(4,128)(2,1)S(1)} all-gather(bf16[4,24,192]{2,0,1:T(4,128)(2,1)S(1)} %copy.261), channel_id=1, replica_groups=mesh['dp'=16,'mp'=2] {'dp'}, dimensions={1}, use_global_device_ids=true | all-gather | bytes 626688 | tf_op jit(solution)/shard_map/all_gather | solution.py:514
  55.4 1.5 copy.184
  57.0 0.7 convert_element_type.63
  58.6 35.7 %all-gather = bf16[16,24,8]{1,2,0:T(8,128)(2,1)S(1)} all-gather(bf16[1,24,8]{1,2,0:T(8,128)(2,1)S(1)} %convert_bitcast_fusion.1), channel_id=1, replica_groups=mesh['dp'=16,'mp'=2] {'dp'}, dimensions={0}, use_global_device_ids=true | all-gather | bytes 6528 | tf_op jit(solution)/shard_map/all_gather | solution.py:513
  94.5 1.0 copy.198
  95.5 2.8 slice.64
  98.3 2.6 copy.232
  100.9 2.2 copy.231
  103.1 22.6 %all-gather.4.cloned.1.call-done = bf16[384,2304]{1,0:T(8,128)(2,1)} async-done(((bf16[24,2304]{1,0:T(8,128)(2,1)}), bf16[384,2304]{1,0:T(8,128)(2,1)}) %all-gather.4.cloned.1.call-update) | async-done | bytes 1769488 | tf_op jit(solution)/shard_map/all_gather | solution.py:512
  125.7 1.8 fusion.43
  128.0 0.9 copy-done.38
  128.9 1.5 convert_bitcast_fusion
  133.3 1.0 multiply_reduce_fusion.1
  134.3 1.1 exponential_reduce_fusion
  135.4 1.5 copy-done.2
  137.0 1.2 convolution_convert_fusion.3
  138.4 1.9 multiply_add_fusion.3
  142.3 2.6 fusion.4.d_ref
  145.7 0.9 maximum_maximum_fusion.gate_ref
  146.6 231.8 %experts.1 = (f32[1024,384]{1,0:T(8,128)}, f32[1024,384]{1,0:T(8,128)}, f32[1024,128]{1,0:T(8,128)}, f32[10,48,768]{2,1,0:T(8,128)}) custom-call(f32[2,10,24,768]{3,2,1,0:T(8,128)} %w_ref.1, bf16[1024,384]{1,0:T(8,128)(2,1)} %bitcast.197, bf16[1024,384]{1,0:T(8,128)(2,1)} %fusion.4.d_ref, f32[1024,128]{1,0:T(8,128)} %maximum_maximum_fusion.gate_ref), custom_call_target="tpu_custom_call" | custom-call | flops 72477573120 | bytes 2949120 | tf_op jit(solution)/shard_map/experts/pallas_call | solution.py:442
  378.4 2.1 multiply_reduce_fusion.2
  382.1 1.5 fusion.3
  383.7 2.8 fusion.5
  386.9 2.9 multiply_reduce_fusion.3
  390.0 1.0 copy-done.8
  391.0 0.9 copy-done.26
  391.9 0.6 convolution_convert_fusion.4
  392.5 1.2 copy.200
  393.7 1.9 reshape.229
  395.7 5.1 fusion.12
  400.7 2.1 multiply_reduce_fusion
  402.9 1.6 multiply_convert_fusion
  404.6 1.1 fusion.11
  406.8 0.6 copy.213
  407.4 1.0 copy.233
  408.5 0.6 copy.211
  409.7 0.6 copy.205
  410.9 0.6 copy.208
  412.2 1.0 copy-done.39
  413.2 1.4 convolution_convert_fusion.1
  416.2 0.6 copy.216
  416.8 4.6 copy.212
  421.5 4.9 fusion.2
  426.4 0.7 fusion.1
  427.1 1.8 pad_maximum_fusion
  429.0 10.6 %reduce-scatter.5.cloned.1.call-done = bf16[1,384,1920]{2,1,0:T(8,128)(2,1)} async-done(((bf16[2,384,1920]{2,1,0:T(8,128)(2,1)}), bf16[1,384,1920]{2,1,0:T(8,128)(2,1)}) %reduce-scatter.5.cloned.1.call-update) | async-done | bytes 1474576 | tf_op jit(solution)/shard_map/reduce_scatter | solution.py:613
  439.9 41.0 %psum.14 = f32[384,8]{0,1:T(8,128)S(1)} all-reduce(f32[384,8]{0,1:T(8,128)S(1)} %fusion.56), channel_id=1, replica_groups=mesh['dp'=16,'mp'=2] {'dp','mp'}, use_global_device_ids=true, to_apply=%region_24.25 | all-reduce | flops 3072 | bytes 24576 | tf_op jit(solution)/shard_map/psum | solution.py:618
  480.9 0.7 multiply_reduce_fusion.12
  481.6 2.4 multiply_reduce_fusion.8
  484.0 80.2 %reduce-scatter.7.cloned.1.call-done = bf16[24,1920]{1,0:T(8,128)(2,1)} async-done(((bf16[384,1920]{1,0:T(8,128)(2,1)}), bf16[24,1920]{1,0:T(8,128)(2,1)}) %reduce-scatter.7.cloned.1.call-update) | async-done | bytes 92176
  564.2 0.9 convert_element_type.80
  565.1 0.6 multiply_reduce_fusion.11
  565.8 0.8 slice.68
  566.6 2.0 all_gather.19
  568.5 0.7 multiply_reduce_fusion.10
  571.8 2.7 multiply_add_fusion
  574.5 40.0 %psum.15 = f32[]{:T(128)} all-reduce(f32[]{:T(128)S(6)} %add.206), channel_id=1, replica_groups=mesh['dp'=16,'mp'=2] {'dp','mp'}, use_global_device_ids=true, to_apply=%region_28.29 | all-reduce | flops 1 | bytes 8 | tf_op jit(solution)/shard_map/psum | solution.py:623
  615.3 0.9 slice_multiply_fusion.1
  616.2 1.5 broadcast_multiply_fusion
  617.9 1.5 multiply_subtract_fusion.3
  619.4 2.1 multiply_subtract_fusion.1
  621.5 1.6 multiply_subtract_fusion.2
  623.2 4.6 multiply_subtract_fusion
  (172 shorter events, 14.7 us)
Async XLA Ops:
  7.2 87.2 %copy-start = (s32[2048,2]{0,1:T(2,128)S(1)}, s32[2048,2]{0,1:T(2,128)}, u32[]{:S(2)}) copy-start(s32[2048,2]{0,1:T(2,128)} %param.19) | copy-start | bytes 49156
  7.2 49.8 %copy-start.36 = (f32[24,2304]{1,0:T(8,128)S(1)}, f32[24,2304]{1,0:T(8,128)}, u32[]{:S(2)}) copy-start(f32[24,2304]{1,0:T(8,128)} %param.20) | copy-start | bytes 663556
  7.2 88.3 %all-gather.6.cloned.1.call-start = ((), (), s32[]{:S(2)}) async-start(), calls=%async_computation.3 | async-start | bytes 1769472 | tf_op jit(solution)/shard_map/all_gather | solution.py:515
  8.2 49.6 %copy-start.3 = (f32[1024,384]{1,0:T(8,128)S(1)}, f32[1024,384]{1,0:T(8,128)}, u32[]{:S(2)}) copy-start(f32[1024,384]{1,0:T(8,128)} %param.16) | copy-start | bytes 4718596
  56.9 68.8 %all-gather.4.cloned.1.call-start = ((), (), s32[]{:S(2)}) async-start(), calls=%async_computation.2 | async-start | bytes 1880064 | tf_op jit(solution)/shard_map/all_gather | solution.py:512
  57.7 382.0 %reduce-scatter.5.cloned.1.call-start = ((), (), s32[]{:S(2)}) async-start(), calls=%async_computation.4 | async-start | bytes 4423680 | tf_op jit(solution)/shard_map/reduce_scatter | solution.py:613
  57.9 0.7 copy-start.44
  95.5 5.5 copy-start.29
  98.3 27.4 %copy-start.46 = (f32[8,384]{1,0:T(8,128)S(1)}, f32[8,384]{1,0:T(8,128)}, u32[]{:S(2)}) copy-start(f32[8,384]{1,0:T(8,128)} %param.17) | copy-start | bytes 36868
  127.5 1.4 copy-start.35
  128.0 0.9 copy-start.38
  131.5 1.8 copy-start.18
  132.4 0.9 copy-start.12
  133.3 2.2 copy-start.22
  134.3 2.7 copy-start.2
  137.0 1.4 copy-start.4
  138.2 2.1 copy-start.20
  141.2 0.9 copy-start.16
  142.3 3.4 copy-start.10
  142.3 3.0 copy-start.14
  378.4 2.2 copy-start.11
  378.4 2.2 copy-start.15
  378.4 2.3 copy-start.32
  380.7 1.4 copy-start.33
  381.7 1.9 copy-start.30
  383.6 2.8 copy-start.6
  383.6 2.8 copy-start.7
  383.7 3.3 copy-start.24
  389.8 1.1 copy-start.8
  391.0 0.9 copy-start.26
  391.9 8.8 %slice-start = ((s8[6291456]{0:T(1024)(128)(4,1)}), s8[2097152]{0:T(1024)(128)(4,1)S(1)}, s32[]{:S(2)}) async-start(s8[6291456]{0:T(1024)(128)(4,1)} %bitcast.192), calls=%async_computation.6 | async-start | bytes 4194304
  395.6 5.1 slice-start.1
  395.7 5.1 copy-start.23
  402.9 1.7 copy-start.19
  404.6 1.1 copy-start.13
  405.7 1.1 copy-start.21
  406.8 1.7 copy-start.28
  412.1 1.1 copy-start.39
  413.2 1.4 copy-start.25
  413.2 1.7 copy-start.27
  413.2 2.2 copy-start.37
  416.8 4.6 copy-start.5
  429.0 10.7 %copy-start.17 = (bf16[4,256,384]{2,1,0:T(8,128)(2,1)S(1)}, bf16[4,256,384]{2,1,0:T(8,128)(2,1)}, u32[]{:S(2)}) copy-start(bf16[4,256,384]{2,1,0:T(8,128)(2,1)} %copy-done.16) | copy-start | bytes 2359300
  429.0 10.7 %copy-start.31 = (bf16[1024,8]{1,0:T(8,128)(2,1)S(1)}, bf16[1024,8]{1,0:T(8,128)(2,1)}, u32[]{:S(2)}) copy-start(bf16[1024,8]{1,0:T(8,128)(2,1)} %copy-done.30) | copy-start | bytes 49156
  429.0 135.2 %reduce-scatter.7.cloned.1.call-start = ((), (), s32[]{:S(2)}) async-start(), calls=%async_computation.5 | async-start | bytes 1566720
  439.9 131.9 %copy-start.9 = (f32[4,256,384]{2,1,0:T(8,128)S(1)}, f32[4,256,384]{2,1,0:T(8,128)}, u32[]{:S(2)}) copy-start(f32[4,256,384]{2,1,0:T(8,128)} %copy-done.8) | copy-start | bytes 4718596
  480.9 84.8 %copy-start.43 = (f32[384,8]{0,1:T(8,128)}, f32[384,8]{0,1:T(8,128)S(1)}, u32[]{:S(2)}) copy-start(f32[384,8]{0,1:T(8,128)S(1)} %psum.14) | copy-start | bytes 36868
  565.1 0.7 copy-start.40
  616.2 1.7 copy-start.45
  616.2 1.7 copy-start.47
  616.2 1.7 copy-start.48
  617.7 3.8 copy-start.41
  617.7 3.8 copy-start.42
  617.7 5.4 copy-start.34
  623.2 4.6 copy-start.1
Sparse Core Ops, SparseCore 0:
  57.0 5.0 all-gather.5
  65.5 60.1 all-gather.3
  429.1 10.4 reduce-scatter.4
  445.1 118.9 reduce-scatter.6

commit v2 on v1

v2 whole, which is shorter than its diff:
```python
import functools
import math

import jax
import jax.numpy as jnp
from jax import lax
from jax.experimental import pallas as pl
from jax.experimental.pallas import tpu as pltpu
from jax.sharding import PartitionSpec as P

HD = 64
PATCH = 256
STEP = 10
LANES = 128
SUB = 16
TILE = 512
SLOTS = 4

EPS_NORM = 1e-06
CLIP_NORM = 0.1
RATE = 0.08
BETA_ONE = 0.9
BETA_TWO = 0.95
ADAM_EPS = 1e-08
DECAY = 0.01
GELU_LIN = 0.7978845608
GELU_CUBE = 0.7978845608 * 0.044715

MESH = pl.DeviceIdType.MESH
VMEM_BYTES = 127 * 512 * 1024
bf16 = jnp.bfloat16
f32 = jnp.float32
NN = (((1,), (0,)), ((), ()))
NT = (((1,), (1,)), ((), ()))
TN = (((0,), (0,)), ((), ()))


def mxu(left, right, dims=NN):
    return lax.dot_general(left, right, dims, preferred_element_type=f32)


def layer_norm(value):
    center = value - jnp.mean(value, axis=-1, keepdims=True)
    inverse = lax.rsqrt(jnp.mean(center * center, axis=-1, keepdims=True) + EPS_NORM)
    return (center * inverse, inverse)


def norm_back(grad, normed, inverse):
    mean_grad = jnp.mean(grad, axis=-1, keepdims=True)
    mean_proj = jnp.mean(grad * normed, axis=-1, keepdims=True)
    return inverse * (grad - mean_grad - normed * mean_proj)


def adam(master, first, second, grad):
    first_new = BETA_ONE * first + (1.0 - BETA_ONE) * grad
    second_new = BETA_TWO * second + (1.0 - BETA_TWO) * grad * grad
    fix_one = 1.0 - BETA_ONE**STEP
    fix_two = 1.0 - BETA_TWO**STEP
    update = first_new / fix_one / (jnp.sqrt(second_new / fix_two) + ADAM_EPS) + DECAY * master
    return (master - RATE * update, first_new, second_new)


def gelu_both(value):
    square = value * value
    tanh = jnp.tanh(value * (GELU_CUBE * square + GELU_LIN))
    half = 0.5 * tanh + 0.5
    act = value * half
    slope = half + act * (1.0 - tanh) * (3.0 * GELU_CUBE * square + GELU_LIN)
    return act, slope


def dp_sizes(count):
    side = 4 if count >= 64 else 2
    return count // (side * side), side


class Place:
    def __init__(self, count):
        self.count = count
        self.depth, self.side = dp_sizes(count)
        self.dp = lax.axis_index("dp")
        self.mp = lax.axis_index("mp")
        side = self.side
        self.z = self.dp // (side * side)
        y = (self.dp // side) % side
        x = self.dp % side
        self.a = jnp.where(self.mp == 0, y, x)
        self.b = jnp.where(self.mp == 0, x, y)
        self.slot = self.slot_at(self.a, self.b, self.z)

    def slot_at(self, a, b, z):
        return (a * self.side + b) * self.depth + z

    def device(self, a, b, z):
        side = self.side
        dp = jnp.where(self.mp == 0, (z * side + a) * side + b, (z * side + b) * side + a)
        return (dp, self.mp)

    def slot_of(self, dp, core=None):
        side = self.side
        z, y, x = dp // (side * side), (dp // side) % side, dp % side
        core = self.mp if core is None else core
        return jnp.where(core == 0, self.slot_at(y, x, z), self.slot_at(x, y, z))

    def peers_z(self):
        return [self.device(self.a, self.b, (self.z + k) % self.depth) for k in range(1, self.depth)]

    def peers_b(self):
        return [self.device(self.a, (self.b + k) % self.side, self.z) for k in range(1, self.side)]

    def peers_a(self):
        return [self.device((self.a + k) % self.side, self.b, self.z) for k in range(1, self.side)]

    def other_core(self):
        return (self.dp, 1 - self.mp)

    def greet(self):
        peers = self.peers_z() + self.peers_b() + self.peers_a() + [self.other_core()]
        barrier = pltpu.get_barrier_semaphore()
        for peer in peers:
            pl.semaphore_signal(barrier, inc=1, device_id=peer, device_id_type=MESH)
        pl.semaphore_wait(barrier, len(peers))


def remote(src, dst, send, recv, peer):
    return pltpu.make_async_remote_copy(
        src_ref=src, dst_ref=dst, send_sem=send, recv_sem=recv, device_id=peer, device_id_type=MESH
    )


class Gather:
    def __init__(self, place, buf, send, recv):
        self.p, self.buf, self.send, self.recv = place, buf, send, recv

    def copies(self, stage, e):
        p = self.p
        if stage == 0:
            src = self.buf.at[e, pl.ds(p.slot, 1)]
            peers, base = p.peers_z(), 0
        elif stage == 1:
            src = self.buf.at[e, pl.ds(p.slot_at(p.a, p.b, 0), p.depth)]
            peers, base = p.peers_b(), p.depth - 1
        else:
            src = self.buf.at[e, pl.ds(p.slot_at(p.a, 0, 0), p.depth * p.side)]
            peers, base = p.peers_a(), p.depth - 1 + p.side - 1
        return [
            remote(src, src, self.send.at[e, base + k], self.recv.at[e, base + k], peer)
            for k, peer in enumerate(peers)
        ]

    def start(self, stage, e):
        for copy in self.copies(stage, e):
            copy.start()

    def arrive(self, stage, e):
        for copy in self.copies(stage, e):
            copy.wait_recv()

    def sent(self, e):
        for stage in range(3):
            for copy in self.copies(stage, e):
                copy.wait_send()


class Scatter:
    def __init__(self, place, buf, boxes, send, recv):
        self.p, self.buf, self.boxes, self.send, self.recv = place, buf, boxes, send, recv

    def copies(self, stage, e):
        p = self.p
        made = []
        for k in range(1, p.side if stage < 2 else p.depth):
            if stage == 0:
                a = (p.a + k) % p.side
                src = self.buf.at[e, pl.ds(p.slot_at(a, 0, 0), p.depth * p.side)]
                peer, base = p.device(a, p.b, p.z), 0
            elif stage == 1:
                b = (p.b + k) % p.side
                src = self.buf.at[e, pl.ds(p.slot_at(p.a, b, 0), p.depth)]
                peer, base = p.device(p.a, b, p.z), p.side - 1
            else:
                z = (p.z + k) % p.depth
                src = self.buf.at[e, pl.ds(p.slot_at(p.a, p.b, z), 1)]
                peer, base = p.device(p.a, p.b, z), 2 * (p.side - 1)
            at = base + k - 1
            made.append(remote(src, self.boxes[stage].at[e % SLOTS, k - 1], self.send.at[e, at], self.recv.at[e, at], peer))
        return made

    def start(self, stage, e):
        for copy in self.copies(stage, e):
            copy.start()

    def arrive(self, stage, e):
        for copy in self.copies(stage, e):
            copy.wait()

    def add(self, stage, e):
        p = self.p
        if stage == 0:
            first, many = p.slot_at(p.a, 0, 0), p.depth * p.side
        else:
            first, many = p.slot_at(p.a, p.b, 0), p.depth
        box = self.boxes[stage]

        def one(i, carry):
            total = self.buf[e, first + i].astype(f32)
            for k in range(p.side - 1):
                total = total + box[e % SLOTS, k, i].astype(f32)
            self.buf[e, first + i] = total.astype(bf16)
            return carry

        lax.fori_loop(0, many, one, 0)

    def last(self, e):
        p = self.p
        total = self.buf[e, p.slot].astype(f32)
        for k in range(p.depth - 1):
            total = total + self.boxes[2][e % SLOTS, k, 0].astype(f32)
        return total


def block_rows(rows, parts):
    return (parts * rows + SUB - 1) // SUB * SUB


def blocks_to_weights(place, rows, buf, core, outs):
    many = SUB // math.gcd(SUB, rows)
    for first in range(0, place.count, many):
        blocks = [buf[place.slot_of(first + i, core)].astype(f32) for i in range(many)]
        for part, out in enumerate(outs):
            pieces = [block[part * rows : (part + 1) * rows] for block in blocks]
            out[pl.ds(first * rows, many * rows), :] = jnp.concatenate(pieces, axis=0).astype(bf16)


def grads_to_blocks(place, rows, grads, buf):
    block = buf.shape[1]
    for dp in range(place.count):
        pieces = [grad[dp * rows : (dp + 1) * rows, :] for grad in grads]
        if block > rows * len(grads):
            pieces.append(jnp.zeros((block - rows * len(grads), buf.shape[2]), f32))
        buf[place.slot_of(dp)] = jnp.concatenate(pieces, axis=0).astype(bf16)


def all_sum(place, value, src, box, send, recv):
    stages = (
        (place.depth, place.z, lambda i: place.device(place.a, place.b, i)),
        (place.side, place.b, lambda i: place.device(place.a, i, place.z)),
        (place.side, place.a, lambda i: place.device(i, place.b, place.z)),
        (2, place.mp, lambda i: (place.dp, i)),
    )
    at = 0
    for stage, (many, mine, device) in enumerate(stages):
        src[stage] = value
        box[stage, mine] = value
        copies = []
        for k in range(1, many):
            peer = device((mine + k) % many)
            copies.append(remote(src.at[stage], box.at[stage, mine], send.at[at], recv.at[at], peer))
            at += 1
        for copy in copies:
            copy.start()
        for copy in copies:
            copy.wait()
        value = box[stage, 0]
        for i in range(1, many):
            value = value + box[stage, i]
    return value


def block_kernel(
    count, rows, experts, tile,
    tok_ref, cot_ref, cond_ref, route_ref, ada_ref, gate_ref, attn_ref, w_ref,
    output_ref, grad_tok_ref, ada_out, attn_out, total_ref, norm_out,
    buf, box_a, box_b, box_z,
    ada_buf, ada_a, ada_b, ada_z, attn_buf, attn_a, attn_b, attn_z, attn_far, attn_w, gate_w,
    cond_low, mod, grad_mod, grad_mod_in, triple, mixed, h_one, soft,
    h_all, d_all, gate_all, branch_acc, grad_h_acc, grad_gate_acc, gate_in, share_in,
    up_w, down_w, up_grad, down_grad, gate_grad, gate_grad_in, attn_share, attn_in, norm_src, norm_box,
    load_sem, gather_send, gather_recv, scatter_send, scatter_recv,
    ada_send, ada_recv, attn_send, attn_recv, ada_back_send, ada_back_recv, attn_back_send, attn_back_recv,
    core_send, core_recv, token_send, token_recv, norm_send, norm_recv,
):
    place = Place(count)
    mp = place.mp
    wide_experts = w_ref.shape[1]
    own_tok, width = tok_ref.shape
    images = own_tok // PATCH
    half = attn_ref.shape[2]
    heads = half // HD
    wide = ada_ref.shape[1] // 2
    cut = ada_buf.shape[3]
    scale = HD ** (-0.5)
    own_at = pl.multiple_of(mp * own_tok, own_tok)
    their_at = pl.multiple_of((1 - mp) * own_tok, own_tok)
    own, theirs = pl.ds(own_at, own_tok), pl.ds(their_at, own_tok)
    other = place.other_core()

    loads = [
        pltpu.make_async_copy(tok_ref, branch_acc.at[pl.ds(0, own_tok)], load_sem.at[0]),
        pltpu.make_async_copy(cot_ref, branch_acc.at[pl.ds(own_tok, own_tok)], load_sem.at[1]),
    ]
    for load in loads:
        load.start()

    def put(target, block):
        if block.shape[0] != target.shape[1]:
            target[place.slot] = jnp.zeros(target.shape[1:], bf16)
        target[place.slot, pl.ds(0, block.shape[0])] = block

    cols = ada_ref[:, pl.ds(pl.multiple_of(mp * wide, LANES), wide)]
    gate = jnp.concatenate([gate_ref[...], jnp.zeros((rows, 2 * cut - wide - experts), f32)], axis=1)
    tail = jnp.concatenate([cols[:, cut:], gate], axis=1)
    put(ada_buf.at[0], jnp.concatenate([cols[:, :cut], tail], axis=0).astype(bf16))
    parts = attn_ref.shape[0]
    put(attn_buf.at[0], jnp.concatenate([attn_ref[j] for j in range(parts)], axis=0).astype(bf16))
    place.greet()
    ada_gather = Gather(place, ada_buf, ada_send, ada_recv)
    attn_gather = Gather(place, attn_buf, attn_send, attn_recv)
    gather = Gather(place, buf, gather_send, gather_recv)
    scatter = Scatter(place, buf, (box_a, box_b, box_z), scatter_send, scatter_recv)
    ada_gather.start(0, 0)
    attn_gather.start(0, 0)

    def fill(e, carry):
        put(buf.at[e], jnp.concatenate([w_ref[0, e], w_ref[1, e]], axis=0).astype(bf16))
        return carry

    lax.fori_loop(0, wide_experts, fill, 0)

    def tick(k):
        @pl.when(k + 4 < wide_experts)
        def _():
            gather.start(0, k + 4)

        @pl.when((k + 2 >= 0) & (k + 2 < wide_experts))
        def _():
            gather.arrive(0, k + 2)
            gather.start(1, k + 2)

        @pl.when((k + 1 >= 0) & (k + 1 < wide_experts))
        def _():
            gather.arrive(1, k + 1)
            gather.start(2, k + 1)

    cond = cond_ref[...]
    cond_low[...] = (cond / (1.0 + jnp.exp(-cond))).astype(bf16)
    grad_mod[...] = jnp.zeros_like(grad_mod)
    for stage in range(3):
        for small in (ada_gather, attn_gather):
            small.arrive(stage, 0)
            if stage < 2:
                small.start(stage + 1, 0)
        if stage == 0:
            for e in range(3):
                gather.start(0, e)
    attn_cross = remote(attn_buf.at[0], attn_far, core_send.at[0], core_recv.at[0], other)
    attn_cross.start()

    low_cut = pl.ds(0, cut)
    blocks_to_weights(place, rows, ada_buf.at[0], mp, (up_w.at[:, low_cut], down_w.at[:, low_cut]))
    mod[mp, :, pl.ds(0, cut)] = mxu(cond_low[...], up_w[:, low_cut])
    mod[mp, :, pl.ds(cut, cut)] = mxu(cond_low[...], down_w[:, low_cut])
    gate_w[...] = down_w[:, pl.ds(cut - LANES, LANES)]
    mod_cross = remote(mod.at[mp], mod.at[mp], core_send.at[1], core_recv.at[1], other)
    mod_cross.start()
    blocks_to_weights(place, rows, attn_buf.at[0], mp, [attn_w.at[mp, j] for j in range(parts)])
    for load in loads:
        load.wait()
    ada_gather.sent(0)
    attn_gather.sent(0)
    gather.arrive(0, 0)
    gather.start(1, 0)
    attn_cross.wait()
    blocks_to_weights(place, rows, attn_far, 1 - mp, [attn_w.at[1 - mp, j] for j in range(parts)])
    mod_cross.wait()

    lane_pair = lax.broadcasted_iota(jnp.int32, (PATCH, 2 * HD), 1)
    masks = [(lane_pair < HD).astype(f32).astype(bf16), (lane_pair >= HD).astype(f32).astype(bf16)]
    groups = [(at, min(2, heads - at)) for at in range(0, heads, 2)]
    expert_lane = lax.broadcasted_iota(jnp.int32, (PATCH, LANES), 1)

    def mod_row(image, vector):
        flat = vector % 3 * width
        return mod[vector // 3, pl.ds(mp * images + image, 1), pl.ds(flat, width)]

    def add_grad_mod(image, vector, value):
        grad_mod[vector // 3, pl.ds(mp * images + image, 1), pl.ds(vector % 3 * width, width)] = value

    def one_head(value, group, head):
        return value if group[1] == 1 else value * masks[head]

    def route(h, image):
        logits = jnp.where(expert_lane < experts, mxu(h, gate_w[...]), -jnp.inf)
        power = jnp.exp(logits - jnp.max(logits, axis=1, keepdims=True))
        router = power / jnp.sum(power, axis=1, keepdims=True)
        picks = route_ref[pl.ds(image * PATCH, PATCH), :]
        chosen = jnp.where((picks[:, 0:1] == expert_lane) | (picks[:, 1:2] == expert_lane), 1.0, 0.0)
        return router, chosen

    def attend(at):
        return mxu(mixed[0, at, :], attn_w[0, 3], NT) + mxu(mixed[1, at, :], attn_w[1, 3], NT)

    def token_copies(image):
        at = pl.ds(pl.multiple_of(own_at + image * PATCH, PATCH), PATCH)
        return [
            remote(ref.at[at], ref.at[at], token_send.at[image, i], token_recv.at[image, i], other)
            for i, ref in enumerate((h_all, d_all, gate_all))
        ]

    def forward(image, carry):
        at = pl.ds(pl.multiple_of(image * PATCH, PATCH), PATCH)
        cot_at = pl.ds(pl.multiple_of(own_tok + image * PATCH, PATCH), PATCH)
        all_at = pl.ds(pl.multiple_of(own_at + image * PATCH, PATCH), PATCH)
        normed, _ = layer_norm(branch_acc[at, :])
        h = (normed * (1.0 + mod_row(image, 1)) + mod_row(image, 0)).astype(bf16)
        h_one[at, :] = h
        for core in range(2):
            for j in range(3):
                triple[core, j, at, :] = mxu(h, attn_w[core, j]).astype(bf16)
            for group in groups:
                lanes = pl.ds(group[0] * HD, group[1] * HD)
                query, key, value = (triple[core, j, at, lanes] for j in range(3))
                total = 0.0
                for head in range(group[1]):
                    scores = mxu(one_head(query, group, head), key, NT) * scale
                    power = jnp.exp(scores - jnp.max(scores, axis=1, keepdims=True))
                    low = (power * (1.0 / jnp.sum(power, axis=1, keepdims=True))).astype(bf16)
                    soft[image, core * heads + group[0] + head] = low
                    total = total + mxu(low, one_head(value, group, head))
                mixed[core, at, lanes] = total.astype(bf16)
        x_one = branch_acc[at, :] + mod_row(image, 2) * attend(at)
        normed, _ = layer_norm(x_one)
        h = (normed * (1.0 + mod_row(image, 4)) + mod_row(image, 3)).astype(bf16)
        h_all[all_at, :] = h
        router, chosen = route(h, image)
        shared = (expert_lane >= experts) & (expert_lane < wide_experts)
        gate_all[all_at, :] = jnp.where(shared, 1.0, router * chosen)
        d_all[all_at, :] = (branch_acc[cot_at, :] * mod_row(image, 5)).astype(bf16)
        for copy in token_copies(image):
            copy.start()

        @pl.when(image % 2 == 1)
        def _():
            tick(image // 2 - 1)

        return carry

    lax.fori_loop(0, images, forward, 0)
    ahead = images // 2 - 1

    branch_acc[...] = jnp.zeros_like(branch_acc)
    grad_h_acc[...] = jnp.zeros_like(grad_h_acc)
    grad_gate_acc[...] = jnp.zeros_like(grad_gate_acc)

    def all_tokens(image, carry):
        for copy in token_copies(image):
            copy.wait()
        return carry

    lax.fori_loop(0, images, all_tokens, 0)

    def compute(e):
        blocks_to_weights(place, rows, buf.at[e], mp, (up_w, down_w))
        up_grad[...] = jnp.zeros_like(up_grad)
        down_grad[...] = jnp.zeros_like(down_grad)

        def one_tile(t, carry):
            at = pl.ds(pl.multiple_of(t * tile, tile), tile)
            h = h_all[at, :]
            d = d_all[at, :]
            lane = lax.broadcasted_iota(jnp.int32, (tile, LANES), 1)
            gate = jnp.sum(jnp.where(lane == e, gate_all[at, :], 0.0), axis=1, keepdims=True)
            pre = mxu(h, up_w[...])
            back = mxu(d, down_w[...])
            act, slope = gelu_both(pre)
            inner = jnp.sum(act * back, axis=1, keepdims=True)
            grad_gate_acc[at, :] += jnp.where(lane == e, inner, 0.0)
            act_low = (gate * act).astype(bf16)
            pre_low = (gate * back * slope).astype(bf16)
            branch_acc[at, :] += mxu(act_low, down_w[...], NT)
            grad_h_acc[at, :] += mxu(pre_low, up_w[...], NT)
            up_grad[...] += mxu(h, pre_low, TN)
            down_grad[...] += mxu(d, act_low, TN)
            return carry

        lax.fori_loop(0, h_all.shape[0] // tile, one_tile, 0)

    def collect(k):
        @pl.when((k >= 1) & (k - 1 < wide_experts))
        def _():
            scatter.arrive(0, k - 1)
            scatter.add(0, k - 1)
            scatter.start(1, k - 1)

        @pl.when((k >= 2) & (k - 2 < wide_experts))
        def _():
            scatter.arrive(1, k - 2)
            scatter.add(1, k - 2)
            scatter.start(2, k - 2)

        @pl.when((k >= 3) & (k - 3 < wide_experts))
        def _():
            scatter.arrive(2, k - 3)
            total_ref[k - 3] = scatter.last(k - 3)

    def step(e, carry):
        tick(e + ahead)
        gather.arrive(2, e)
        compute(e)
        gather.sent(e)
        grads_to_blocks(place, rows, (up_grad, down_grad), buf.at[e])
        scatter.start(0, e)
        collect(e)
        return carry

    lax.fori_loop(0, wide_experts, step, 0)

    h_all[theirs, :] = branch_acc[theirs, :].astype(bf16)
    d_all[theirs, :] = grad_h_acc[theirs, :].astype(bf16)
    shares = [
        remote(h_all.at[theirs], share_in.at[0], core_send.at[2], core_recv.at[2], other),
        remote(d_all.at[theirs], share_in.at[1], core_send.at[3], core_recv.at[3], other),
        remote(grad_gate_acc.at[theirs], gate_in, core_send.at[4], core_recv.at[4], other),
    ]
    loads = [
        pltpu.make_async_copy(tok_ref, branch_acc.at[theirs], load_sem.at[0]),
        pltpu.make_async_copy(cot_ref, grad_h_acc.at[theirs], load_sem.at[1]),
    ]
    for copy in shares + loads:
        copy.start()
    gate_grad[...] = jnp.zeros_like(gate_grad)
    for copy in shares + loads:
        copy.wait()

    def backward(image, carry):
        at = pl.ds(pl.multiple_of(image * PATCH, PATCH), PATCH)
        own_rows = pl.ds(pl.multiple_of(own_at + image * PATCH, PATCH), PATCH)
        load_rows = pl.ds(pl.multiple_of(their_at + image * PATCH, PATCH), PATCH)
        tok, cot = branch_acc[load_rows, :], grad_h_acc[load_rows, :]
        branch = branch_acc[own_rows, :] + share_in[0, at, :].astype(f32)
        attention = attend(at)
        x_one = tok + mod_row(image, 2) * attention
        normed, inverse = layer_norm(x_one)
        branch_acc[own_rows, :] = x_one + mod_row(image, 5) * branch
        add_grad_mod(image, 5, jnp.sum(cot * branch, axis=0, keepdims=True))
        h = h_all[own_rows, :]
        router, chosen = route(h, image)
        grad_router = (grad_gate_acc[own_rows, :] + gate_in[at, :]) * chosen
        grad_logits = (router * (grad_router - jnp.sum(router * grad_router, axis=1, keepdims=True))).astype(bf16)
        gate_grad[...] += mxu(h, grad_logits, TN)
        grad_h = grad_h_acc[own_rows, :] + share_in[1, at, :].astype(f32) + mxu(grad_logits, gate_w[...], NT)
        add_grad_mod(image, 3, jnp.sum(grad_h, axis=0, keepdims=True))
        add_grad_mod(image, 4, jnp.sum(grad_h * normed, axis=0, keepdims=True))
        grad_x = cot + norm_back(grad_h * (1.0 + mod_row(image, 4)), normed, inverse)
        add_grad_mod(image, 2, jnp.sum(grad_x * attention, axis=0, keepdims=True))
        grad_att = (grad_x * mod_row(image, 2)).astype(bf16)
        d_all[own_rows, :] = grad_att
        grad_h_one = 0.0
        for core in range(2):
            grad_mixed = mxu(grad_att, attn_w[core, 3]).astype(bf16)
            for group in groups:
                lanes = pl.ds(group[0] * HD, group[1] * HD)
                query, key, value = (triple[core, j, at, lanes] for j in range(3))
                back = grad_mixed[:, group[0] * HD : (group[0] + group[1]) * HD]
                grads = [0.0, 0.0, 0.0]
                for head in range(group[1]):
                    low = soft[image, core * heads + group[0] + head]
                    prob = low.astype(f32)
                    head_back = one_head(back, group, head)
                    grad_soft = mxu(head_back, value, NT)
                    delta = jnp.sum(prob * grad_soft, axis=1, keepdims=True)
                    grad_scores = (prob * (grad_soft - delta) * scale).astype(bf16)
                    grads[0] = grads[0] + mxu(grad_scores, one_head(key, group, head))
                    grads[1] = grads[1] + mxu(grad_scores, one_head(query, group, head), TN)
                    grads[2] = grads[2] + mxu(low, head_back, TN)
                for j in range(3):
                    triple[core, j, at, lanes] = grads[j].astype(bf16)
            for j in range(3):
                grad_h_one = grad_h_one + mxu(triple[core, j, at, :], attn_w[core, j], NT)
        normed, inverse = layer_norm(tok)
        add_grad_mod(image, 0, jnp.sum(grad_h_one, axis=0, keepdims=True))
        add_grad_mod(image, 1, jnp.sum(grad_h_one * normed, axis=0, keepdims=True))
        grad_h_acc[own_rows, :] = grad_x + norm_back(grad_h_one * (1.0 + mod_row(image, 1)), normed, inverse)
        collect(wide_experts + image)
        return carry

    lax.fori_loop(0, images, backward, 0)
    for k in range(images, 3):
        collect(wide_experts + k)
    stores = [
        pltpu.make_async_copy(branch_acc.at[own], output_ref, load_sem.at[2]),
        pltpu.make_async_copy(grad_h_acc.at[own], grad_tok_ref, load_sem.at[3]),
    ]
    for copy in stores:
        copy.start()

    crosses = [
        remote(grad_mod.at[1 - mp], grad_mod_in, core_send.at[5], core_recv.at[5], other),
        remote(gate_grad, gate_grad_in, core_send.at[6], core_recv.at[6], other),
        remote(attn_share, attn_in, core_send.at[7], core_recv.at[7], other),
    ]
    crosses[0].start()
    crosses[1].start()

    def attn_grad(core, j):
        if j == parts - 1:
            return mxu(d_all[own, :], mixed[core], TN)
        return mxu(h_one[...], triple[core, j], TN)

    for j in range(parts):
        attn_share[j] = attn_grad(1 - mp, j).astype(bf16)

    crosses[2].start()
    ada_scatter = Scatter(place, ada_buf, (ada_a, ada_b, ada_z), ada_back_send, ada_back_recv)
    attn_scatter = Scatter(place, attn_buf, (attn_a, attn_b, attn_z), attn_back_send, attn_back_recv)
    crosses[0].wait()
    crosses[1].wait()
    grad_low = (grad_mod[mp] + grad_mod_in[...]).astype(bf16)
    up_grad[:, low_cut] = mxu(cond_low[...], grad_low[:, :cut], TN)
    down_grad[:, low_cut] = mxu(cond_low[...], grad_low[:, cut:], TN)
    down_grad[:, pl.ds(cut - LANES, LANES)] = gate_grad[...] + gate_grad_in[...]
    grads_to_blocks(place, rows, (up_grad[:, low_cut], down_grad[:, low_cut]), ada_buf.at[0])
    ada_scatter.start(0, 0)
    crosses[2].wait()
    grads = [attn_grad(mp, j) + attn_in[j].astype(f32) for j in range(parts)]
    grads_to_blocks(place, rows, grads, attn_buf.at[0])
    attn_scatter.start(0, 0)
    scatters = (ada_scatter, attn_scatter)
    for stage in range(2):
        for small in scatters:
            small.arrive(stage, 0)
            small.add(stage, 0)
            small.start(stage + 1, 0)
    square = jnp.zeros((1, 1), f32)
    for e in range(wide_experts):
        square = square + jnp.sum(total_ref[e] * total_ref[e])
    for small in scatters:
        small.arrive(2, 0)
    ada, attn = ada_scatter.last(0), attn_scatter.last(0)
    ada_out[...] = ada
    attn_out[...] = attn
    row = lax.broadcasted_iota(jnp.int32, ada.shape, 0)
    lane = lax.broadcasted_iota(jnp.int32, ada.shape, 1)
    twice = (row >= rows) & (lane >= cut - LANES)
    square = square + jnp.sum(jnp.where(twice, 0.5, 1.0) * ada * ada) + jnp.sum(attn * attn)
    value = jnp.broadcast_to(square, norm_out.shape)
    norm_out[...] = all_sum(place, value, norm_src, norm_box, norm_send, norm_recv)
    for copy in stores:
        copy.wait()


def block_call(tokens, condition, cotangent, routes, w_ada, w_gate, w_attn, w_expert):
    count = lax.axis_size("dp")
    own_tok, width = tokens.shape
    rows, wide = w_ada.shape
    experts = w_gate.shape[1]
    parts, _, half = w_attn.shape
    _, wide_experts, _, hidden = w_expert.shape
    depth, side = dp_sizes(count)
    images = own_tok // PATCH
    cut = (wide // 2 + LANES) // 2
    block, ada_block, attn_block = block_rows(rows, 2), block_rows(rows, 2), block_rows(rows, parts)
    tok = 2 * own_tok
    tile = TILE if count <= 16 else TILE // 2
    vmem = pl.BlockSpec(memory_space=pltpu.VMEM)
    hbm = pl.BlockSpec(memory_space=pl.ANY)
    hops = depth + 2 * side - 3

    def sems(*shape):
        return pltpu.SemaphoreType.DMA(shape)

    def boxes(slots, height, lanes):
        return [
            pltpu.VMEM((slots, side - 1, side * depth, height, lanes), bf16),
            pltpu.VMEM((slots, side - 1, depth, height, lanes), bf16),
            pltpu.VMEM((slots, depth - 1, 1, height, lanes), bf16),
        ]

    return pl.pallas_call(
        functools.partial(block_kernel, count, rows, experts, tile),
        out_shape=(
            jax.ShapeDtypeStruct((own_tok, width), f32),
            jax.ShapeDtypeStruct((own_tok, width), f32),
            jax.ShapeDtypeStruct((ada_block, cut), f32),
            jax.ShapeDtypeStruct((attn_block, half), f32),
            jax.ShapeDtypeStruct((wide_experts, block, hidden), f32),
            jax.ShapeDtypeStruct((8, LANES), f32),
        ),
        in_specs=[hbm, hbm] + [vmem] * 6,
        out_specs=(hbm, hbm) + (vmem,) * 4,
        scratch_shapes=[
            pltpu.VMEM((wide_experts, count, block, hidden), bf16),
            *boxes(SLOTS, block, hidden),
            pltpu.VMEM((1, count, ada_block, cut), bf16),
            *boxes(1, ada_block, cut),
            pltpu.VMEM((1, count, attn_block, half), bf16),
            *boxes(1, attn_block, half),
            pltpu.VMEM((count, attn_block, half), bf16),
            pltpu.VMEM((2, parts, width, half), bf16),
            pltpu.VMEM((width, LANES), bf16),
            pltpu.VMEM(condition.shape, bf16),
            pltpu.VMEM((2, condition.shape[0], 2 * cut), f32),
            pltpu.VMEM((2, condition.shape[0], 2 * cut), f32),
            pltpu.VMEM((condition.shape[0], 2 * cut), f32),
            pltpu.VMEM((2, 3, own_tok, half), bf16),
            pltpu.VMEM((2, own_tok, half), bf16),
            pltpu.VMEM((own_tok, width), bf16),
            pltpu.VMEM((images, width // HD, PATCH, PATCH), bf16),
            pltpu.VMEM((tok, width), bf16),
            pltpu.VMEM((tok, width), bf16),
            pltpu.VMEM((tok, LANES), f32),
            pltpu.VMEM((tok, width), f32),
            pltpu.VMEM((tok, width), f32),
            pltpu.VMEM((tok, LANES), f32),
            pltpu.VMEM((own_tok, LANES), f32),
            pltpu.VMEM((2, own_tok, width), bf16),
            pltpu.VMEM((width, hidden), bf16),
            pltpu.VMEM((width, hidden), bf16),
            pltpu.VMEM((width, hidden), f32),
            pltpu.VMEM((width, hidden), f32),
            pltpu.VMEM((width, LANES), f32),
            pltpu.VMEM((width, LANES), f32),
            pltpu.VMEM((parts, width, half), bf16),
            pltpu.VMEM((parts, width, half), bf16),
            pltpu.VMEM((4, 8, LANES), f32),
            pltpu.VMEM((4, max(depth, side), 8, LANES), f32),
            sems(4),
            *[sems(wide_experts, hops)] * 4,
            *[sems(1, hops)] * 8,
            sems(8),
            sems(8),
            sems(images, 3),
            sems(images, 3),
            sems(hops + 1),
            sems(hops + 1),
        ],
        compiler_params=pltpu.CompilerParams(collective_id=1, has_side_effects=True, vmem_limit_bytes=VMEM_BYTES),
        cost_estimate=pl.CostEstimate(
            flops=12 * tok * width * hidden * wide_experts, bytes_accessed=16 * w_expert.size, transcendentals=0
        ),
        name="block",
    )(tokens, cotangent, condition, routes, w_ada, w_gate, w_attn, w_expert)


def per_device(
    tokens,
    condition,
    cotangent,
    routes,
    w_ada,
    ada_first,
    ada_second,
    w_gate,
    gate_first,
    gate_second,
    w_attn,
    attn_first,
    attn_second,
    w_expert,
    expert_first,
    expert_second,
):
    tok_dev, width = tokens.shape
    experts = w_gate.shape[1]
    rows = w_expert.shape[2]
    half = w_attn.shape[2]
    wide = w_ada.shape[1] // 2
    own_routes = lax.dynamic_slice_in_dim(routes, lax.axis_index("mp") * tok_dev, tok_dev, 0)
    output, grad_tokens, ada_block, attn_block, expert_blocks, square_sum = block_call(
        tokens, condition, cotangent, own_routes, w_ada, w_gate, w_attn, w_expert
    )
    expert_total = expert_blocks[:, : 2 * rows].reshape(-1, 2, rows, w_expert.shape[3]).transpose(1, 0, 2, 3)
    ada_half = jnp.concatenate([ada_block[:rows], ada_block[rows : 2 * rows]], axis=1)
    gate_total = ada_half[:, wide : wide + experts]
    ada_total = lax.all_gather(ada_half[:, :wide], "mp", axis=1, tiled=True)
    attn_total = attn_block[: 4 * rows].reshape(4, rows, half)
    grad_norm = jnp.sqrt(square_sum[0, 0])
    factor = jnp.minimum(1.0, CLIP_NORM / (grad_norm + 1e-06))
    ada_new, ada_first_new, ada_second_new = adam(w_ada, ada_first, ada_second, ada_total * factor)
    gate_new, gate_first_new, gate_second_new = adam(
        w_gate, gate_first, gate_second, gate_total * factor
    )
    attn_new, attn_first_new, attn_second_new = adam(
        w_attn, attn_first, attn_second, attn_total * factor
    )
    expert_new, expert_first_new, expert_second_new = adam(
        w_expert, expert_first, expert_second, expert_total * factor
    )
    return (
        output,
        grad_tokens,
        grad_norm,
        ada_new,
        ada_first_new,
        ada_second_new,
        gate_new,
        gate_first_new,
        gate_second_new,
        attn_new,
        attn_first_new,
        attn_second_new,
        expert_new,
        expert_first_new,
        expert_second_new,
    )


def solution(mesh):
    placed = (
        P(("dp", "mp"), None),
        P("dp", None),
        P(("dp", "mp"), None),
        P("dp", None),
        P("dp", None),
        P("dp", None),
        P("dp", None),
        P("dp", None),
        P("dp", None),
        P("dp", None),
        P(None, "dp", "mp"),
        P(None, "dp", "mp"),
        P(None, "dp", "mp"),
        P(None, None, "dp", "mp"),
        P(None, None, "dp", "mp"),
        P(None, None, "dp", "mp"),
    )
    return jax.shard_map(
        per_device,
        mesh=mesh,
        in_specs=placed,
        out_specs=(
            P(("dp", "mp"), None),
            P(("dp", "mp"), None),
            P(),
            P("dp", None),
            P("dp", None),
            P("dp", None),
            P("dp", None),
            P("dp", None),
            P("dp", None),
            P(None, "dp", "mp"),
            P(None, "dp", "mp"),
            P(None, "dp", "mp"),
            P(None, None, "dp", "mp"),
            P(None, None, "dp", "mp"),
            P(None, None, "dp", "mp"),
        ),
        check_vma=False,
    )
```

time: 639 us -> 321 us (0.50)
  blocking collectives: 166 us -> 1.95 us
  waiting for transfers between devices: 113 us -> 0 us
  Pallas kernels: 232 us -> 294 us
  other arithmetic: 40.7 us -> 10.8 us
  local copies, waits for them, and re-layouts: 37.9 us -> 10.9 us
  matrix products: 26.4 us -> 0 us
  between operations: 19.4 us -> 2.63 us
    all_gather x3 -> x1, blocking collectives: 84.8 us -> 1.95 us  [per_device(): ada_total = lax.all_gather(ada_half[:, :wide], 'mp', axis=1, tiled=True)]
    psum x2 -> x0, blocking collectives: 81 us -> none  [the longest x1 41 us: per_device(): gate_total = lax.psum(grad_gate_w, ('dp', 'mp'))]
    unnamed x5 -> x0, waiting for transfers between devices: 80.3 us -> none
    pallas_call x1, Pallas kernels: 232 us -> 294 us  [block_call(): pl.pallas_call(functools.partial(block_kernel, count, rows, experts, tile...]
    dot_general x17 -> x0, matrix products: 26.4 us -> none  [the longest x1 5.06 us: per_device(): jnp.einsum('ihqk,iqhc->ikhc', soft_low, grad_mixed_heads, preferred_eleme...]
    all_gather x2 -> x0, waiting for transfers between devices: 22.6 us -> none  [the longest x1 22.6 us: per_device(): ada_low = lax.all_gather(w_ada.astype(bf16), 'dp', axis=0, tiled=True)]
    reduce_sum x15 -> x0, other arithmetic: 15.3 us -> none  [the longest x1 2.91 us: per_device(): grad_gate_one = jnp.sum(grad_x_one * attention_img, axis=1, keepdims=True)]
    reduce_scatter x1 -> x0, waiting for transfers between devices: 10.6 us -> none  [per_device(): small = lax.psum_scatter(small, 'mp', scatter_dimension=0, tiled=False)]
  transfers between devices with their start and end apart: 4 -> 0, of which waited for: 3 -> 0; matrix products, arithmetic and copies ran while one was open for 2% -> 0% of each run, Pallas kernels for 0% -> 0%
where the time goes in v2:
time: 321 us; the launch traced here: 320 us
  Pallas kernels  294 us (92%)
  local copies, waits for them, and re-layouts  10.9 us (3%)
  other arithmetic  10.8 us (3%)
    pallas_call x1, Pallas kernels, block_call(): pl.pallas_call(functools.partial(block_kernel, count, rows, experts, tile...  294 us
    unnamed x27, local copies, waits for them, and re-layouts  9.75 us
    sub x4, other arithmetic, adam(): return (master - RATE * update, first_new, second_new)  9.19 us

profile of v2, /device:TPU:0, one launch (start us, length us, event | category | flops | bytes accessed | tf_op | source)
XLA Modules:
  0.0 320.5 jit_solution(11650920269343586347)
XLA Ops:
  0.6 0.0 copy-start
  0.7 0.7 copy-done
  1.4 1.4 copy.42.gate_ref
  2.7 0.8 copy.43
  3.5 0.8 copy.45
  4.2 1.0 copy.52.route_ref
  5.3 0.0 copy-start.8
  5.3 294.2 %block.1 = (f32[1024,384]{1,0:T(8,128)}, f32[1024,384]{1,0:T(8,128)}, f32[48,640]{1,0:T(8,128)}, f32[96,192]{1,0:T(8,128)}, f32[10,48,768]{2,1,0:T(8,128)}, /*index=5*/f32[8,128]{1,0:T(8,128)}) custom-call(f32[1024,384]{1,0:T(8,128)} %tok_ref.1, f32[1024,384]{1,0:T(8,128)} %cot_ref.1, f32[8,384]{1,0:T(8,128)} %cond_ref.1, s32[1024,2]{1,0:T(8,128)} %copy.52.route_ref, ...), custom_call_target="tpu_custom_call" | custom-call | flops 72477573120 | bytes 5898240 | tf_op jit(solution)/shard_map/block/pallas_call | solution.py:679
  299.5 1.2 slice.16
  301.4 0.0 copy-done.8
  301.4 0.7 multiply_subtract_fusion.3
  302.2 0.0 copy-start.6
  302.2 0.0 copy-start.5
  302.2 0.0 copy-start.7
  302.2 1.6 broadcast_multiply_fusion
  303.8 0.0 copy-start.4
  303.8 0.0 copy-done.6
  303.8 0.7 copy.49
  304.5 0.0 copy-done.5
  304.5 0.0 copy-start.3
  304.5 0.7 copy.50
  305.2 0.7 copy.51
  305.8 2.0 all_gather.3
  307.8 0.0 copy-done.7
  307.8 1.7 multiply_subtract_fusion.2
  309.5 0.0 copy-done.4
  309.5 2.0 multiply_subtract_fusion.1
  311.4 0.0 copy-done.3
  311.5 0.0 copy-start.2
  311.5 4.8 %multiply_subtract_fusion = (f32[2,10,24,768]{3,2,1,0:T(8,128)}, f32[2,10,24,768]{3,2,1,0:T(8,128)}, f32[2,10,24,768]{3,2,1,0:T(8,128)}) fusion(f32[2,10,24,768]{3,2,1,0:T(8,128)S(1)} %copy-done.3, f32[10,2,24,768]{3,2,1,0:T(8,128)S(1)} %bitcast.10, f32[2,10,24,768]{3,2,1,0:T(8,128)} %param.30, f32[2,10,24,768]{3,2,1,0:T(8,128)} %param.31), kind=kLoop, calls=%fused_computation.4 | loop fusion | flops 5529600 | bytes 10321920 | tf_op jit(solution)/shard_map/sub | solution.py:60
  316.2 0.0 copy-done.2
  316.2 0.0 copy-start.1
  316.2 1.1 copy.59
  317.4 0.8 copy-done.1
  318.2 1.1 copy.60
  (4 shorter events, 0.0 us)
Async XLA Ops:
  0.6 0.7 copy-start
  5.3 296.1 %copy-start.8 = (f32[24,8]{1,0:T(8,128)S(1)}, f32[24,8]{1,0:T(8,128)}, u32[]{:S(2)}) copy-start(f32[24,8]{1,0:T(8,128)} %copy.42.gate_ref) | copy-start | bytes 2308
  302.2 1.6 copy-start.6
  302.2 2.3 copy-start.5
  302.2 5.6 %copy-start.7 = (f32[4,24,192]{2,1,0:T(8,128)S(1)}, f32[4,24,192]{2,1,0:T(8,128)}, u32[]{:S(2)}) copy-start(f32[4,24,192]{2,1,0:T(8,128)} %attn_ref.1) | copy-start | bytes 221188
  303.8 5.7 %copy-start.4 = (f32[24,2304]{1,0:T(8,128)S(1)}, f32[24,2304]{1,0:T(8,128)}, u32[]{:S(2)}) copy-start(f32[24,2304]{1,0:T(8,128)} %ada_ref.1) | copy-start | bytes 663556
  304.5 7.0 %copy-start.3 = (f32[2,10,24,768]{3,2,1,0:T(8,128)S(1)}, f32[2,10,24,768]{3,2,1,0:T(8,128)}, u32[]{:S(2)}) copy-start(f32[2,10,24,768]{3,2,1,0:T(8,128)} %w_ref.1) | copy-start | bytes 4423684
  311.5 4.8 %copy-start.2 = (f32[1024,384]{1,0:T(8,128)S(1)}, f32[1024,384]{1,0:T(8,128)}, u32[]{:S(2)}) copy-start(f32[1024,384]{1,0:T(8,128)} %get-tuple-element.86) | copy-start | bytes 4718596
  316.2 2.0 copy-start.1

commit v3 on v2

v3 whole, which is shorter than its diff:
```python
import functools
import math

import jax
import jax.numpy as jnp
from jax import lax
from jax.experimental import pallas as pl
from jax.experimental.pallas import tpu as pltpu
from jax.sharding import PartitionSpec as P

HD = 64
PATCH = 256
STEP = 10
LANES = 128
SUB = 16
TILE = 512
SLOTS = 4
ZBA, BZA = "zba", "bza"
CUT_ONE, CUT_ALL = 2, 3

EPS_NORM = 1e-06
CLIP_NORM = 0.1
RATE = 0.08
BETA_ONE = 0.9
BETA_TWO = 0.95
ADAM_EPS = 1e-08
DECAY = 0.01
GELU_LIN = 0.7978845608
GELU_CUBE = 0.7978845608 * 0.044715

MESH = pl.DeviceIdType.MESH
VMEM_BYTES = 127 * 512 * 1024
bf16 = jnp.bfloat16
f32 = jnp.float32
NN = (((1,), (0,)), ((), ()))
NT = (((1,), (1,)), ((), ()))
TN = (((0,), (0,)), ((), ()))


def mxu(left, right, dims=NN):
    return lax.dot_general(left, right, dims, preferred_element_type=f32)


def layer_norm(value):
    center = value - jnp.mean(value, axis=-1, keepdims=True)
    inverse = lax.rsqrt(jnp.mean(center * center, axis=-1, keepdims=True) + EPS_NORM)
    return (center * inverse, inverse)


def norm_back(grad, normed, inverse):
    mean_grad = jnp.mean(grad, axis=-1, keepdims=True)
    mean_proj = jnp.mean(grad * normed, axis=-1, keepdims=True)
    return inverse * (grad - mean_grad - normed * mean_proj)


def adam(master, first, second, grad):
    first_new = BETA_ONE * first + (1.0 - BETA_ONE) * grad
    second_new = BETA_TWO * second + (1.0 - BETA_TWO) * grad * grad
    fix_one = 1.0 - BETA_ONE**STEP
    fix_two = 1.0 - BETA_TWO**STEP
    update = first_new / fix_one / (jnp.sqrt(second_new / fix_two) + ADAM_EPS) + DECAY * master
    return (master - RATE * update, first_new, second_new)


def gelu_both(value):
    square = value * value
    tanh = jnp.tanh(value * (GELU_CUBE * square + GELU_LIN))
    half = 0.5 * tanh + 0.5
    act = value * half
    slope = half + act * (1.0 - tanh) * (3.0 * GELU_CUBE * square + GELU_LIN)
    return act, slope


def dp_sizes(count):
    side = 4 if count >= 64 else 2
    return count // (side * side), side


class Place:
    def __init__(self, count):
        self.count = count
        self.depth, self.side = dp_sizes(count)
        self.dp = lax.axis_index("dp")
        self.mp = lax.axis_index("mp")
        side = self.side
        y = (self.dp // side) % side
        x = self.dp % side
        self.at = {
            "z": self.dp // (side * side),
            "a": jnp.where(self.mp == 0, y, x),
            "b": jnp.where(self.mp == 0, x, y),
        }
        self.size = {"z": self.depth, "a": side, "b": side}

    def slot_at(self, order, at):
        slot = 0
        for axis in reversed(order):
            slot = slot * self.size[axis] + at.get(axis, 0)
        return slot

    def slot(self, order=ZBA):
        return self.slot_at(order, self.at)

    def slot_of(self, dp, core, order=ZBA):
        side = self.side
        z, y, x = dp // (side * side), (dp // side) % side, dp % side
        one = self.slot_at(order, {"z": z, "a": y, "b": x})
        two = self.slot_at(order, {"z": z, "a": x, "b": y})
        return jnp.where(core == 0, one, two)

    def device(self, at):
        z, a, b = at["z"], at["a"], at["b"]
        side = self.side
        dp = jnp.where(self.mp == 0, (z * side + a) * side + b, (z * side + b) * side + a)
        return (dp, self.mp)

    def along(self, axis, step):
        return (self.at[axis] + step) % self.size[axis]

    def peers(self, axis):
        return [self.device({**self.at, axis: self.along(axis, k)}) for k in range(1, self.size[axis])]

    def other_core(self):
        return (self.dp, 1 - self.mp)

    def peers_layer(self):
        layer = self.side * self.side
        first = self.dp - self.dp % layer
        peers = []
        for k in range(1, 2 * layer):
            spot = (self.dp % layer * 2 + self.mp + k) % (2 * layer)
            peers.append((first + spot // 2, spot % 2))
        return peers

    def greet(self):
        peers = self.peers("z") + self.peers_layer()
        barrier = pltpu.get_barrier_semaphore()
        for peer in peers:
            pl.semaphore_signal(barrier, inc=1, device_id=peer, device_id_type=MESH)
        pl.semaphore_wait(barrier, len(peers))


def remote(src, dst, send, recv, peer):
    return pltpu.make_async_remote_copy(
        src_ref=src, dst_ref=dst, send_sem=send, recv_sem=recv, device_id=peer, device_id_type=MESH
    )


def span(place, order, stage):
    return math.prod(place.size[axis] for axis in order[:stage])


class Gather:
    def __init__(self, place, buf, send, recv, order=ZBA):
        self.p, self.buf, self.send, self.recv, self.order = place, buf, send, recv, order

    def copies(self, stage, e):
        p, order = self.p, self.order
        fixed = {axis: p.at[axis] for axis in order[stage:]}
        src = self.buf.at[e, pl.ds(p.slot_at(order, fixed), span(p, order, stage))]
        base = sum(p.size[axis] - 1 for axis in order[:stage])
        return [
            remote(src, src, self.send.at[e, base + k], self.recv.at[e, base + k], peer)
            for k, peer in enumerate(p.peers(order[stage]))
        ]

    def start(self, stage, e):
        for copy in self.copies(stage, e):
            copy.start()

    def arrive(self, stage, e):
        for copy in self.copies(stage, e):
            copy.wait_recv()

    def sent(self, e):
        for stage in range(3):
            for copy in self.copies(stage, e):
                copy.wait_send()


class Scatter:
    def __init__(self, place, buf, box, send, recv, order=ZBA):
        self.p, self.buf, self.box, self.send, self.recv, self.order = place, buf, box, send, recv, order

    def parts(self, stage):
        p, order = self.p, self.order
        base = 0
        for before in range(3 - 1, 2 - stage, -1):
            base += (p.size[order[before]] - 1) * span(p, order, before)
        return order[2 - stage], span(p, order, 2 - stage), base

    def copies(self, stage, e):
        p, order = self.p, self.order
        axis, many, base = self.parts(stage)
        sem = sum(p.size[order[2 - before]] - 1 for before in range(stage))
        made = []
        for k, peer in enumerate(p.peers(axis)):
            fixed = {name: p.at[name] for name in order[2 - stage :]}
            fixed[axis] = p.along(axis, k + 1)
            src = self.buf.at[e, pl.ds(p.slot_at(order, fixed), many)]
            dst = self.box.at[e % SLOTS, pl.ds(base + k * many, many)]
            made.append(remote(src, dst, self.send.at[e, sem + k], self.recv.at[e, sem + k], peer))
        return made

    def start(self, stage, e):
        for copy in self.copies(stage, e):
            copy.start()

    def arrive(self, stage, e):
        for copy in self.copies(stage, e):
            copy.wait()

    def add(self, stage, e):
        p, order = self.p, self.order
        axis, many, base = self.parts(stage)
        first = p.slot_at(order, {name: p.at[name] for name in order[2 - stage :]})

        def one(i, carry):
            total = self.buf[e, first + i].astype(f32)
            for k in range(p.size[axis] - 1):
                total = total + self.box[e % SLOTS, base + k * many + i].astype(f32)
            self.buf[e, first + i] = total.astype(bf16)
            return carry

        lax.fori_loop(0, many, one, 0)

    def last(self, e):
        p, order = self.p, self.order
        axis, many, base = self.parts(2)
        total = self.buf[e, p.slot(order)].astype(f32)
        for k in range(p.size[axis] - 1):
            total = total + self.box[e % SLOTS, base + k].astype(f32)
        return total


def block_rows(rows, parts):
    return (parts * rows + SUB - 1) // SUB * SUB


def blocks_to_weights(place, rows, buf, core, outs, order=ZBA):
    many = SUB // math.gcd(SUB, rows)
    for first in range(0, place.count, many):
        blocks = [buf[place.slot_of(first + i, core, order)].astype(f32) for i in range(many)]
        for part, out in enumerate(outs):
            pieces = [block[part * rows : (part + 1) * rows] for block in blocks]
            out[pl.ds(first * rows, many * rows), :] = jnp.concatenate(pieces, axis=0).astype(bf16)


def grads_to_blocks(place, rows, grads, buf, order=ZBA):
    block = buf.shape[1]
    for dp in range(place.count):
        pieces = [grad[dp * rows : (dp + 1) * rows, :] for grad in grads]
        if block > rows * len(grads):
            pieces.append(jnp.zeros((block - rows * len(grads), buf.shape[2]), f32))
        buf[place.slot_of(dp, place.mp, order)] = jnp.concatenate(pieces, axis=0).astype(bf16)


def all_sum(place, value, src, box, send, recv):
    layer = place.side * place.side
    spot = place.dp % layer
    z = place.at["z"]
    src[0] = value
    box[z] = value
    copies = [
        remote(src.at[0], box.at[z], send.at[k], recv.at[k], peer) for k, peer in enumerate(place.peers("z"))
    ]
    for copy in copies:
        copy.start()
    for copy in copies:
        copy.wait()
    total = box[0]
    for i in range(1, place.depth):
        total = total + box[i]
    mine = spot * 2 + place.mp
    base = place.depth
    src[1] = total
    box[base + mine] = total
    at = place.depth - 1
    copies = [
        remote(src.at[1], box.at[base + mine], send.at[at + k], recv.at[at + k], peer)
        for k, peer in enumerate(place.peers_layer())
    ]
    for copy in copies:
        copy.start()
    for copy in copies:
        copy.wait()
    total = box[base]
    for i in range(1, 2 * layer):
        total = total + box[base + i]
    return total


class Both:
    def __init__(self, *both):
        self.both = both

    def start(self, stage, e):
        for one in self.both:
            one.start(stage, e)

    def arrive(self, stage, e):
        for one in self.both:
            one.arrive(stage, e)

    def add(self, stage, e):
        for one in self.both:
            one.add(stage, e)

    def sent(self, e):
        for one in self.both:
            one.sent(e)


def block_kernel(
    count, rows, experts, tile,
    tok_ref, cot_ref, cond_ref, route_ref, ada_ref, gate_ref, attn_ref, w_ref,
    output_ref, grad_tok_ref, ada_out, attn_out, total_ref, norm_out,
    buf_one, buf_two, box_one, box_two,
    ada_buf, sc_buf, mod_buf, mod_far, attn_buf, attn_box, attn_far, attn_w,
    cond_low, mod, grad_mod, grad_mod_in, triple, mixed, h_one, soft,
    h_all, d_all, gate_all, branch_acc, grad_h_acc, grad_gate_acc, gate_in, share_in,
    up_w, down_w, up_grad, down_grad, gate_grad, attn_share, attn_in, norm_src, norm_box,
    load_sem, gather_send, gather_recv, gather_send_two, gather_recv_two,
    scatter_send, scatter_recv, scatter_send_two, scatter_recv_two,
    ada_send, ada_recv, sc_send, sc_recv, mod_send, mod_recv, attn_send, attn_recv, attn_back_send, attn_back_recv,
    core_send, core_recv, token_send, token_recv, norm_send, norm_recv,
):
    place = Place(count)
    mp = place.mp
    wide_experts = w_ref.shape[1]
    own_tok, width = tok_ref.shape
    images = own_tok // PATCH
    half = attn_ref.shape[2]
    first = half // LANES * LANES
    heads = half // HD
    wide = ada_ref.shape[1] // 2
    cut = ada_buf.shape[3]
    scale = HD ** (-0.5)
    own_at = pl.multiple_of(mp * own_tok, own_tok)
    their_at = pl.multiple_of((1 - mp) * own_tok, own_tok)
    own, theirs = pl.ds(own_at, own_tok), pl.ds(their_at, own_tok)
    other = place.other_core()

    loads = [
        pltpu.make_async_copy(tok_ref, branch_acc.at[pl.ds(0, own_tok)], load_sem.at[0]),
        pltpu.make_async_copy(cot_ref, branch_acc.at[pl.ds(own_tok, own_tok)], load_sem.at[1]),
    ]
    for load in loads:
        load.start()

    def put(target, block, order=ZBA):
        if block.shape[0] != target.shape[1]:
            target[place.slot(order)] = jnp.zeros(target.shape[1:], bf16)
        target[place.slot(order), pl.ds(0, block.shape[0])] = block

    cols = ada_ref[:, pl.ds(pl.multiple_of(mp * wide, LANES), wide)]
    tail = jnp.concatenate([cols[:, cut:], jnp.zeros((rows, 2 * cut - wide), f32)], axis=1)
    put(ada_buf.at[0], jnp.concatenate([cols[:, :cut], tail], axis=0).astype(bf16))
    parts = attn_ref.shape[0]
    side_by = lax.broadcasted_iota(jnp.int32, (experts, LANES), 1) == lax.broadcasted_iota(
        jnp.int32, (experts, LANES), 0
    )
    gate = mxu(gate_ref[...].astype(bf16), side_by.astype(f32).astype(bf16), TN)[:, : 2 * LANES - half]
    spare = [gate] + [jnp.zeros_like(gate)] * (parts - 1)
    both = [jnp.concatenate([attn_ref[j], spare[j]], axis=1) for j in range(parts)]
    put(attn_buf.at[0], jnp.concatenate(both, axis=0).astype(bf16))
    cond = cond_ref[...]
    cond = cond / (1.0 + jnp.exp(-cond))
    cond_low[...] = cond.astype(bf16)
    sc_buf[0, place.slot()] = jnp.concatenate([cond, jnp.zeros((SUB - cond.shape[0], width), f32)], axis=0).astype(bf16)
    place.greet()
    ada_gather = Gather(place, ada_buf, ada_send, ada_recv)
    attn_gather = Gather(place, attn_buf, attn_send, attn_recv)
    cuts = (pl.ds(0, buf_one.shape[3]), pl.ds(buf_one.shape[3], buf_two.shape[3]))
    streams = tuple(zip((buf_one, buf_two), cuts, (ZBA, BZA)))
    gather = Both(
        Gather(place, buf_one, gather_send, gather_recv, ZBA),
        Gather(place, buf_two, gather_send_two, gather_recv_two, BZA),
    )
    scatter = Both(
        Scatter(place, buf_one, box_one, scatter_send, scatter_recv, ZBA),
        Scatter(place, buf_two, box_two, scatter_send_two, scatter_recv_two, BZA),
    )
    sc_gather = Gather(place, sc_buf, sc_send, sc_recv)
    ada_gather.start(0, 0)
    attn_gather.start(0, 0)
    sc_gather.start(0, 0)

    def fill(e, carry):
        both = jnp.concatenate([w_ref[0, e], w_ref[1, e]], axis=0).astype(bf16)
        for buf, lanes, order in streams:
            put(buf.at[e], both[:, lanes.start : lanes.start + lanes.size], order)
        return carry

    lax.fori_loop(0, wide_experts, fill, 0)

    def tick(k):
        @pl.when(k + 4 < wide_experts)
        def _():
            gather.start(0, k + 4)

        @pl.when((k + 2 >= 0) & (k + 2 < wide_experts))
        def _():
            gather.arrive(0, k + 2)
            gather.start(1, k + 2)

        @pl.when((k + 1 >= 0) & (k + 1 < wide_experts))
        def _():
            gather.arrive(1, k + 1)
            gather.start(2, k + 1)

    grad_mod[...] = jnp.zeros_like(grad_mod)
    gather.start(0, 0)
    gather.start(0, 1)
    for stage in range(2):
        for small in (ada_gather, attn_gather):
            small.arrive(stage, 0)
            small.start(stage + 1, 0)
    gather.start(0, 2)
    gather.arrive(0, 0)
    gather.start(1, 0)
    ada_gather.arrive(2, 0)

    low_cut = pl.ds(0, cut)
    blocks_to_weights(place, rows, ada_buf.at[0], mp, (up_w.at[:, low_cut], down_w.at[:, low_cut]))
    mod[mp, :, pl.ds(0, cut)] = mxu(cond_low[...], up_w[:, low_cut])
    mod[mp, :, pl.ds(cut, cut)] = mxu(cond_low[...], down_w[:, low_cut])
    mod_cross = remote(mod.at[mp], mod.at[mp], core_send.at[1], core_recv.at[1], other)
    mod_cross.start()
    attn_gather.arrive(2, 0)
    attn_cross = remote(attn_buf.at[0], attn_far, core_send.at[0], core_recv.at[0], other)
    attn_cross.start()
    blocks_to_weights(place, rows, attn_buf.at[0], mp, [attn_w.at[mp, j] for j in range(parts)])
    for load in loads:
        load.wait()
    ada_gather.sent(0)
    attn_gather.sent(0)
    sc_gather.arrive(0, 0)
    sc_gather.start(1, 0)
    attn_cross.wait()
    blocks_to_weights(place, rows, attn_far, 1 - mp, [attn_w.at[1 - mp, j] for j in range(parts)])
    mod_cross.wait()
    gate_lanes = pl.ds(first, LANES)
    half_lanes = pl.ds(0, half)

    def weight(core, j):
        return attn_w[core, j, :, half_lanes]

    lane_pair = lax.broadcasted_iota(jnp.int32, (PATCH, 2 * HD), 1)
    masks = [(lane_pair < HD).astype(f32).astype(bf16), (lane_pair >= HD).astype(f32).astype(bf16)]
    groups = [(at, min(2, heads - at)) for at in range(0, heads, 2)]
    expert_lane = lax.broadcasted_iota(jnp.int32, (PATCH, LANES), 1) - (half - first)

    def mod_row(image, vector):
        flat = vector % 3 * width
        return mod[vector // 3, pl.ds(mp * images + image, 1), pl.ds(flat, width)]

    def add_grad_mod(image, vector, value):
        grad_mod[vector // 3, pl.ds(mp * images + image, 1), pl.ds(vector % 3 * width, width)] = value

    def one_head(value, group, head):
        return value if group[1] == 1 else value * masks[head]

    def route(h, image):
        valid = (expert_lane >= 0) & (expert_lane < experts)
        logits = jnp.where(valid, mxu(h, attn_w[0, 0, :, gate_lanes]), -jnp.inf)
        power = jnp.exp(logits - jnp.max(logits, axis=1, keepdims=True))
        router = power / jnp.sum(power, axis=1, keepdims=True)
        picks = route_ref[:, pl.ds(pl.multiple_of(own_at + image * PATCH, PATCH), PATCH)]
        spot = lax.broadcasted_iota(jnp.int32, (LANES, PATCH), 0) - (half - first)
        picked = jnp.where((picks[0:1, :] == spot) | (picks[1:2, :] == spot), 1.0, 0.0)
        return router, picked.T

    def attend(at):
        return mxu(mixed[0, at, :], weight(0, 3), NT) + mxu(mixed[1, at, :], weight(1, 3), NT)

    def token_copies(image):
        at = pl.ds(pl.multiple_of(own_at + image * PATCH, PATCH), PATCH)
        return [
            remote(ref.at[at], ref.at[at], token_send.at[image, i], token_recv.at[image, i], other)
            for i, ref in enumerate((h_all, d_all, gate_all))
        ]

    def forward(image, carry):
        at = pl.ds(pl.multiple_of(image * PATCH, PATCH), PATCH)
        cot_at = pl.ds(pl.multiple_of(own_tok + image * PATCH, PATCH), PATCH)
        all_at = pl.ds(pl.multiple_of(own_at + image * PATCH, PATCH), PATCH)
        normed, _ = layer_norm(branch_acc[at, :])
        h = (normed * (1.0 + mod_row(image, 1)) + mod_row(image, 0)).astype(bf16)
        h_one[at, :] = h
        for core in range(2):
            for j in range(3):
                triple[core, j, at, :] = mxu(h, weight(core, j)).astype(bf16)
            for group in groups:
                lanes = pl.ds(group[0] * HD, group[1] * HD)
                query, key, value = (triple[core, j, at, lanes] for j in range(3))
                total = 0.0
                for head in range(group[1]):
                    scores = mxu(one_head(query, group, head), key, NT) * scale
                    power = jnp.exp(scores - jnp.max(scores, axis=1, keepdims=True))
                    low = (power * (1.0 / jnp.sum(power, axis=1, keepdims=True))).astype(bf16)
                    soft[image, core * heads + group[0] + head] = low
                    total = total + mxu(low, one_head(value, group, head))
                mixed[core, at, lanes] = total.astype(bf16)
        x_one = branch_acc[at, :] + mod_row(image, 2) * attend(at)
        normed, _ = layer_norm(x_one)
        h = (normed * (1.0 + mod_row(image, 4)) + mod_row(image, 3)).astype(bf16)
        h_all[all_at, :] = h
        router, chosen = route(h, image)
        shared = (expert_lane >= experts) & (expert_lane < wide_experts)
        gate_all[all_at, :] = jnp.where(shared, 1.0, router * chosen)
        d_all[all_at, :] = (branch_acc[cot_at, :] * mod_row(image, 5)).astype(bf16)
        for copy in token_copies(image):
            copy.start()

        @pl.when(image % 2 == 1)
        def _():
            tick(image // 2 - 1)

        @pl.when(image == 0)
        def _():
            sc_gather.arrive(1, 0)
            sc_gather.start(2, 0)

        return carry

    lax.fori_loop(0, images, forward, 0)
    ahead = images // 2 - 1
    sc_gather.arrive(2, 0)
    sc_gather.sent(0)

    branch_acc[...] = jnp.zeros_like(branch_acc)
    grad_h_acc[...] = jnp.zeros_like(grad_h_acc)
    grad_gate_acc[...] = jnp.zeros_like(grad_gate_acc)

    def all_tokens(image, carry):
        for copy in token_copies(image):
            copy.wait()
        return carry

    lax.fori_loop(0, images, all_tokens, 0)

    def compute(e):
        for buf, lanes, order in streams:
            blocks_to_weights(place, rows, buf.at[e], mp, (up_w.at[:, lanes], down_w.at[:, lanes]), order)
        up_grad[...] = jnp.zeros_like(up_grad)
        down_grad[...] = jnp.zeros_like(down_grad)

        def one_tile(t, carry):
            at = pl.ds(pl.multiple_of(t * tile, tile), tile)
            h = h_all[at, :]
            d = d_all[at, :]
            lane = lax.broadcasted_iota(jnp.int32, (tile, LANES), 1) - (half - first)
            gate = jnp.sum(jnp.where(lane == e, gate_all[at, :], 0.0), axis=1, keepdims=True)
            pre = mxu(h, up_w[...])
            back = mxu(d, down_w[...])
            act, slope = gelu_both(pre)
            inner = jnp.sum(act * back, axis=1, keepdims=True)
            grad_gate_acc[at, :] += jnp.where(lane == e, inner, 0.0)
            act_low = (gate * act).astype(bf16)
            pre_low = (gate * back * slope).astype(bf16)
            branch_acc[at, :] += mxu(act_low, down_w[...], NT)
            grad_h_acc[at, :] += mxu(pre_low, up_w[...], NT)
            up_grad[...] += mxu(h, pre_low, TN)
            down_grad[...] += mxu(d, act_low, TN)
            return carry

        lax.fori_loop(0, h_all.shape[0] // tile, one_tile, 0)

    def put_total(e):
        for part, (_, lanes, _) in zip(scatter.both, streams):
            total_ref[e, :, lanes] = part.last(e)

    def collect(k):
        @pl.when((k >= 1) & (k - 1 < wide_experts))
        def _():
            scatter.arrive(0, k - 1)
            scatter.add(0, k - 1)
            scatter.start(1, k - 1)

        @pl.when((k >= 2) & (k - 2 < wide_experts))
        def _():
            scatter.arrive(1, k - 2)
            scatter.add(1, k - 2)
            scatter.start(2, k - 2)

        @pl.when((k >= 3) & (k - 3 < wide_experts))
        def _():
            scatter.arrive(2, k - 3)
            put_total(k - 3)

    def step(e, carry):
        tick(e + ahead)
        gather.arrive(2, e)
        compute(e)
        gather.sent(e)
        for buf, lanes, order in streams:
            grads_to_blocks(place, rows, (up_grad.at[:, lanes], down_grad.at[:, lanes]), buf.at[e], order)
        scatter.start(0, e)
        collect(e)
        return carry

    lax.fori_loop(0, wide_experts, step, 0)

    h_all[theirs, :] = branch_acc[theirs, :].astype(bf16)
    d_all[theirs, :] = grad_h_acc[theirs, :].astype(bf16)
    shares = [
        remote(h_all.at[theirs], share_in.at[0], core_send.at[2], core_recv.at[2], other),
        remote(d_all.at[theirs], share_in.at[1], core_send.at[3], core_recv.at[3], other),
        remote(grad_gate_acc.at[theirs], gate_in, core_send.at[4], core_recv.at[4], other),
    ]
    loads = [
        pltpu.make_async_copy(tok_ref, branch_acc.at[theirs], load_sem.at[0]),
        pltpu.make_async_copy(cot_ref, grad_h_acc.at[theirs], load_sem.at[1]),
    ]
    for copy in shares + loads:
        copy.start()
    gate_grad[...] = jnp.zeros_like(gate_grad)
    for copy in shares + loads:
        copy.wait()

    def backward(image, carry):
        at = pl.ds(pl.multiple_of(image * PATCH, PATCH), PATCH)
        own_rows = pl.ds(pl.multiple_of(own_at + image * PATCH, PATCH), PATCH)
        load_rows = pl.ds(pl.multiple_of(their_at + image * PATCH, PATCH), PATCH)
        tok, cot = branch_acc[load_rows, :], grad_h_acc[load_rows, :]
        branch = branch_acc[own_rows, :] + share_in[0, at, :].astype(f32)
        attention = attend(at)
        x_one = tok + mod_row(image, 2) * attention
        normed, inverse = layer_norm(x_one)
        branch_acc[own_rows, :] = x_one + mod_row(image, 5) * branch
        add_grad_mod(image, 5, jnp.sum(cot * branch, axis=0, keepdims=True))
        h = h_all[own_rows, :]
        router, chosen = route(h, image)
        grad_router = (grad_gate_acc[own_rows, :] + gate_in[at, :]) * chosen
        grad_logits = (router * (grad_router - jnp.sum(router * grad_router, axis=1, keepdims=True))).astype(bf16)
        gate_grad[...] += mxu(h, grad_logits, TN)
        grad_h = grad_h_acc[own_rows, :] + share_in[1, at, :].astype(f32) + mxu(grad_logits, attn_w[0, 0, :, gate_lanes], NT)
        add_grad_mod(image, 3, jnp.sum(grad_h, axis=0, keepdims=True))
        add_grad_mod(image, 4, jnp.sum(grad_h * normed, axis=0, keepdims=True))
        grad_x = cot + norm_back(grad_h * (1.0 + mod_row(image, 4)), normed, inverse)
        add_grad_mod(image, 2, jnp.sum(grad_x * attention, axis=0, keepdims=True))
        grad_att = (grad_x * mod_row(image, 2)).astype(bf16)
        d_all[own_rows, :] = grad_att
        grad_h_one = 0.0
        for core in range(2):
            grad_mixed = mxu(grad_att, weight(core, 3)).astype(bf16)
            for group in groups:
                lanes = pl.ds(group[0] * HD, group[1] * HD)
                query, key, value = (triple[core, j, at, lanes] for j in range(3))
                back = grad_mixed[:, group[0] * HD : (group[0] + group[1]) * HD]
                grads = [0.0, 0.0, 0.0]
                for head in range(group[1]):
                    low = soft[image, core * heads + group[0] + head]
                    prob = low.astype(f32)
                    head_back = one_head(back, group, head)
                    grad_soft = mxu(head_back, value, NT)
                    delta = jnp.sum(prob * grad_soft, axis=1, keepdims=True)
                    grad_scores = (prob * (grad_soft - delta) * scale).astype(bf16)
                    grads[0] = grads[0] + mxu(grad_scores, one_head(key, group, head))
                    grads[1] = grads[1] + mxu(grad_scores, one_head(query, group, head), TN)
                    grads[2] = grads[2] + mxu(low, head_back, TN)
                for j in range(3):
                    triple[core, j, at, lanes] = grads[j].astype(bf16)
            for j in range(3):
                grad_h_one = grad_h_one + mxu(triple[core, j, at, :], weight(core, j), NT)
        normed, inverse = layer_norm(tok)
        add_grad_mod(image, 0, jnp.sum(grad_h_one, axis=0, keepdims=True))
        add_grad_mod(image, 1, jnp.sum(grad_h_one * normed, axis=0, keepdims=True))
        grad_h_acc[own_rows, :] = grad_x + norm_back(grad_h_one * (1.0 + mod_row(image, 1)), normed, inverse)
        collect(wide_experts + image)
        return carry

    lax.fori_loop(0, images, backward, 0)
    for k in range(images, 3):
        collect(wide_experts + k)
    stores = [
        pltpu.make_async_copy(branch_acc.at[own], output_ref, load_sem.at[2]),
        pltpu.make_async_copy(grad_h_acc.at[own], grad_tok_ref, load_sem.at[3]),
    ]
    for copy in stores:
        copy.start()

    crosses = [
        remote(grad_mod.at[1 - mp], grad_mod_in, core_send.at[5], core_recv.at[5], other),
        remote(attn_share, attn_in, core_send.at[6], core_recv.at[6], other),
        remote(mod_buf.at[0], mod_far, core_send.at[7], core_recv.at[7], other),
    ]
    crosses[0].start()

    def attn_grad(core, j):
        if j == parts - 1:
            return mxu(d_all[own, :], mixed[core], TN)
        return mxu(h_one[...], triple[core, j], TN)

    spare = pl.ds(half, 2 * LANES - half)
    for j in range(parts):
        attn_share[j, :, half_lanes] = attn_grad(1 - mp, j).astype(bf16)
        if j > 0:
            attn_share[j, :, spare] = jnp.zeros((width, 2 * LANES - half), bf16)
    attn_share[0, :, spare] = gate_grad[:, pl.ds(half - first, 2 * LANES - half)].astype(bf16)
    crosses[1].start()
    crosses[0].wait()
    grad_low = grad_mod[mp] + grad_mod_in[...]
    mod_buf[0, place.slot()] = jnp.concatenate([grad_low[:, :cut], grad_low[:, cut:]], axis=0).astype(bf16)
    mod_gather = Gather(place, mod_buf, mod_send, mod_recv)
    mod_gather.start(0, 0)
    crosses[1].wait()
    places = [(up_grad, 0), (up_grad, 1), (up_grad, 2), (down_grad, 0)]
    for j in range(parts):
        ref, at = places[j]
        ref[:, pl.ds(at * 2 * LANES, half)] = attn_grad(mp, j) + attn_in[j, :, half_lanes].astype(f32)
        if j > 0:
            ref[:, pl.ds(at * 2 * LANES + half, 2 * LANES - half)] = jnp.zeros((width, 2 * LANES - half), f32)
    up_grad[:, spare] = gate_grad[:, pl.ds(half - first, 2 * LANES - half)] + attn_in[0, :, spare].astype(f32)
    grads = [ref[:, pl.ds(at * 2 * LANES, 2 * LANES)] for ref, at in places]
    grads_to_blocks(place, rows, grads, attn_buf.at[0])
    attn_scatter = Scatter(place, attn_buf, attn_box, attn_back_send, attn_back_recv)
    attn_scatter.start(0, 0)
    for stage in range(2):
        mod_gather.arrive(stage, 0)
        mod_gather.start(stage + 1, 0)
        attn_scatter.arrive(stage, 0)
        attn_scatter.add(stage, 0)
        attn_scatter.start(stage + 1, 0)
    square = jnp.zeros((1, 1), f32)
    for e in range(wide_experts):
        square = square + jnp.sum(total_ref[e] * total_ref[e])
    mod_gather.arrive(2, 0)
    crosses[2].start()
    row = lax.broadcasted_iota(jnp.int32, (width, LANES), 0)
    lane = lax.broadcasted_iota(jnp.int32, (width, LANES), 1)
    pick = ((row == place.dp * rows + lane) & (lane < rows)).astype(f32).astype(bf16)
    group = cond_ref.shape[0]

    def in_order(ref, core, at):
        pieces = [ref[place.slot_of(dp, core)].astype(f32)[at : at + group] for dp in range(count)]
        return jnp.concatenate(pieces, axis=0).astype(bf16)

    conds = mxu(in_order(sc_buf.at[0], mp, 0), pick).astype(bf16)

    def ada_grad(ref, core):
        low = mxu(conds, in_order(ref, core, 0), TN)[:rows]
        high = mxu(conds, in_order(ref, core, group), TN)[:rows, : wide - cut]
        start = pl.multiple_of(core * wide, LANES)
        ada_out[:, pl.ds(start, cut)] = low
        ada_out[:, pl.ds(pl.multiple_of(start + cut, LANES), wide - cut)] = high
        return jnp.sum(low * low) + jnp.sum(high * high)

    small = ada_grad(mod_buf.at[0], mp)
    mod_gather.sent(0)
    crosses[2].wait()
    small = small + ada_grad(mod_far, 1 - mp)
    attn_scatter.arrive(2, 0)
    attn = attn_scatter.last(0)
    attn_out[...] = attn
    lane = lax.broadcasted_iota(jnp.int32, attn.shape, 1)
    square = square + 0.5 * small + jnp.sum(jnp.where(lane < half, 1.0, 0.5) * attn * attn)
    value = jnp.broadcast_to(square, norm_out.shape)
    norm_out[...] = all_sum(place, value, norm_src, norm_box, norm_send, norm_recv)
    for copy in stores:
        copy.wait()


def block_call(tokens, condition, cotangent, routes, w_ada, w_gate, w_attn, w_expert):
    count = lax.axis_size("dp")
    own_tok, width = tokens.shape
    rows, wide = w_ada.shape
    experts = w_gate.shape[0]
    parts, _, half = w_attn.shape
    _, wide_experts, _, hidden = w_expert.shape
    depth, side = dp_sizes(count)
    images = own_tok // PATCH
    cut = (wide // 4 + LANES - 1) // LANES * LANES
    spare = 2 * LANES
    block, ada_block, attn_block = block_rows(rows, 2), block_rows(rows, 2), block_rows(rows, parts)
    tok = 2 * own_tok
    tile = TILE if count <= 16 else TILE // 2
    vmem = pl.BlockSpec(memory_space=pltpu.VMEM)
    hbm = pl.BlockSpec(memory_space=pl.ANY)
    hops = depth + 2 * side - 3

    def sems(*shape):
        return pltpu.SemaphoreType.DMA(shape)

    def box(slots, height, lanes):
        return pltpu.VMEM((slots, count - 1, height, lanes), bf16)

    one = hidden * CUT_ONE // CUT_ALL // LANES * LANES
    two = hidden - one

    return pl.pallas_call(
        functools.partial(block_kernel, count, rows, experts, tile),
        out_shape=(
            jax.ShapeDtypeStruct((own_tok, width), f32),
            jax.ShapeDtypeStruct((own_tok, width), f32),
            jax.ShapeDtypeStruct((rows, wide), f32),
            jax.ShapeDtypeStruct((attn_block, spare), f32),
            jax.ShapeDtypeStruct((wide_experts, block, hidden), f32),
            jax.ShapeDtypeStruct((8, LANES), f32),
        ),
        in_specs=[hbm, hbm] + [vmem] * 6,
        out_specs=(hbm, hbm) + (vmem,) * 4,
        scratch_shapes=[
            pltpu.VMEM((wide_experts, count, block, one), bf16),
            pltpu.VMEM((wide_experts, count, block, two), bf16),
            box(SLOTS, block, one),
            box(SLOTS, block, two),
            pltpu.VMEM((1, count, ada_block, cut), bf16),
            pltpu.VMEM((1, count, SUB, width), bf16),
            pltpu.VMEM((1, count, SUB, cut), bf16),
            pltpu.VMEM((count, SUB, cut), bf16),
            pltpu.VMEM((1, count, attn_block, spare), bf16),
            box(1, attn_block, spare),
            pltpu.VMEM((count, attn_block, spare), bf16),
            pltpu.VMEM((2, parts, width, spare), bf16),
            pltpu.VMEM(condition.shape, bf16),
            pltpu.VMEM((2, condition.shape[0], 2 * cut), f32),
            pltpu.VMEM((2, condition.shape[0], 2 * cut), f32),
            pltpu.VMEM((condition.shape[0], 2 * cut), f32),
            pltpu.VMEM((2, 3, own_tok, half), bf16),
            pltpu.VMEM((2, own_tok, half), bf16),
            pltpu.VMEM((own_tok, width), bf16),
            pltpu.VMEM((images, width // HD, PATCH, PATCH), bf16),
            pltpu.VMEM((tok, width), bf16),
            pltpu.VMEM((tok, width), bf16),
            pltpu.VMEM((tok, LANES), f32),
            pltpu.VMEM((tok, width), f32),
            pltpu.VMEM((tok, width), f32),
            pltpu.VMEM((tok, LANES), f32),
            pltpu.VMEM((own_tok, LANES), f32),
            pltpu.VMEM((2, own_tok, width), bf16),
            pltpu.VMEM((width, hidden), bf16),
            pltpu.VMEM((width, hidden), bf16),
            pltpu.VMEM((width, hidden), f32),
            pltpu.VMEM((width, hidden), f32),
            pltpu.VMEM((width, LANES), f32),
            pltpu.VMEM((parts, width, spare), bf16),
            pltpu.VMEM((parts, width, spare), bf16),
            pltpu.VMEM((2, 8, LANES), f32),
            pltpu.VMEM((depth + 2 * side * side, 8, LANES), f32),
            sems(4),
            *[sems(wide_experts, hops)] * 8,
            *[sems(1, hops)] * 10,
            sems(8),
            sems(8),
            sems(images, 3),
            sems(images, 3),
            sems(depth + 2 * side * side),
            sems(depth + 2 * side * side),
        ],
        compiler_params=pltpu.CompilerParams(collective_id=1, has_side_effects=True, vmem_limit_bytes=VMEM_BYTES),
        cost_estimate=pl.CostEstimate(
            flops=12 * tok * width * hidden * wide_experts, bytes_accessed=16 * w_expert.size, transcendentals=0
        ),
        name="block",
    )(tokens, cotangent, condition, routes, w_ada, w_gate, w_attn, w_expert)
def update_kernel(rows, half, output_ref, grad_tok_ref, norm_ref, expert_ref, attn_ref, ada_ref, *refs):
    ada, gate, attn, expert = (refs[3 * i : 3 * i + 3] for i in range(4))
    outs, hold, sem = refs[12:-2], refs[-2], refs[-1]
    ada_new, gate_new, attn_new, expert_new = (outs[3 * i : 3 * i + 3] for i in range(4))
    loads = [pltpu.make_async_copy(ref, hold.at[i], sem.at[i]) for i, ref in enumerate((output_ref, grad_tok_ref))]
    stores = [pltpu.make_async_copy(hold.at[i], outs[13 + i], sem.at[2 + i]) for i in range(2)]
    for copy in loads:
        copy.start()
    total = jnp.sqrt(norm_ref[...])
    outs[12][0, 0] = jnp.max(total)
    factor = jnp.minimum(1.0, CLIP_NORM / (total[0:1, 0:1] + 1e-06))

    def write(ins, news, at, grad):
        for new, value in zip(news, adam(ins[0][at], ins[1][at], ins[2][at], grad * factor)):
            new[at] = value

    everything = (slice(None), slice(None))
    write(ada, ada_new, everything, ada_ref[...])
    for load, store in zip(loads, stores):
        load.wait()
        store.start()
    first = half // LANES * LANES
    small = attn_ref[pl.ds(0, rows), pl.ds(first, LANES)]
    square = jnp.concatenate([small, jnp.zeros((LANES - rows, LANES), f32)], axis=0).T
    experts = gate[0].shape[0]
    write(gate, gate_new, everything, square[half - first : half - first + experts, :rows])
    for j in range(attn[0].shape[0]):
        write(attn, attn_new, (j,), attn_ref[pl.ds(j * rows, rows), pl.ds(0, half)])

    def one(e, carry):
        for part in range(2):
            write(expert, expert_new, (part, e), expert_ref[e, pl.ds(part * rows, rows), :])
        return carry

    lax.fori_loop(0, expert[0].shape[1], one, 0)
    for copy in stores:
        copy.wait()


def update_call(rows, half, output, grad_tokens, norm, expert, attn, ada, weights):
    vmem = pl.BlockSpec(memory_space=pltpu.VMEM)
    hbm = pl.BlockSpec(memory_space=pl.ANY)
    shapes = [jax.ShapeDtypeStruct(w.shape, f32) for w in weights]
    return pl.pallas_call(
        functools.partial(update_kernel, rows, half),
        out_shape=shapes
        + [jax.ShapeDtypeStruct((1, 1), f32)]
        + [jax.ShapeDtypeStruct(output.shape, f32), jax.ShapeDtypeStruct(grad_tokens.shape, f32)],
        in_specs=[hbm, hbm] + [vmem] * (4 + len(weights)),
        out_specs=[vmem] * len(weights) + [pl.BlockSpec(memory_space=pltpu.SMEM), hbm, hbm],
        scratch_shapes=[pltpu.VMEM((2, *output.shape), f32), pltpu.SemaphoreType.DMA((4,))],
        compiler_params=pltpu.CompilerParams(vmem_limit_bytes=VMEM_BYTES),
        name="update",
    )(output, grad_tokens, norm, expert, attn, ada, *weights)


def per_device(
    tokens,
    condition,
    cotangent,
    routes,
    w_ada,
    ada_first,
    ada_second,
    w_gate,
    gate_first,
    gate_second,
    w_attn,
    attn_first,
    attn_second,
    w_expert,
    expert_first,
    expert_second,
):
    output, grad_tokens, ada_total, attn_total, expert_total, square_sum = block_call(
        tokens, condition, cotangent, routes.T, w_ada, w_gate.T, w_attn, w_expert
    )
    updated = update_call(
        w_ada.shape[0], w_attn.shape[2], output, grad_tokens, square_sum, expert_total, attn_total, ada_total,
        (
            w_ada, ada_first, ada_second,
            w_gate.T, gate_first.T, gate_second.T,
            w_attn, attn_first, attn_second,
            w_expert, expert_first, expert_second,
        ),
    )
    gates = [gate.T for gate in updated[3:6]]
    return (*updated[13:], updated[12].reshape(()), *updated[:3], *gates, *updated[6:12])


def solution(mesh):
    placed = (
        P(("dp", "mp"), None),
        P("dp", None),
        P(("dp", "mp"), None),
        P("dp", None),
        P("dp", None),
        P("dp", None),
        P("dp", None),
        P("dp", None),
        P("dp", None),
        P("dp", None),
        P(None, "dp", "mp"),
        P(None, "dp", "mp"),
        P(None, "dp", "mp"),
        P(None, None, "dp", "mp"),
        P(None, None, "dp", "mp"),
        P(None, None, "dp", "mp"),
    )
    return jax.shard_map(
        per_device,
        mesh=mesh,
        in_specs=placed,
        out_specs=(
            P(("dp", "mp"), None),
            P(("dp", "mp"), None),
            P(),
            P("dp", None),
            P("dp", None),
            P("dp", None),
            P("dp", None),
            P("dp", None),
            P("dp", None),
            P(None, "dp", "mp"),
            P(None, "dp", "mp"),
            P(None, "dp", "mp"),
            P(None, None, "dp", "mp"),
            P(None, None, "dp", "mp"),
            P(None, None, "dp", "mp"),
        ),
        check_vma=False,
    )
```

time: 321 us -> 297 us (0.925)
  local copies, waits for them, and re-layouts: 10.9 us -> 0 us
  other arithmetic: 10.8 us -> 0 us
    unnamed x27 -> x0, local copies, waits for them, and re-layouts: 9.75 us -> none
    sub x4 -> x0, other arithmetic: 9.19 us -> none  [adam(): return (master - RATE * update, first_new, second_new)]
    pallas_call x0 -> x1, Pallas kernels: none -> 9.01 us  [update_call(): pl.pallas_call(functools.partial(update_kernel, rows, half), out_shape=sh...]
    pallas_call x1, Pallas kernels: 294 us -> 287 us  [block_call(): pl.pallas_call(functools.partial(block_kernel, count, rows, experts, tile...]
where the time goes in v3:
time: 297 us
  Pallas kernels  296 us (100%)
    pallas_call x1, Pallas kernels, block_call(): pl.pallas_call(functools.partial(block_kernel, count, rows, experts, tile...  287 us
    pallas_call x1, Pallas kernels, update_call(): pl.pallas_call(functools.partial(update_kernel, rows, half), out_shape=sh...  9.01 us

profile of v3, /device:TPU:0, one launch (start us, length us, event | category | flops | bytes accessed | tf_op | source)
XLA Modules:
  0.0 296.6 jit_solution(14411754155837556007)
XLA Ops:
  0.6 286.7 %block.1 = (f32[1024,384]{1,0:T(8,128)}, f32[1024,384]{1,0:T(8,128)}, f32[24,2304]{1,0:T(8,128)}, f32[96,256]{1,0:T(8,128)}, f32[10,48,768]{2,1,0:T(8,128)}, /*index=5*/f32[8,128]{1,0:T(8,128)}) custom-call(f32[1024,384]{1,0:T(8,128)} %tok_ref.1, f32[1024,384]{1,0:T(8,128)} %cot_ref.1, f32[8,384]{1,0:T(8,128)} %cond_ref.1, s32[2,2048]{1,0:T(2,128)} %bitcast.12, ...), custom_call_target="tpu_custom_call" | custom-call | flops 72477573120 | bytes 5898240 | tf_op jit(solution)/shard_map/block/pallas_call | solution.py:792
  287.4 9.0 %update.1 = (f32[24,2304]{1,0:T(8,128)}, f32[24,2304]{1,0:T(8,128)}, f32[24,2304]{1,0:T(8,128)}, f32[8,24]{1,0:T(8,128)}, f32[8,24]{1,0:T(8,128)}, /*index=5*/f3...) custom-call(f32[1024,384]{1,0:T(8,128)} %get-tuple-element.36.output, ...), custom_call_target="tpu_custom_call" | custom-call | tf_op jit(solution)/shard_map/update/pallas_call | solution.py:901

commit v4 on v3

--- a/solution.py
+++ b/solution.py
@@ -91,6 +91,15 @@
             "b": jnp.where(self.mp == 0, x, y),
         }
         self.size = {"z": self.depth, "a": side, "b": side}
+        self.near = {axis: self.peers(axis) for axis in "zab"}
+        self.first, self.others = {}, {}
+        for order in (ZBA, BZA):
+            for stage, axis in enumerate(order):
+                fixed = {name: self.at[name] for name in order[stage:]}
+                self.first[order, stage] = self.slot_at(order, fixed)
+                self.others[order, stage] = [
+                    self.slot_at(order, {**fixed, axis: self.along(axis, k)}) for k in range(1, self.size[axis])
+                ]
 
     def slot_at(self, order, at):
         slot = 0
@@ -99,7 +108,7 @@
         return slot
 
     def slot(self, order=ZBA):
-        return self.slot_at(order, self.at)
+        return self.first[order, 0]
 
     def slot_of(self, dp, core, order=ZBA):
         side = self.side
@@ -156,12 +165,11 @@
 
     def copies(self, stage, e):
         p, order = self.p, self.order
-        fixed = {axis: p.at[axis] for axis in order[stage:]}
-        src = self.buf.at[e, pl.ds(p.slot_at(order, fixed), span(p, order, stage))]
+        src = self.buf.at[e, pl.ds(p.first[order, stage], span(p, order, stage))]
         base = sum(p.size[axis] - 1 for axis in order[:stage])
         return [
             remote(src, src, self.send.at[e, base + k], self.recv.at[e, base + k], peer)
-            for k, peer in enumerate(p.peers(order[stage]))
+            for k, peer in enumerate(p.near[order[stage]])
         ]
 
     def start(self, stage, e):
@@ -179,26 +187,24 @@
 
 
 class Scatter:
-    def __init__(self, place, buf, box, send, recv, order=ZBA):
-        self.p, self.buf, self.box, self.send, self.recv, self.order = place, buf, box, send, recv, order
-
-    def parts(self, stage):
-        p, order = self.p, self.order
-        base = 0
-        for before in range(3 - 1, 2 - stage, -1):
-            base += (p.size[order[before]] - 1) * span(p, order, before)
-        return order[2 - stage], span(p, order, 2 - stage), base
+    def __init__(self, place, buf, boxes, send, recv, order=ZBA):
+        self.p, self.buf, self.boxes, self.send, self.recv, self.order = place, buf, boxes, send, recv, order
+
+    def box(self, stage, e, block, many):
+        box = self.boxes[min(stage, 1)]
+        if stage == 2:
+            order = self.order
+            block = block + (self.p.size[order[1]] - 1) * span(self.p, order, 1)
+        return box.at[e % box.shape[0], pl.ds(block, many)]
 
     def copies(self, stage, e):
         p, order = self.p, self.order
-        axis, many, base = self.parts(stage)
+        axis, many = order[2 - stage], span(p, order, 2 - stage)
         sem = sum(p.size[order[2 - before]] - 1 for before in range(stage))
         made = []
-        for k, peer in enumerate(p.peers(axis)):
-            fixed = {name: p.at[name] for name in order[2 - stage :]}
-            fixed[axis] = p.along(axis, k + 1)
-            src = self.buf.at[e, pl.ds(p.slot_at(order, fixed), many)]
-            dst = self.box.at[e % SLOTS, pl.ds(base + k * many, many)]
+        for k, peer in enumerate(p.near[axis]):
+            src = self.buf.at[e, pl.ds(p.others[order, 2 - stage][k], many)]
+            dst = self.box(stage, e, k * many, many)
             made.append(remote(src, dst, self.send.at[e, sem + k], self.recv.at[e, sem + k], peer))
         return made
 
@@ -210,27 +216,23 @@
         for copy in self.copies(stage, e):
             copy.wait()
 
+    def total(self, stage, e, i):
+        p, order = self.p, self.order
+        many = span(p, order, 2 - stage)
+        total = self.buf[e, p.first[order, 2 - stage] + i].astype(f32)
+        for k in range(p.size[order[2 - stage]] - 1):
+            total = total + self.box(stage, e, k * many + i, 1)[0].astype(f32)
+        return total
+
     def add(self, stage, e):
-        p, order = self.p, self.order
-        axis, many, base = self.parts(stage)
-        first = p.slot_at(order, {name: p.at[name] for name in order[2 - stage :]})
-
         def one(i, carry):
-            total = self.buf[e, first + i].astype(f32)
-            for k in range(p.size[axis] - 1):
-                total = total + self.box[e % SLOTS, base + k * many + i].astype(f32)
-            self.buf[e, first + i] = total.astype(bf16)
+            self.buf[e, self.p.first[self.order, 2 - stage] + i] = self.total(stage, e, i).astype(bf16)
             return carry
 
-        lax.fori_loop(0, many, one, 0)
+        lax.fori_loop(0, span(self.p, self.order, 2 - stage), one, 0)
 
     def last(self, e):
-        p, order = self.p, self.order
-        axis, many, base = self.parts(2)
-        total = self.buf[e, p.slot(order)].astype(f32)
-        for k in range(p.size[axis] - 1):
-            total = total + self.box[e % SLOTS, base + k].astype(f32)
-        return total
+        return self.total(2, e, 0)
 
 
 def block_rows(rows, parts):
@@ -262,7 +264,7 @@
     src[0] = value
     box[z] = value
     copies = [
-        remote(src.at[0], box.at[z], send.at[k], recv.at[k], peer) for k, peer in enumerate(place.peers("z"))
+        remote(src.at[0], box.at[z], send.at[k], recv.at[k], peer) for k, peer in enumerate(place.near["z"])
     ]
     for copy in copies:
         copy.start()
@@ -312,11 +314,11 @@
 
 
 def block_kernel(
-    count, rows, experts, tile,
+    count, rows, experts, tile, lag,
     tok_ref, cot_ref, cond_ref, route_ref, ada_ref, gate_ref, attn_ref, w_ref,
     output_ref, grad_tok_ref, ada_out, attn_out, total_ref, norm_out,
-    buf_one, buf_two, box_one, box_two,
-    ada_buf, sc_buf, mod_buf, mod_far, attn_buf, attn_box, attn_far, attn_w,
+    buf_one, buf_two, box_one, rest_one, box_two, rest_two,
+    ada_buf, sc_buf, mod_buf, mod_far, attn_buf, attn_box, attn_rest, attn_far, attn_w,
     cond_low, mod, grad_mod, grad_mod_in, triple, mixed, h_one, soft,
     h_all, d_all, gate_all, branch_acc, grad_h_acc, grad_gate_acc, gate_in, share_in,
     up_w, down_w, up_grad, down_grad, gate_grad, attn_share, attn_in, norm_src, norm_box,
@@ -363,7 +365,9 @@
     gate = mxu(gate_ref[...].astype(bf16), side_by.astype(f32).astype(bf16), TN)[:, : 2 * LANES - half]
     spare = [gate] + [jnp.zeros_like(gate)] * (parts - 1)
     both = [jnp.concatenate([attn_ref[j], spare[j]], axis=1) for j in range(parts)]
-    put(attn_buf.at[0], jnp.concatenate(both, axis=0).astype(bf16))
+    pair = parts // 2
+    for i in range(2):
+        put(attn_buf.at[i], jnp.concatenate(both[i * pair : (i + 1) * pair], axis=0).astype(bf16))
     cond = cond_ref[...]
     cond = cond / (1.0 + jnp.exp(-cond))
     cond_low[...] = cond.astype(bf16)
@@ -378,12 +382,13 @@
         Gather(place, buf_two, gather_send_two, gather_recv_two, BZA),
     )
     scatter = Both(
-        Scatter(place, buf_one, box_one, scatter_send, scatter_recv, ZBA),
-        Scatter(place, buf_two, box_two, scatter_send_two, scatter_recv_two, BZA),
+        Scatter(place, buf_one, (box_one, rest_one), scatter_send, scatter_recv, ZBA),
+        Scatter(place, buf_two, (box_two, rest_two), scatter_send_two, scatter_recv_two, BZA),
     )
     sc_gather = Gather(place, sc_buf, sc_send, sc_recv)
     ada_gather.start(0, 0)
     attn_gather.start(0, 0)
+    attn_gather.start(0, 1)
     sc_gather.start(0, 0)
 
     def fill(e, carry):
@@ -395,16 +400,16 @@
     lax.fori_loop(0, wide_experts, fill, 0)
 
     def tick(k):
-        @pl.when(k + 4 < wide_experts)
+        @pl.when(k + 5 < wide_experts)
         def _():
-            gather.start(0, k + 4)
-
-        @pl.when((k + 2 >= 0) & (k + 2 < wide_experts))
+            gather.start(0, k + 5)
+
+        @pl.when(k + 3 < wide_experts)
         def _():
-            gather.arrive(0, k + 2)
-            gather.start(1, k + 2)
-
-        @pl.when((k + 1 >= 0) & (k + 1 < wide_experts))
+            gather.arrive(0, k + 3)
+            gather.start(1, k + 3)
+
+        @pl.when(k + 1 < wide_experts)
         def _():
             gather.arrive(1, k + 1)
             gather.start(2, k + 1)
@@ -413,10 +418,11 @@
     gather.start(0, 0)
     gather.start(0, 1)
     for stage in range(2):
-        for small in (ada_gather, attn_gather):
-            small.arrive(stage, 0)
-            small.start(stage + 1, 0)
+        for small, i in ((ada_gather, 0), (attn_gather, 0), (attn_gather, 1)):
+            small.arrive(stage, i)
+            small.start(stage + 1, i)
     gather.start(0, 2)
+    gather.start(0, 3)
     gather.arrive(0, 0)
     gather.start(1, 0)
     ada_gather.arrive(2, 0)
@@ -427,19 +433,29 @@
     mod[mp, :, pl.ds(cut, cut)] = mxu(cond_low[...], down_w[:, low_cut])
     mod_cross = remote(mod.at[mp], mod.at[mp], core_send.at[1], core_recv.at[1], other)
     mod_cross.start()
-    attn_gather.arrive(2, 0)
-    attn_cross = remote(attn_buf.at[0], attn_far, core_send.at[0], core_recv.at[0], other)
-    attn_cross.start()
-    blocks_to_weights(place, rows, attn_buf.at[0], mp, [attn_w.at[mp, j] for j in range(parts)])
+    attn_cross = []
+    for i in range(2):
+        attn_gather.arrive(2, i)
+        attn_cross.append(
+            remote(attn_buf.at[i], attn_far.at[i], core_send.at[8 + i], core_recv.at[8 + i], other)
+        )
+        attn_cross[i].start()
+        outs = [attn_w.at[mp, j] for j in range(i * pair, (i + 1) * pair)]
+        blocks_to_weights(place, rows, attn_buf.at[i], mp, outs)
     for load in loads:
         load.wait()
     ada_gather.sent(0)
     attn_gather.sent(0)
+    attn_gather.sent(1)
     sc_gather.arrive(0, 0)
     sc_gather.start(1, 0)
-    attn_cross.wait()
-    blocks_to_weights(place, rows, attn_far, 1 - mp, [attn_w.at[1 - mp, j] for j in range(parts)])
+    for i in range(2):
+        attn_cross[i].wait()
+        outs = [attn_w.at[1 - mp, j] for j in range(i * pair, (i + 1) * pair)]
+        blocks_to_weights(place, rows, attn_far.at[i], 1 - mp, outs)
     mod_cross.wait()
+    gather.arrive(0, 1)
+    gather.start(1, 1)
     gate_lanes = pl.ds(first, LANES)
     half_lanes = pl.ds(0, half)
 
@@ -513,9 +529,7 @@
         for copy in token_copies(image):
             copy.start()
 
-        @pl.when(image % 2 == 1)
-        def _():
-            tick(image // 2 - 1)
+        tick(image - 1)
 
         @pl.when(image == 0)
         def _():
@@ -525,7 +539,7 @@
         return carry
 
     lax.fori_loop(0, images, forward, 0)
-    ahead = images // 2 - 1
+    ahead = images - 1
     sc_gather.arrive(2, 0)
     sc_gather.sent(0)
 
@@ -539,6 +553,17 @@
         return carry
 
     lax.fori_loop(0, images, all_tokens, 0)
+
+    shares = [
+        remote(h_all.at[theirs], share_in.at[0], core_send.at[2], core_recv.at[2], other),
+        remote(d_all.at[theirs], share_in.at[1], core_send.at[3], core_recv.at[3], other),
+        remote(grad_gate_acc.at[theirs], gate_in, core_send.at[4], core_recv.at[4], other),
+    ]
+    loads = [
+        pltpu.make_async_copy(tok_ref, branch_acc.at[theirs], load_sem.at[0]),
+        pltpu.make_async_copy(cot_ref, grad_h_acc.at[theirs], load_sem.at[1]),
+    ]
+    tiles = h_all.shape[0] // tile
 
     def compute(e):
         for buf, lanes, order in streams:
@@ -547,7 +572,16 @@
         down_grad[...] = jnp.zeros_like(down_grad)
 
         def one_tile(t, carry):
-            at = pl.ds(pl.multiple_of(t * tile, tile), tile)
+            @pl.when((e == wide_experts - 1) & (t == tiles // 2))
+            def _():
+                h_all[theirs, :] = branch_acc[theirs, :].astype(bf16)
+                d_all[theirs, :] = grad_h_acc[theirs, :].astype(bf16)
+                for copy in shares:
+                    copy.start()
+                for copy in loads:
+                    copy.start()
+
+            at = pl.ds(pl.multiple_of((t + (1 - mp) * (tiles // 2)) % tiles * tile, tile), tile)
             h = h_all[at, :]
             d = d_all[at, :]
             lane = lax.broadcasted_iota(jnp.int32, (tile, LANES), 1) - (half - first)
@@ -565,7 +599,7 @@
             down_grad[...] += mxu(d, act_low, TN)
             return carry
 
-        lax.fori_loop(0, h_all.shape[0] // tile, one_tile, 0)
+        lax.fori_loop(0, tiles, one_tile, 0)
 
     def put_total(e):
         for part, (_, lanes, _) in zip(scatter.both, streams):
@@ -597,24 +631,11 @@
         for buf, lanes, order in streams:
             grads_to_blocks(place, rows, (up_grad.at[:, lanes], down_grad.at[:, lanes]), buf.at[e], order)
         scatter.start(0, e)
-        collect(e)
+        collect(e - lag)
         return carry
 
     lax.fori_loop(0, wide_experts, step, 0)
 
-    h_all[theirs, :] = branch_acc[theirs, :].astype(bf16)
-    d_all[theirs, :] = grad_h_acc[theirs, :].astype(bf16)
-    shares = [
-        remote(h_all.at[theirs], share_in.at[0], core_send.at[2], core_recv.at[2], other),
-        remote(d_all.at[theirs], share_in.at[1], core_send.at[3], core_recv.at[3], other),
-        remote(grad_gate_acc.at[theirs], gate_in, core_send.at[4], core_recv.at[4], other),
-    ]
-    loads = [
-        pltpu.make_async_copy(tok_ref, branch_acc.at[theirs], load_sem.at[0]),
-        pltpu.make_async_copy(cot_ref, grad_h_acc.at[theirs], load_sem.at[1]),
-    ]
-    for copy in shares + loads:
-        copy.start()
     gate_grad[...] = jnp.zeros_like(gate_grad)
     for copy in shares + loads:
         copy.wait()
@@ -668,12 +689,12 @@
         add_grad_mod(image, 0, jnp.sum(grad_h_one, axis=0, keepdims=True))
         add_grad_mod(image, 1, jnp.sum(grad_h_one * normed, axis=0, keepdims=True))
         grad_h_acc[own_rows, :] = grad_x + norm_back(grad_h_one * (1.0 + mod_row(image, 1)), normed, inverse)
-        collect(wide_experts + image)
+        collect(wide_experts - lag + image)
         return carry
 
     lax.fori_loop(0, images, backward, 0)
-    for k in range(images, 3):
-        collect(wide_experts + k)
+    for k in range(images, 3 + lag):
+        collect(wide_experts - lag + k)
     stores = [
         pltpu.make_async_copy(branch_acc.at[own], output_ref, load_sem.at[2]),
         pltpu.make_async_copy(grad_h_acc.at[own], grad_tok_ref, load_sem.at[3]),
@@ -683,8 +704,14 @@
 
     crosses = [
         remote(grad_mod.at[1 - mp], grad_mod_in, core_send.at[5], core_recv.at[5], other),
-        remote(attn_share, attn_in, core_send.at[6], core_recv.at[6], other),
-        remote(mod_buf.at[0], mod_far, core_send.at[7], core_recv.at[7], other),
+        *[
+            remote(
+                attn_share.at[pl.ds(i * pair, pair)], attn_in.at[pl.ds(i * pair, pair)],
+                core_send.at[6 + i], core_recv.at[6 + i], other,
+            )
+            for i in range(2)
+        ],
+        remote(mod_buf.at[0], mod_far, core_send.at[0], core_recv.at[0], other),
     ]
     crosses[0].start()
 
@@ -694,40 +721,46 @@
         return mxu(h_one[...], triple[core, j], TN)
 
     spare = pl.ds(half, 2 * LANES - half)
-    for j in range(parts):
-        attn_share[j, :, half_lanes] = attn_grad(1 - mp, j).astype(bf16)
-        if j > 0:
-            attn_share[j, :, spare] = jnp.zeros((width, 2 * LANES - half), bf16)
-    attn_share[0, :, spare] = gate_grad[:, pl.ds(half - first, 2 * LANES - half)].astype(bf16)
-    crosses[1].start()
+    places = [(up_grad, 0), (up_grad, 1), (up_grad, 2), (down_grad, 0)]
+    attn_scatter = Scatter(place, attn_buf, (attn_box, attn_rest), attn_back_send, attn_back_recv)
+    for i in range(2):
+        for j in range(i * pair, (i + 1) * pair):
+            attn_share[j, :, half_lanes] = attn_grad(1 - mp, j).astype(bf16)
+            extra = gate_grad[:, pl.ds(half - first, 2 * LANES - half)].astype(bf16)
+            attn_share[j, :, spare] = extra if j == 0 else jnp.zeros_like(extra)
+        crosses[1 + i].start()
     crosses[0].wait()
     grad_low = grad_mod[mp] + grad_mod_in[...]
     mod_buf[0, place.slot()] = jnp.concatenate([grad_low[:, :cut], grad_low[:, cut:]], axis=0).astype(bf16)
     mod_gather = Gather(place, mod_buf, mod_send, mod_recv)
+    for i in range(2):
+        for j in range(i * pair, (i + 1) * pair):
+            ref, at = places[j]
+            ref[:, pl.ds(at * 2 * LANES, half)] = attn_grad(mp, j)
+        crosses[1 + i].wait()
+        grads = []
+        for j in range(i * pair, (i + 1) * pair):
+            ref, at = places[j]
+            lanes = pl.ds(at * 2 * LANES, half)
+            ref[:, lanes] += attn_in[j, :, half_lanes].astype(f32)
+            extra = gate_grad[:, pl.ds(half - first, 2 * LANES - half)] + attn_in[0, :, spare].astype(f32)
+            ref[:, pl.ds(at * 2 * LANES + half, 2 * LANES - half)] = extra if j == 0 else jnp.zeros_like(extra)
+            grads.append(ref[:, pl.ds(at * 2 * LANES, 2 * LANES)])
+        grads_to_blocks(place, rows, grads, attn_buf.at[i])
+        attn_scatter.start(0, i)
     mod_gather.start(0, 0)
-    crosses[1].wait()
-    places = [(up_grad, 0), (up_grad, 1), (up_grad, 2), (down_grad, 0)]
-    for j in range(parts):
-        ref, at = places[j]
-        ref[:, pl.ds(at * 2 * LANES, half)] = attn_grad(mp, j) + attn_in[j, :, half_lanes].astype(f32)
-        if j > 0:
-            ref[:, pl.ds(at * 2 * LANES + half, 2 * LANES - half)] = jnp.zeros((width, 2 * LANES - half), f32)
-    up_grad[:, spare] = gate_grad[:, pl.ds(half - first, 2 * LANES - half)] + attn_in[0, :, spare].astype(f32)
-    grads = [ref[:, pl.ds(at * 2 * LANES, 2 * LANES)] for ref, at in places]
-    grads_to_blocks(place, rows, grads, attn_buf.at[0])
-    attn_scatter = Scatter(place, attn_buf, attn_box, attn_back_send, attn_back_recv)
-    attn_scatter.start(0, 0)
     for stage in range(2):
+        for i in range(2):
+            attn_scatter.arrive(stage, i)
+            attn_scatter.add(stage, i)
+            attn_scatter.start(stage + 1, i)
         mod_gather.arrive(stage, 0)
         mod_gather.start(stage + 1, 0)
-        attn_scatter.arrive(stage, 0)
-        attn_scatter.add(stage, 0)
-        attn_scatter.start(stage + 1, 0)
     square = jnp.zeros((1, 1), f32)
     for e in range(wide_experts):
         square = square + jnp.sum(total_ref[e] * total_ref[e])
     mod_gather.arrive(2, 0)
-    crosses[2].start()
+    crosses[3].start()
     row = lax.broadcasted_iota(jnp.int32, (width, LANES), 0)
     lane = lax.broadcasted_iota(jnp.int32, (width, LANES), 1)
     pick = ((row == place.dp * rows + lane) & (lane < rows)).astype(f32).astype(bf16)
@@ -749,13 +782,15 @@
 
     small = ada_grad(mod_buf.at[0], mp)
     mod_gather.sent(0)
-    crosses[2].wait()
+    crosses[3].wait()
     small = small + ada_grad(mod_far, 1 - mp)
-    attn_scatter.arrive(2, 0)
-    attn = attn_scatter.last(0)
-    attn_out[...] = attn
-    lane = lax.broadcasted_iota(jnp.int32, attn.shape, 1)
-    square = square + 0.5 * small + jnp.sum(jnp.where(lane < half, 1.0, 0.5) * attn * attn)
+    square = square + 0.5 * small
+    for i in range(2):
+        attn_scatter.arrive(2, i)
+        attn = attn_scatter.last(i)
+        attn_out[i] = attn
+        lane = lax.broadcasted_iota(jnp.int32, attn.shape, 1)
+        square = square + jnp.sum(jnp.where(lane < half, 1.0, 0.5) * attn * attn)
     value = jnp.broadcast_to(square, norm_out.shape)
     norm_out[...] = all_sum(place, value, norm_src, norm_box, norm_send, norm_recv)
     for copy in stores:
@@ -773,9 +808,9 @@
     images = own_tok // PATCH
     cut = (wide // 4 + LANES - 1) // LANES * LANES
     spare = 2 * LANES
-    block, ada_block, attn_block = block_rows(rows, 2), block_rows(rows, 2), block_rows(rows, parts)
+    block, ada_block, attn_block = block_rows(rows, 2), block_rows(rows, 2), block_rows(rows, parts // 2)
     tok = 2 * own_tok
-    tile = TILE if count <= 16 else TILE // 2
+    tile, lag = (TILE, 2) if count <= 16 else (TILE // 2, 0)
     vmem = pl.BlockSpec(memory_space=pltpu.VMEM)
     hbm = pl.BlockSpec(memory_space=pl.ANY)
     hops = depth + 2 * side - 3
@@ -783,19 +818,25 @@
     def sems(*shape):
         return pltpu.SemaphoreType.DMA(shape)
 
-    def box(slots, height, lanes):
-        return pltpu.VMEM((slots, count - 1, height, lanes), bf16)
+    def boxes(slots, order, height, lanes):
+        size = {"z": depth, "a": side, "b": side}
+        span = size[order[0]] * size[order[1]]
+        first = (size[order[2]] - 1) * span
+        return [
+            pltpu.VMEM((slots, first, height, lanes), bf16),
+            pltpu.VMEM((min(slots, SLOTS), span - 1, height, lanes), bf16),
+        ]
 
     one = hidden * CUT_ONE // CUT_ALL // LANES * LANES
     two = hidden - one
 
     return pl.pallas_call(
-        functools.partial(block_kernel, count, rows, experts, tile),
+        functools.partial(block_kernel, count, rows, experts, tile, lag),
         out_shape=(
             jax.ShapeDtypeStruct((own_tok, width), f32),
             jax.ShapeDtypeStruct((own_tok, width), f32),
             jax.ShapeDtypeStruct((rows, wide), f32),
-            jax.ShapeDtypeStruct((attn_block, spare), f32),
+            jax.ShapeDtypeStruct((2, attn_block, spare), f32),
             jax.ShapeDtypeStruct((wide_experts, block, hidden), f32),
             jax.ShapeDtypeStruct((8, LANES), f32),
         ),
@@ -804,15 +845,15 @@
         scratch_shapes=[
             pltpu.VMEM((wide_experts, count, block, one), bf16),
             pltpu.VMEM((wide_experts, count, block, two), bf16),
-            box(SLOTS, block, one),
-            box(SLOTS, block, two),
+            *boxes(SLOTS + 2 * lag, ZBA, block, one),
+            *boxes(SLOTS + 2 * lag, BZA, block, two),
             pltpu.VMEM((1, count, ada_block, cut), bf16),
             pltpu.VMEM((1, count, SUB, width), bf16),
             pltpu.VMEM((1, count, SUB, cut), bf16),
             pltpu.VMEM((count, SUB, cut), bf16),
-            pltpu.VMEM((1, count, attn_block, spare), bf16),
-            box(1, attn_block, spare),
-            pltpu.VMEM((count, attn_block, spare), bf16),
+            pltpu.VMEM((2, count, attn_block, spare), bf16),
+            *boxes(2, ZBA, attn_block, spare),
+            pltpu.VMEM((2, count, attn_block, spare), bf16),
             pltpu.VMEM((2, parts, width, spare), bf16),
             pltpu.VMEM(condition.shape, bf16),
             pltpu.VMEM((2, condition.shape[0], 2 * cut), f32),
@@ -841,9 +882,10 @@
             pltpu.VMEM((depth + 2 * side * side, 8, LANES), f32),
             sems(4),
             *[sems(wide_experts, hops)] * 8,
-            *[sems(1, hops)] * 10,
-            sems(8),
-            sems(8),
+            *[sems(1, hops)] * 6,
+            *[sems(2, hops)] * 4,
+            sems(10),
+            sems(10),
             sems(images, 3),
             sems(images, 3),
             sems(depth + 2 * side * side),
@@ -855,13 +897,34 @@
         ),
         name="block",
     )(tokens, cotangent, condition, routes, w_ada, w_gate, w_attn, w_expert)
-def update_kernel(rows, half, output_ref, grad_tok_ref, norm_ref, expert_ref, attn_ref, ada_ref, *refs):
-    ada, gate, attn, expert = (refs[3 * i : 3 * i + 3] for i in range(4))
-    outs, hold, sem = refs[12:-2], refs[-2], refs[-1]
+def update_kernel(rows, half, output_ref, grad_tok_ref, expert_w, expert_m, expert_v, expert_ref, norm_ref, attn_ref, ada_ref, *refs):
+    ada, gate, attn = (refs[3 * i : 3 * i + 3] for i in range(3))
+    outs, (hold, held, grads, sem, token_sem) = refs[9:-5], refs[-5:]
     ada_new, gate_new, attn_new, expert_new = (outs[3 * i : 3 * i + 3] for i in range(4))
-    loads = [pltpu.make_async_copy(ref, hold.at[i], sem.at[i]) for i, ref in enumerate((output_ref, grad_tok_ref))]
-    stores = [pltpu.make_async_copy(hold.at[i], outs[13 + i], sem.at[2 + i]) for i in range(2)]
-    for copy in loads:
+    expert = (expert_w, expert_m, expert_v)
+    many = expert_w.shape[1] // 2
+    chunks = [(part, h) for h in range(2) for part in range(2)]
+    grad_loads = [
+        pltpu.make_async_copy(expert_ref.at[pl.ds(h * many, many)], grads.at[pl.ds(h * many, many)], token_sem.at[4 + h])
+        for h in range(2)
+    ]
+
+    def moves(c, refs, back):
+        part, h = chunks[c]
+        made = []
+        for i, ref in enumerate(refs):
+            far, near = ref.at[part, pl.ds(h * many, many)], held.at[i, part, pl.ds(h * many, many)]
+            made.append(pltpu.make_async_copy(*((near, far) if back else (far, near)), sem.at[int(back), c, i]))
+        return made
+
+    for c in range(4):
+        if chunks[c][0] == 0:
+            grad_loads[chunks[c][1]].start()
+        for copy in moves(c, expert, False):
+            copy.start()
+    token_loads = [pltpu.make_async_copy(ref, hold.at[i], token_sem.at[i]) for i, ref in enumerate((output_ref, grad_tok_ref))]
+    token_stores = [pltpu.make_async_copy(hold.at[i], outs[13 + i], token_sem.at[2 + i]) for i in range(2)]
+    for copy in token_loads:
         copy.start()
     total = jnp.sqrt(norm_ref[...])
     outs[12][0, 0] = jnp.max(total)
@@ -873,24 +936,36 @@
 
     everything = (slice(None), slice(None))
     write(ada, ada_new, everything, ada_ref[...])
-    for load, store in zip(loads, stores):
-        load.wait()
-        store.start()
     first = half // LANES * LANES
-    small = attn_ref[pl.ds(0, rows), pl.ds(first, LANES)]
+    small = attn_ref[0, pl.ds(0, rows), pl.ds(first, LANES)]
     square = jnp.concatenate([small, jnp.zeros((LANES - rows, LANES), f32)], axis=0).T
     experts = gate[0].shape[0]
     write(gate, gate_new, everything, square[half - first : half - first + experts, :rows])
-    for j in range(attn[0].shape[0]):
-        write(attn, attn_new, (j,), attn_ref[pl.ds(j * rows, rows), pl.ds(0, half)])
-
-    def one(e, carry):
-        for part in range(2):
-            write(expert, expert_new, (part, e), expert_ref[e, pl.ds(part * rows, rows), :])
-        return carry
-
-    lax.fori_loop(0, expert[0].shape[1], one, 0)
-    for copy in stores:
+    parts = attn[0].shape[0]
+    for j in range(parts):
+        grad = attn_ref[j // (parts // 2), pl.ds(j % (parts // 2) * rows, rows), pl.ds(0, half)]
+        write(attn, attn_new, (j,), grad)
+    here = [held.at[i] for i in range(3)]
+    for c, (part, h) in enumerate(chunks):
+        if part == 0:
+            grad_loads[h].wait()
+        for copy in moves(c, expert, False):
+            copy.wait()
+
+        def one(e, carry):
+            write(here, here, (part, e), grads[e, pl.ds(part * rows, rows), :])
+            return carry
+
+        lax.fori_loop(h * many, (h + 1) * many, one, 0)
+        for copy in moves(c, expert_new, True):
+            copy.start()
+    for load, store in zip(token_loads, token_stores):
+        load.wait()
+        store.start()
+    for c in range(4):
+        for copy in moves(c, expert_new, True):
+            copy.wait()
+    for copy in token_stores:
         copy.wait()
 
 
@@ -903,12 +978,18 @@
         out_shape=shapes
         + [jax.ShapeDtypeStruct((1, 1), f32)]
         + [jax.ShapeDtypeStruct(output.shape, f32), jax.ShapeDtypeStruct(grad_tokens.shape, f32)],
-        in_specs=[hbm, hbm] + [vmem] * (4 + len(weights)),
-        out_specs=[vmem] * len(weights) + [pl.BlockSpec(memory_space=pltpu.SMEM), hbm, hbm],
-        scratch_shapes=[pltpu.VMEM((2, *output.shape), f32), pltpu.SemaphoreType.DMA((4,))],
+        in_specs=[hbm] * 6 + [vmem] * (3 + 9),
+        out_specs=[vmem] * 9 + [hbm] * 3 + [pl.BlockSpec(memory_space=pltpu.SMEM), hbm, hbm],
+        scratch_shapes=[
+            pltpu.VMEM((2, *output.shape), f32),
+            pltpu.VMEM((3, *weights[9].shape), f32),
+            pltpu.VMEM(expert.shape, f32),
+            pltpu.SemaphoreType.DMA((2, 4, 3)),
+            pltpu.SemaphoreType.DMA((6,)),
+        ],
         compiler_params=pltpu.CompilerParams(vmem_limit_bytes=VMEM_BYTES),
         name="update",
-    )(output, grad_tokens, norm, expert, attn, ada, *weights)
+    )(output, grad_tokens, *weights[9:], expert, norm, attn, ada, *weights[:9])
 
 
 def per_device(

time: 297 us -> 280 us (0.943)
  Pallas kernels: 296 us -> 279 us
    pallas_call x1, Pallas kernels: 287 us -> 271 us  [block_call(): pl.pallas_call(functools.partial(block_kernel, count, rows, experts, tile...]
where the time goes in v4:
time: 280 us
  Pallas kernels  279 us (100%)
    pallas_call x1, Pallas kernels, block_call(): pl.pallas_call(functools.partial(block_kernel, count, rows, experts, tile...  271 us
    pallas_call x1, Pallas kernels, update_call(): pl.pallas_call(functools.partial(update_kernel, rows, half), out_shape=sh...  8.14 us

profile of v4, /device:TPU:0, one launch (start us, length us, event | category | flops | bytes accessed | tf_op | source)
XLA Modules:
  0.0 279.6 jit_solution(7070913527095656395)
XLA Ops:
  0.6 270.7 %block.1 = (f32[1024,384]{1,0:T(8,128)}, f32[1024,384]{1,0:T(8,128)}, f32[24,2304]{1,0:T(8,128)}, f32[2,48,256]{2,1,0:T(8,128)}, f32[10,48,768]{2,1,0:T(8,128)}, /*index=5*/f32[8,128]{1,0:T(8,128)}) custom-call(f32[1024,384]{1,0:T(8,128)} %tok_ref.1, f32[1024,384]{1,0:T(8,128)} %cot_ref.1, f32[8,384]{1,0:T(8,128)} %cond_ref.1, s32[2,2048]{1,0:T(2,128)} %bitcast.12, ...), custom_call_target="tpu_custom_call" | custom-call | flops 72477573120 | bytes 5898240 | tf_op jit(solution)/shard_map/block/pallas_call | solution.py:833
  271.3 8.1 %update.1 = (f32[24,2304]{1,0:T(8,128)}, f32[24,2304]{1,0:T(8,128)}, f32[24,2304]{1,0:T(8,128)}, f32[8,24]{1,0:T(8,128)}, f32[8,24]{1,0:T(8,128)}, /*index=5*/f3...) custom-call(f32[1024,384]{1,0:T(8,128)} %get-tuple-element.36.output, ...), custom_call_target="tpu_custom_call" | custom-call | tf_op jit(solution)/shard_map/update/pallas_call | solution.py:976

commit v5 on v4

--- a/solution.py
+++ b/solution.py
@@ -14,7 +14,7 @@
 LANES = 128
 SUB = 16
 TILE = 512
-SLOTS = 4
+SLOTS, REST = 4, 4
 ZBA, BZA = "zba", "bza"
 CUT_ONE, CUT_ALL = 2, 3
 
@@ -100,6 +100,12 @@
                 self.others[order, stage] = [
                     self.slot_at(order, {**fixed, axis: self.along(axis, k)}) for k in range(1, self.size[axis])
                 ]
+        z = self.at["z"]
+        self.line = self.depth == 4
+        self.end = (z == 0) | (z == 3)
+        self.next_end = jnp.where(z < 2, 0, 3)
+        self.inside = jnp.where(z < 2, 1, 2)
+        self.far_end = 3 - self.next_end
 
     def slot_at(self, order, at):
         slot = 0
@@ -160,8 +166,9 @@
 
 
 class Gather:
-    def __init__(self, place, buf, send, recv, order=ZBA):
+    def __init__(self, place, buf, send, recv, order=ZBA, relay=False):
         self.p, self.buf, self.send, self.recv, self.order = place, buf, send, recv, order
+        self.relayed = relay and place.line
 
     def copies(self, stage, e):
         p, order = self.p, self.order
@@ -172,29 +179,60 @@
             for k, peer in enumerate(p.near[order[stage]])
         ]
 
+    def passed(self, e):
+        p, order = self.p, self.order
+        stage = order.index("z")
+        base = sum(p.size[axis] - 1 for axis in order[:stage])
+        fixed = {name: p.at[name] for name in order[stage:]}
+        src = self.buf.at[e, pl.ds(p.slot_at(order, {**fixed, "z": p.far_end}), span(p, order, stage))]
+        extra = sum(size - 1 for size in p.size.values())
+        recv = self.recv.at[e, base + jnp.where(p.next_end == 0, 0, 2)]
+        return remote(src, src, self.send.at[e, extra], recv, p.device({**p.at, "z": p.next_end}))
+
+    def each(self, stage, e, act):
+        for k, copy in enumerate(self.copies(stage, e)):
+            if self.relayed and self.order[stage] == "z" and k != 1:
+                pl.when(self.p.at["z"] != (3 if k == 0 else 0))(functools.partial(act, copy))
+            else:
+                act(copy)
+
     def start(self, stage, e):
-        for copy in self.copies(stage, e):
-            copy.start()
+        self.each(stage, e, lambda copy: copy.start())
+
+    def relay(self, e):
+        if self.relayed:
+
+            @pl.when(~self.p.end)
+            def _():
+                self.copies(self.order.index("z"), e)[1].wait_recv()
+                self.passed(e).start()
 
     def arrive(self, stage, e):
-        for copy in self.copies(stage, e):
-            copy.wait_recv()
+        for k, copy in enumerate(self.copies(stage, e)):
+            if self.relayed and self.order[stage] == "z" and k == 1:
+                pl.when(self.p.end)(copy.wait_recv)
+            else:
+                copy.wait_recv()
 
     def sent(self, e):
         for stage in range(3):
-            for copy in self.copies(stage, e):
-                copy.wait_send()
+            self.each(stage, e, lambda copy: copy.wait_send())
+        if self.relayed:
+            pl.when(~self.p.end)(lambda: self.passed(e).wait_send())
 
 
 class Scatter:
-    def __init__(self, place, buf, boxes, send, recv, order=ZBA):
+    def __init__(self, place, buf, boxes, send, recv, order=ZBA, relay=False):
         self.p, self.buf, self.boxes, self.send, self.recv, self.order = place, buf, boxes, send, recv, order
+        self.relayed = relay and place.line
 
     def box(self, stage, e, block, many):
         box = self.boxes[min(stage, 1)]
-        if stage == 2:
+        if stage >= 2:
             order = self.order
             block = block + (self.p.size[order[1]] - 1) * span(self.p, order, 1)
+        if stage == 3:
+            block = block + self.p.size[self.order[0]] - 1
         return box.at[e % box.shape[0], pl.ds(block, many)]
 
     def copies(self, stage, e):
@@ -208,20 +246,62 @@
             made.append(remote(src, dst, self.send.at[e, sem + k], self.recv.at[e, sem + k], peer))
         return made
 
+    def passed(self, e):
+        p, order = self.p, self.order
+        at = order.index("z")
+        many = span(p, order, at)
+        fixed = {name: p.at[name] for name in order[at:]}
+        src = self.buf.at[e, pl.ds(p.slot_at(order, {**fixed, "z": p.far_end}), many)]
+        extra = sum(size - 1 for size in p.size.values())
+        peer = p.device({**p.at, "z": p.inside})
+        return remote(src, self.box(3, e, 0, many), self.send.at[e, extra], self.recv.at[e, extra], peer)
+
+    def on_line(self, stage):
+        return self.relayed and self.order[2 - stage] == "z"
+
     def start(self, stage, e):
-        for copy in self.copies(stage, e):
-            copy.start()
+        for k, copy in enumerate(self.copies(stage, e)):
+            if self.on_line(stage):
+                here = self.p.end if k == 1 else self.p.at["z"] != (3 if k == 0 else 0)
+                pl.when(here)(copy.start)
+            else:
+                copy.start()
+        if self.on_line(stage):
+            pl.when(self.p.end)(lambda: self.passed(e).start())
+
+    def relay(self, e):
+        if self.relayed:
+            stage = 2 - self.order.index("z")
+            many = span(self.p, self.order, 2 - stage)
+
+            @pl.when(~self.p.end)
+            def _():
+                self.passed(e).wait_recv()
+                to = self.p.others[self.order, 2 - stage][1]
+                for i in range(many):
+                    total = self.buf[e, to + i].astype(f32) + self.box(3, e, i, 1)[0].astype(f32)
+                    self.buf[e, to + i] = total.astype(bf16)
+                self.copies(stage, e)[1].start()
 
     def arrive(self, stage, e):
-        for copy in self.copies(stage, e):
-            copy.wait()
+        for k, copy in enumerate(self.copies(stage, e)):
+            if self.on_line(stage) and k != 1:
+                pl.when(self.p.at["z"] != (3 if k == 0 else 0))(copy.wait_send)
+                pl.when(self.p.at["z"] != (0 if k == 0 else 3))(copy.wait_recv)
+            else:
+                copy.wait()
+        if self.on_line(stage):
+            pl.when(self.p.end)(lambda: self.passed(e).wait_send())
 
     def total(self, stage, e, i):
         p, order = self.p, self.order
         many = span(p, order, 2 - stage)
         total = self.buf[e, p.first[order, 2 - stage] + i].astype(f32)
         for k in range(p.size[order[2 - stage]] - 1):
-            total = total + self.box(stage, e, k * many + i, 1)[0].astype(f32)
+            term = self.box(stage, e, k * many + i, 1)[0].astype(f32)
+            if self.on_line(stage) and k != 1:
+                term = jnp.where(p.at["z"] != (0 if k == 0 else 3), term, 0.0)
+            total = total + term
         return total
 
     def add(self, stage, e):
@@ -292,27 +372,6 @@
     return total
 
 
-class Both:
-    def __init__(self, *both):
-        self.both = both
-
-    def start(self, stage, e):
-        for one in self.both:
-            one.start(stage, e)
-
-    def arrive(self, stage, e):
-        for one in self.both:
-            one.arrive(stage, e)
-
-    def add(self, stage, e):
-        for one in self.both:
-            one.add(stage, e)
-
-    def sent(self, e):
-        for one in self.both:
-            one.sent(e)
-
-
 def block_kernel(
     count, rows, experts, tile, lag,
     tok_ref, cot_ref, cond_ref, route_ref, ada_ref, gate_ref, attn_ref, w_ref,
@@ -377,13 +436,13 @@
     attn_gather = Gather(place, attn_buf, attn_send, attn_recv)
     cuts = (pl.ds(0, buf_one.shape[3]), pl.ds(buf_one.shape[3], buf_two.shape[3]))
     streams = tuple(zip((buf_one, buf_two), cuts, (ZBA, BZA)))
-    gather = Both(
-        Gather(place, buf_one, gather_send, gather_recv, ZBA),
-        Gather(place, buf_two, gather_send_two, gather_recv_two, BZA),
+    gathers = (
+        Gather(place, buf_one, gather_send, gather_recv, ZBA, True),
+        Gather(place, buf_two, gather_send_two, gather_recv_two, BZA, True),
     )
-    scatter = Both(
-        Scatter(place, buf_one, (box_one, rest_one), scatter_send, scatter_recv, ZBA),
-        Scatter(place, buf_two, (box_two, rest_two), scatter_send_two, scatter_recv_two, BZA),
+    scatters = (
+        Scatter(place, buf_one, (box_one, rest_one), scatter_send, scatter_recv, ZBA, True),
+        Scatter(place, buf_two, (box_two, rest_two), scatter_send_two, scatter_recv_two, BZA, True),
     )
     sc_gather = Gather(place, sc_buf, sc_send, sc_recv)
     ada_gather.start(0, 0)
@@ -399,32 +458,34 @@
 
     lax.fori_loop(0, wide_experts, fill, 0)
 
+    def begin(e):
+        for one in gathers:
+            one.start(0, e)
+
+    def onward(stage, e):
+        for one in gathers:
+            one.arrive(stage, e)
+            one.start(stage + 1, e)
+
     def tick(k):
-        @pl.when(k + 5 < wide_experts)
-        def _():
-            gather.start(0, k + 5)
-
-        @pl.when(k + 3 < wide_experts)
-        def _():
-            gather.arrive(0, k + 3)
-            gather.start(1, k + 3)
-
-        @pl.when(k + 1 < wide_experts)
-        def _():
-            gather.arrive(1, k + 1)
-            gather.start(2, k + 1)
+        pl.when(k + 5 < wide_experts)(lambda: begin(k + 5))
+        pl.when(k + 4 < wide_experts)(lambda: gathers[0].relay(k + 4))
+        pl.when(k + 3 < wide_experts)(lambda: onward(0, k + 3))
+        pl.when(k + 2 < wide_experts)(lambda: gathers[1].relay(k + 2))
+        pl.when(k + 1 < wide_experts)(lambda: onward(1, k + 1))
 
     grad_mod[...] = jnp.zeros_like(grad_mod)
-    gather.start(0, 0)
-    gather.start(0, 1)
     for stage in range(2):
         for small, i in ((ada_gather, 0), (attn_gather, 0), (attn_gather, 1)):
             small.arrive(stage, i)
             small.start(stage + 1, i)
-    gather.start(0, 2)
-    gather.start(0, 3)
-    gather.arrive(0, 0)
-    gather.start(1, 0)
+        if stage == 0:
+            begin(0)
+            begin(1)
+    begin(2)
+    begin(3)
+    gathers[0].relay(0)
+    onward(0, 0)
     ada_gather.arrive(2, 0)
 
     low_cut = pl.ds(0, cut)
@@ -454,8 +515,10 @@
         outs = [attn_w.at[1 - mp, j] for j in range(i * pair, (i + 1) * pair)]
         blocks_to_weights(place, rows, attn_far.at[i], 1 - mp, outs)
     mod_cross.wait()
-    gather.arrive(0, 1)
-    gather.start(1, 1)
+    gathers[0].relay(1)
+    onward(0, 1)
+    gathers[0].relay(2)
+    gathers[1].relay(0)
     gate_lanes = pl.ds(first, LANES)
     half_lanes = pl.ds(0, half)
 
@@ -601,36 +664,38 @@
 
         lax.fori_loop(0, tiles, one_tile, 0)
 
-    def put_total(e):
-        for part, (_, lanes, _) in zip(scatter.both, streams):
-            total_ref[e, :, lanes] = part.last(e)
+    def follow(one, stage, e):
+        one.arrive(stage, e)
+        one.add(stage, e)
+        one.start(stage + 1, e)
+
+    def finish(e):
+        for one, (_, lanes, _) in zip(scatters, streams):
+            one.arrive(2, e)
+            total_ref[e, :, lanes] = one.last(e)
 
     def collect(k):
-        @pl.when((k >= 1) & (k - 1 < wide_experts))
-        def _():
-            scatter.arrive(0, k - 1)
-            scatter.add(0, k - 1)
-            scatter.start(1, k - 1)
-
-        @pl.when((k >= 2) & (k - 2 < wide_experts))
-        def _():
-            scatter.arrive(1, k - 2)
-            scatter.add(1, k - 2)
-            scatter.start(2, k - 2)
-
-        @pl.when((k >= 3) & (k - 3 < wide_experts))
-        def _():
-            scatter.arrive(2, k - 3)
-            put_total(k - 3)
+        def at(late, act):
+            pl.when((k >= late) & (k - late < wide_experts))(lambda: act(k - late))
+
+        at(4, finish)
+        at(3, scatters[0].relay)
+        at(3, lambda e: follow(scatters[1], 1, e))
+        at(2, lambda e: follow(scatters[0], 1, e))
+        at(2, scatters[1].relay)
+        at(1, lambda e: [follow(one, 0, e) for one in scatters] and None)
 
     def step(e, carry):
         tick(e + ahead)
-        gather.arrive(2, e)
+        for one in gathers:
+            one.arrive(2, e)
         compute(e)
-        gather.sent(e)
+        for one in gathers:
+            one.sent(e)
         for buf, lanes, order in streams:
             grads_to_blocks(place, rows, (up_grad.at[:, lanes], down_grad.at[:, lanes]), buf.at[e], order)
-        scatter.start(0, e)
+        for one in scatters:
+            one.start(0, e)
         collect(e - lag)
         return carry
 
@@ -689,12 +754,14 @@
         add_grad_mod(image, 0, jnp.sum(grad_h_one, axis=0, keepdims=True))
         add_grad_mod(image, 1, jnp.sum(grad_h_one * normed, axis=0, keepdims=True))
         grad_h_acc[own_rows, :] = grad_x + norm_back(grad_h_one * (1.0 + mod_row(image, 1)), normed, inverse)
-        collect(wide_experts - lag + image)
+
+        @pl.when(image > 0)
+        def _():
+            collect(wide_experts - lag + image - 1)
+
         return carry
 
     lax.fori_loop(0, images, backward, 0)
-    for k in range(images, 3 + lag):
-        collect(wide_experts - lag + k)
     stores = [
         pltpu.make_async_copy(branch_acc.at[own], output_ref, load_sem.at[2]),
         pltpu.make_async_copy(grad_h_acc.at[own], grad_tok_ref, load_sem.at[3]),
@@ -749,13 +816,18 @@
         grads_to_blocks(place, rows, grads, attn_buf.at[i])
         attn_scatter.start(0, i)
     mod_gather.start(0, 0)
+    left = list(range(wide_experts - lag + images - 1, wide_experts + 4))
     for stage in range(2):
+        if len(left) > 1:
+            collect(left.pop(0))
         for i in range(2):
             attn_scatter.arrive(stage, i)
             attn_scatter.add(stage, i)
             attn_scatter.start(stage + 1, i)
         mod_gather.arrive(stage, 0)
         mod_gather.start(stage + 1, 0)
+    for k in left:
+        collect(k)
     square = jnp.zeros((1, 1), f32)
     for e in range(wide_experts):
         square = square + jnp.sum(total_ref[e] * total_ref[e])
@@ -822,9 +894,10 @@
         size = {"z": depth, "a": side, "b": side}
         span = size[order[0]] * size[order[1]]
         first = (size[order[2]] - 1) * span
+        extra = 0 if slots <= 2 else math.prod(size[axis] for axis in order[: order.index("z")])
         return [
             pltpu.VMEM((slots, first, height, lanes), bf16),
-            pltpu.VMEM((min(slots, SLOTS), span - 1, height, lanes), bf16),
+            pltpu.VMEM((min(slots, REST), span - 1 + extra, height, lanes), bf16),
         ]
 
     one = hidden * CUT_ONE // CUT_ALL // LANES * LANES
@@ -881,7 +954,7 @@
             pltpu.VMEM((2, 8, LANES), f32),
             pltpu.VMEM((depth + 2 * side * side, 8, LANES), f32),
             sems(4),
-            *[sems(wide_experts, hops)] * 8,
+            *[sems(wide_experts, hops + 1)] * 8,
             *[sems(1, hops)] * 6,
             *[sems(2, hops)] * 4,
             sems(10),

time: 280 us -> 261 us (0.932)
  Pallas kernels: 279 us -> 260 us
    pallas_call x1, Pallas kernels: 271 us -> 251 us  [block_call(): pl.pallas_call(functools.partial(block_kernel, count, rows, experts, tile...]
where the time goes in v5:
time: 261 us; the launch traced here: 260 us
  Pallas kernels  260 us (100%)
    pallas_call x1, Pallas kernels, block_call(): pl.pallas_call(functools.partial(block_kernel, count, rows, experts, tile...  251 us
    pallas_call x1, Pallas kernels, update_call(): pl.pallas_call(functools.partial(update_kernel, rows, half), out_shape=sh...  8.14 us

profile of v5, /device:TPU:0, one launch (start us, length us, event | category | flops | bytes accessed | tf_op | source)
XLA Modules:
  0.0 260.3 jit_solution(10125063707611593752)
XLA Ops:
  0.6 251.4 %block.1 = (f32[1024,384]{1,0:T(8,128)}, f32[1024,384]{1,0:T(8,128)}, f32[24,2304]{1,0:T(8,128)}, f32[2,48,256]{2,1,0:T(8,128)}, f32[10,48,768]{2,1,0:T(8,128)}, /*index=5*/f32[8,128]{1,0:T(8,128)}) custom-call(f32[1024,384]{1,0:T(8,128)} %tok_ref.1, f32[1024,384]{1,0:T(8,128)} %cot_ref.1, f32[8,384]{1,0:T(8,128)} %cond_ref.1, s32[2,2048]{1,0:T(2,128)} %bitcast.12, ...), custom_call_target="tpu_custom_call" | custom-call | flops 72477573120 | bytes 5898240 | tf_op jit(solution)/shard_map/block/pallas_call | solution.py:906
  252.0 8.1 %update.1 = (f32[24,2304]{1,0:T(8,128)}, f32[24,2304]{1,0:T(8,128)}, f32[24,2304]{1,0:T(8,128)}, f32[8,24]{1,0:T(8,128)}, f32[8,24]{1,0:T(8,128)}, /*index=5*/f3...) custom-call(f32[1024,384]{1,0:T(8,128)} %get-tuple-element.36.output, ...), custom_call_target="tpu_custom_call" | custom-call | tf_op jit(solution)/shard_map/update/pallas_call | solution.py:1049

commit v6 on v5

--- a/solution.py
+++ b/solution.py
@@ -16,7 +16,7 @@
 TILE = 512
 SLOTS, REST = 4, 4
 ZBA, BZA = "zba", "bza"
-CUT_ONE, CUT_ALL = 2, 3
+CUT_ONE, CUT_ALL = 1, 2
 
 EPS_NORM = 1e-06
 CLIP_NORM = 0.1
@@ -58,7 +58,7 @@
     second_new = BETA_TWO * second + (1.0 - BETA_TWO) * grad * grad
     fix_one = 1.0 - BETA_ONE**STEP
     fix_two = 1.0 - BETA_TWO**STEP
-    update = first_new / fix_one / (jnp.sqrt(second_new / fix_two) + ADAM_EPS) + DECAY * master
+    update = first_new * (1.0 / fix_one) / (jnp.sqrt(second_new * (1.0 / fix_two)) + ADAM_EPS) + DECAY * master
     return (master - RATE * update, first_new, second_new)
 
 
@@ -148,11 +148,11 @@
         return peers
 
     def greet(self):
-        peers = self.peers("z") + self.peers_layer()
+        peers = self.near["z"] + self.peers_layer()
         barrier = pltpu.get_barrier_semaphore()
         for peer in peers:
             pl.semaphore_signal(barrier, inc=1, device_id=peer, device_id_type=MESH)
-        pl.semaphore_wait(barrier, len(peers))
+        return lambda: pl.semaphore_wait(barrier, len(peers))
 
 
 def remote(src, dst, send, recv, peer):
@@ -377,16 +377,17 @@
     tok_ref, cot_ref, cond_ref, route_ref, ada_ref, gate_ref, attn_ref, w_ref,
     output_ref, grad_tok_ref, ada_out, attn_out, total_ref, norm_out,
     buf_one, buf_two, box_one, rest_one, box_two, rest_two,
-    ada_buf, sc_buf, mod_buf, mod_far, attn_buf, attn_box, attn_rest, attn_far, attn_w,
-    cond_low, mod, grad_mod, grad_mod_in, triple, mixed, h_one, soft,
+    ada_one, ada_two, sc_buf, mod_buf, mod_far, attn_buf, attn_box, attn_rest, attn_far, attn_w,
+    cond_low, mod_one, mod_two, grad_mod, grad_mod_in, triple, mixed, h_one, soft,
     h_all, d_all, gate_all, branch_acc, grad_h_acc, grad_gate_acc, gate_in, share_in,
     up_w, down_w, up_grad, down_grad, gate_grad, attn_share, attn_in, norm_src, norm_box,
     load_sem, gather_send, gather_recv, gather_send_two, gather_recv_two,
     scatter_send, scatter_recv, scatter_send_two, scatter_recv_two,
-    ada_send, ada_recv, sc_send, sc_recv, mod_send, mod_recv, attn_send, attn_recv, attn_back_send, attn_back_recv,
+    ada_send, ada_recv, more_send, more_recv, sc_send, sc_recv, mod_send, mod_recv, attn_send, attn_recv, attn_back_send, attn_back_recv,
     core_send, core_recv, token_send, token_recv, norm_send, norm_recv,
 ):
     place = Place(count)
+    met = place.greet()
     mp = place.mp
     wide_experts = w_ref.shape[1]
     own_tok, width = tok_ref.shape
@@ -395,7 +396,7 @@
     first = half // LANES * LANES
     heads = half // HD
     wide = ada_ref.shape[1] // 2
-    cut = ada_buf.shape[3]
+    cut = mod_buf.shape[3]
     scale = HD ** (-0.5)
     own_at = pl.multiple_of(mp * own_tok, own_tok)
     their_at = pl.multiple_of((1 - mp) * own_tok, own_tok)
@@ -414,9 +415,9 @@
             target[place.slot(order)] = jnp.zeros(target.shape[1:], bf16)
         target[place.slot(order), pl.ds(0, block.shape[0])] = block
 
-    cols = ada_ref[:, pl.ds(pl.multiple_of(mp * wide, LANES), wide)]
-    tail = jnp.concatenate([cols[:, cut:], jnp.zeros((rows, 2 * cut - wide), f32)], axis=1)
-    put(ada_buf.at[0], jnp.concatenate([cols[:, :cut], tail], axis=0).astype(bf16))
+    put(ada_one.at[0], ada_ref[:, pl.ds(pl.multiple_of(mp * width, LANES), width)].astype(bf16))
+    cols = ada_ref[:, pl.ds(pl.multiple_of((1 + mp) * 2 * width, LANES), 2 * width)]
+    put(ada_two.at[0], jnp.concatenate([cols[:, :width], cols[:, width:]], axis=0).astype(bf16))
     parts = attn_ref.shape[0]
     side_by = lax.broadcasted_iota(jnp.int32, (experts, LANES), 1) == lax.broadcasted_iota(
         jnp.int32, (experts, LANES), 0
@@ -431,8 +432,9 @@
     cond = cond / (1.0 + jnp.exp(-cond))
     cond_low[...] = cond.astype(bf16)
     sc_buf[0, place.slot()] = jnp.concatenate([cond, jnp.zeros((SUB - cond.shape[0], width), f32)], axis=0).astype(bf16)
-    place.greet()
-    ada_gather = Gather(place, ada_buf, ada_send, ada_recv)
+    met()
+    ada_gather = Gather(place, ada_one, ada_send, ada_recv)
+    more_gather = Gather(place, ada_two, more_send, more_recv)
     attn_gather = Gather(place, attn_buf, attn_send, attn_recv)
     cuts = (pl.ds(0, buf_one.shape[3]), pl.ds(buf_one.shape[3], buf_two.shape[3]))
     streams = tuple(zip((buf_one, buf_two), cuts, (ZBA, BZA)))
@@ -448,6 +450,7 @@
     ada_gather.start(0, 0)
     attn_gather.start(0, 0)
     attn_gather.start(0, 1)
+    more_gather.start(0, 0)
     sc_gather.start(0, 0)
 
     def fill(e, carry):
@@ -468,32 +471,37 @@
             one.start(stage + 1, e)
 
     def tick(k):
-        pl.when(k + 5 < wide_experts)(lambda: begin(k + 5))
+        pl.when(k + 6 < wide_experts)(lambda: begin(k + 6))
         pl.when(k + 4 < wide_experts)(lambda: gathers[0].relay(k + 4))
         pl.when(k + 3 < wide_experts)(lambda: onward(0, k + 3))
-        pl.when(k + 2 < wide_experts)(lambda: gathers[1].relay(k + 2))
-        pl.when(k + 1 < wide_experts)(lambda: onward(1, k + 1))
+        pl.when(k + 1 < wide_experts)(lambda: gathers[1].relay(k + 1))
+        pl.when((k >= 0) & (k < wide_experts))(lambda: onward(1, k))
 
     grad_mod[...] = jnp.zeros_like(grad_mod)
-    for stage in range(2):
-        for small, i in ((ada_gather, 0), (attn_gather, 0), (attn_gather, 1)):
-            small.arrive(stage, i)
-            small.start(stage + 1, i)
-        if stage == 0:
-            begin(0)
-            begin(1)
-    begin(2)
-    begin(3)
-    gathers[0].relay(0)
-    onward(0, 0)
+    items = ((ada_gather, 0), (attn_gather, 0), (attn_gather, 1), (more_gather, 0))
+
+    def wave(w):
+        for i in (w, w - 1):
+            if 0 <= i < len(items):
+                small, which = items[i]
+                small.arrive(w - i, which)
+                small.start(w - i + 1, which)
+
+    for w in range(len(items)):
+        wave(w)
+    begin(0)
+    begin(1)
+    width_lanes = pl.ds(0, width)
     ada_gather.arrive(2, 0)
 
-    low_cut = pl.ds(0, cut)
-    blocks_to_weights(place, rows, ada_buf.at[0], mp, (up_w.at[:, low_cut], down_w.at[:, low_cut]))
-    mod[mp, :, pl.ds(0, cut)] = mxu(cond_low[...], up_w[:, low_cut])
-    mod[mp, :, pl.ds(cut, cut)] = mxu(cond_low[...], down_w[:, low_cut])
-    mod_cross = remote(mod.at[mp], mod.at[mp], core_send.at[1], core_recv.at[1], other)
-    mod_cross.start()
+    blocks_to_weights(place, rows, ada_one.at[0], mp, (up_w.at[:, width_lanes],))
+    mod_one[mp] = mxu(cond_low[...], up_w[:, width_lanes])
+    mod_cross = [
+        remote(ref.at[mp], ref.at[mp], core_send.at[i], core_recv.at[i], other)
+        for i, ref in ((1, mod_one), (0, mod_two))
+    ]
+    mod_cross[0].start()
+    wave(len(items))
     attn_cross = []
     for i in range(2):
         attn_gather.arrive(2, i)
@@ -508,17 +516,21 @@
     ada_gather.sent(0)
     attn_gather.sent(0)
     attn_gather.sent(1)
+    begin(2)
+    begin(3)
+    begin(4)
+    gathers[0].relay(0)
+    onward(0, 0)
     sc_gather.arrive(0, 0)
     sc_gather.start(1, 0)
     for i in range(2):
         attn_cross[i].wait()
         outs = [attn_w.at[1 - mp, j] for j in range(i * pair, (i + 1) * pair)]
         blocks_to_weights(place, rows, attn_far.at[i], 1 - mp, outs)
-    mod_cross.wait()
+    mod_cross[0].wait()
     gathers[0].relay(1)
     onward(0, 1)
     gathers[0].relay(2)
-    gathers[1].relay(0)
     gate_lanes = pl.ds(first, LANES)
     half_lanes = pl.ds(0, half)
 
@@ -531,8 +543,10 @@
     expert_lane = lax.broadcasted_iota(jnp.int32, (PATCH, LANES), 1) - (half - first)
 
     def mod_row(image, vector):
-        flat = vector % 3 * width
-        return mod[vector // 3, pl.ds(mp * images + image, 1), pl.ds(flat, width)]
+        row = pl.ds(mp * images + image, 1)
+        if vector < 2:
+            return mod_one[vector, row, :]
+        return mod_two[vector // 2 - 1, row, pl.ds(vector % 2 * width, width)]
 
     def add_grad_mod(image, vector, value):
         grad_mod[vector // 3, pl.ds(mp * images + image, 1), pl.ds(vector % 3 * width, width)] = value
@@ -560,10 +574,8 @@
             for i, ref in enumerate((h_all, d_all, gate_all))
         ]
 
-    def forward(image, carry):
+    def attention(image, carry):
         at = pl.ds(pl.multiple_of(image * PATCH, PATCH), PATCH)
-        cot_at = pl.ds(pl.multiple_of(own_tok + image * PATCH, PATCH), PATCH)
-        all_at = pl.ds(pl.multiple_of(own_at + image * PATCH, PATCH), PATCH)
         normed, _ = layer_norm(branch_acc[at, :])
         h = (normed * (1.0 + mod_row(image, 1)) + mod_row(image, 0)).astype(bf16)
         h_one[at, :] = h
@@ -581,6 +593,28 @@
                     soft[image, core * heads + group[0] + head] = low
                     total = total + mxu(low, one_head(value, group, head))
                 mixed[core, at, lanes] = total.astype(bf16)
+        tick(image - 1)
+
+        @pl.when(image == 0)
+        def _():
+            sc_gather.arrive(1, 0)
+            sc_gather.start(2, 0)
+
+        return carry
+
+    lax.fori_loop(0, images, attention, 0)
+    more_gather.arrive(2, 0)
+    blocks_to_weights(place, rows, ada_two.at[0], mp, (up_w.at[:, width_lanes], down_w.at[:, width_lanes]))
+    mod_two[mp, :, pl.ds(0, width)] = mxu(cond_low[...], up_w[:, width_lanes])
+    mod_two[mp, :, pl.ds(width, width)] = mxu(cond_low[...], down_w[:, width_lanes])
+    mod_cross[1].start()
+    more_gather.sent(0)
+    mod_cross[1].wait()
+
+    def forward(image, carry):
+        at = pl.ds(pl.multiple_of(image * PATCH, PATCH), PATCH)
+        cot_at = pl.ds(pl.multiple_of(own_tok + image * PATCH, PATCH), PATCH)
+        all_at = pl.ds(pl.multiple_of(own_at + image * PATCH, PATCH), PATCH)
         x_one = branch_acc[at, :] + mod_row(image, 2) * attend(at)
         normed, _ = layer_norm(x_one)
         h = (normed * (1.0 + mod_row(image, 4)) + mod_row(image, 3)).astype(bf16)
@@ -591,13 +625,6 @@
         d_all[all_at, :] = (branch_acc[cot_at, :] * mod_row(image, 5)).astype(bf16)
         for copy in token_copies(image):
             copy.start()
-
-        tick(image - 1)
-
-        @pl.when(image == 0)
-        def _():
-            sc_gather.arrive(1, 0)
-            sc_gather.start(2, 0)
 
         return carry
 
@@ -778,7 +805,7 @@
             )
             for i in range(2)
         ],
-        remote(mod_buf.at[0], mod_far, core_send.at[0], core_recv.at[0], other),
+        remote(mod_buf.at[0], mod_far, core_send.at[1], core_recv.at[1], other),
     ]
     crosses[0].start()
 
@@ -920,7 +947,8 @@
             pltpu.VMEM((wide_experts, count, block, two), bf16),
             *boxes(SLOTS + 2 * lag, ZBA, block, one),
             *boxes(SLOTS + 2 * lag, BZA, block, two),
-            pltpu.VMEM((1, count, ada_block, cut), bf16),
+            pltpu.VMEM((1, count, block_rows(rows, 1), width), bf16),
+            pltpu.VMEM((1, count, ada_block, width), bf16),
             pltpu.VMEM((1, count, SUB, width), bf16),
             pltpu.VMEM((1, count, SUB, cut), bf16),
             pltpu.VMEM((count, SUB, cut), bf16),
@@ -929,7 +957,8 @@
             pltpu.VMEM((2, count, attn_block, spare), bf16),
             pltpu.VMEM((2, parts, width, spare), bf16),
             pltpu.VMEM(condition.shape, bf16),
-            pltpu.VMEM((2, condition.shape[0], 2 * cut), f32),
+            pltpu.VMEM((2, condition.shape[0], width), f32),
+            pltpu.VMEM((2, condition.shape[0], 2 * width), f32),
             pltpu.VMEM((2, condition.shape[0], 2 * cut), f32),
             pltpu.VMEM((condition.shape[0], 2 * cut), f32),
             pltpu.VMEM((2, 3, own_tok, half), bf16),
@@ -955,7 +984,7 @@
             pltpu.VMEM((depth + 2 * side * side, 8, LANES), f32),
             sems(4),
             *[sems(wide_experts, hops + 1)] * 8,
-            *[sems(1, hops)] * 6,
+            *[sems(1, hops)] * 8,
             *[sems(2, hops)] * 4,
             sems(10),
             sems(10),

time: 261 us -> 256 us (0.981)
  Pallas kernels: 260 us -> 255 us
    pallas_call x1, Pallas kernels: 251 us -> 247 us  [block_call(): pl.pallas_call(functools.partial(block_kernel, count, rows, experts, tile...]
where the time goes in v6:
time: 256 us
  Pallas kernels  255 us (100%)
    pallas_call x1, Pallas kernels, block_call(): pl.pallas_call(functools.partial(block_kernel, count, rows, experts, tile...  247 us
    pallas_call x1, Pallas kernels, update_call(): pl.pallas_call(functools.partial(update_kernel, rows, half), out_shape=sh...  8.14 us

profile of v6, /device:TPU:0, one launch (start us, length us, event | category | flops | bytes accessed | tf_op | source)
XLA Modules:
  0.0 255.8 jit_solution(5063521455641005679)
XLA Ops:
  0.6 246.8 %block.1 = (f32[1024,384]{1,0:T(8,128)}, f32[1024,384]{1,0:T(8,128)}, f32[24,2304]{1,0:T(8,128)}, f32[2,48,256]{2,1,0:T(8,128)}, f32[10,48,768]{2,1,0:T(8,128)}, /*index=5*/f32[8,128]{1,0:T(8,128)}) custom-call(f32[1024,384]{1,0:T(8,128)} %tok_ref.1, f32[1024,384]{1,0:T(8,128)} %cot_ref.1, f32[8,384]{1,0:T(8,128)} %cond_ref.1, s32[2,2048]{1,0:T(2,128)} %bitcast.12, ...), custom_call_target="tpu_custom_call" | custom-call | flops 72477573120 | bytes 5898240 | tf_op jit(solution)/shard_map/block/pallas_call | solution.py:933
  247.5 8.1 %update.1 = (f32[24,2304]{1,0:T(8,128)}, f32[24,2304]{1,0:T(8,128)}, f32[24,2304]{1,0:T(8,128)}, f32[8,24]{1,0:T(8,128)}, f32[8,24]{1,0:T(8,128)}, /*index=5*/f3...) custom-call(f32[1024,384]{1,0:T(8,128)} %get-tuple-element.36.output, ...), custom_call_target="tpu_custom_call" | custom-call | tf_op jit(solution)/shard_map/update/pallas_call | solution.py:1078

commit v7 on v6

--- a/solution.py
+++ b/solution.py
@@ -16,7 +16,7 @@
 TILE = 512
 SLOTS, REST = 4, 4
 ZBA, BZA = "zba", "bza"
-CUT_ONE, CUT_ALL = 1, 2
+CUT_ONE, CUT_ALL = 2, 3
 
 EPS_NORM = 1e-06
 CLIP_NORM = 0.1
@@ -381,7 +381,7 @@
     cond_low, mod_one, mod_two, grad_mod, grad_mod_in, triple, mixed, h_one, soft,
     h_all, d_all, gate_all, branch_acc, grad_h_acc, grad_gate_acc, gate_in, share_in,
     up_w, down_w, up_grad, down_grad, gate_grad, attn_share, attn_in, norm_src, norm_box,
-    load_sem, gather_send, gather_recv, gather_send_two, gather_recv_two,
+    w_hold, load_sem, gather_send, gather_recv, gather_send_two, gather_recv_two,
     scatter_send, scatter_recv, scatter_send_two, scatter_recv_two,
     ada_send, ada_recv, more_send, more_recv, sc_send, sc_recv, mod_send, mod_recv, attn_send, attn_recv, attn_back_send, attn_back_recv,
     core_send, core_recv, token_send, token_recv, norm_send, norm_recv,
@@ -407,6 +407,8 @@
         pltpu.make_async_copy(tok_ref, branch_acc.at[pl.ds(0, own_tok)], load_sem.at[0]),
         pltpu.make_async_copy(cot_ref, branch_acc.at[pl.ds(own_tok, own_tok)], load_sem.at[1]),
     ]
+    w_load = pltpu.make_async_copy(w_ref, w_hold, load_sem.at[2])
+    w_load.start()
     for load in loads:
         load.start()
 
@@ -454,11 +456,12 @@
     sc_gather.start(0, 0)
 
     def fill(e, carry):
-        both = jnp.concatenate([w_ref[0, e], w_ref[1, e]], axis=0).astype(bf16)
+        both = jnp.concatenate([w_hold[0, e], w_hold[1, e]], axis=0).astype(bf16)
         for buf, lanes, order in streams:
             put(buf.at[e], both[:, lanes.start : lanes.start + lanes.size], order)
         return carry
 
+    w_load.wait()
     lax.fori_loop(0, wide_experts, fill, 0)
 
     def begin(e):
@@ -474,7 +477,7 @@
         pl.when(k + 6 < wide_experts)(lambda: begin(k + 6))
         pl.when(k + 4 < wide_experts)(lambda: gathers[0].relay(k + 4))
         pl.when(k + 3 < wide_experts)(lambda: onward(0, k + 3))
-        pl.when(k + 1 < wide_experts)(lambda: gathers[1].relay(k + 1))
+        pl.when(k + 2 < wide_experts)(lambda: gathers[1].relay(k + 2))
         pl.when((k >= 0) & (k < wide_experts))(lambda: onward(1, k))
 
     grad_mod[...] = jnp.zeros_like(grad_mod)
@@ -531,6 +534,7 @@
     gathers[0].relay(1)
     onward(0, 1)
     gathers[0].relay(2)
+    gathers[1].relay(0)
     gate_lanes = pl.ds(first, LANES)
     half_lanes = pl.ds(0, half)
 
@@ -727,6 +731,17 @@
         return carry
 
     lax.fori_loop(0, wide_experts, step, 0)
+
+    row = lax.broadcasted_iota(jnp.int32, (width, LANES), 0)
+    lane = lax.broadcasted_iota(jnp.int32, (width, LANES), 1)
+    pick = ((row == place.dp * rows + lane) & (lane < rows)).astype(f32).astype(bf16)
+    group = cond_ref.shape[0]
+
+    def in_order(ref, core, at):
+        pieces = [ref[place.slot_of(dp, core)].astype(f32)[at : at + group] for dp in range(count)]
+        return jnp.concatenate(pieces, axis=0).astype(bf16)
+
+    conds = mxu(in_order(sc_buf.at[0], mp, 0), pick).astype(bf16)
 
     gate_grad[...] = jnp.zeros_like(gate_grad)
     for copy in shares + loads:
@@ -860,17 +875,6 @@
         square = square + jnp.sum(total_ref[e] * total_ref[e])
     mod_gather.arrive(2, 0)
     crosses[3].start()
-    row = lax.broadcasted_iota(jnp.int32, (width, LANES), 0)
-    lane = lax.broadcasted_iota(jnp.int32, (width, LANES), 1)
-    pick = ((row == place.dp * rows + lane) & (lane < rows)).astype(f32).astype(bf16)
-    group = cond_ref.shape[0]
-
-    def in_order(ref, core, at):
-        pieces = [ref[place.slot_of(dp, core)].astype(f32)[at : at + group] for dp in range(count)]
-        return jnp.concatenate(pieces, axis=0).astype(bf16)
-
-    conds = mxu(in_order(sc_buf.at[0], mp, 0), pick).astype(bf16)
-
     def ada_grad(ref, core):
         low = mxu(conds, in_order(ref, core, 0), TN)[:rows]
         high = mxu(conds, in_order(ref, core, group), TN)[:rows, : wide - cut]
@@ -940,7 +944,7 @@
             jax.ShapeDtypeStruct((wide_experts, block, hidden), f32),
             jax.ShapeDtypeStruct((8, LANES), f32),
         ),
-        in_specs=[hbm, hbm] + [vmem] * 6,
+        in_specs=[hbm, hbm] + [vmem] * 5 + [hbm],
         out_specs=(hbm, hbm) + (vmem,) * 4,
         scratch_shapes=[
             pltpu.VMEM((wide_experts, count, block, one), bf16),
@@ -982,6 +986,7 @@
             pltpu.VMEM((parts, width, spare), bf16),
             pltpu.VMEM((2, 8, LANES), f32),
             pltpu.VMEM((depth + 2 * side * side, 8, LANES), f32),
+            pltpu.VMEM(w_expert.shape, f32),
             sems(4),
             *[sems(wide_experts, hops + 1)] * 8,
             *[sems(1, hops)] * 8,

time: 256 us -> 254 us (level)
  no operation moved by 1% of the time
where the time goes in v7:
time: 254 us; the launch traced here: 253 us
  Pallas kernels  253 us (100%)
    pallas_call x1, Pallas kernels, block_call(): pl.pallas_call(functools.partial(block_kernel, count, rows, experts, tile...  244 us
    pallas_call x1, Pallas kernels, update_call(): pl.pallas_call(functools.partial(update_kernel, rows, half), out_shape=sh...  8.14 us

profile of v7, /device:TPU:0, one launch (start us, length us, event | category | flops | bytes accessed | tf_op | source)
XLA Modules:
  0.0 253.4 jit_solution(2005126324058967514)
XLA Ops:
  0.6 244.5 %block.1 = (f32[1024,384]{1,0:T(8,128)}, f32[1024,384]{1,0:T(8,128)}, f32[24,2304]{1,0:T(8,128)}, f32[2,48,256]{2,1,0:T(8,128)}, f32[10,48,768]{2,1,0:T(8,128)}, /*index=5*/f32[8,128]{1,0:T(8,128)}) custom-call(f32[1024,384]{1,0:T(8,128)} %tok_ref.1, f32[1024,384]{1,0:T(8,128)} %cot_ref.1, f32[8,384]{1,0:T(8,128)} %cond_ref.1, s32[2,2048]{1,0:T(2,128)} %bitcast.12, ...), custom_call_target="tpu_custom_call" | custom-call | flops 72477573120 | bytes 5898240 | tf_op jit(solution)/shard_map/block/pallas_call | solution.py:937
  245.1 8.1 %update.1 = (f32[24,2304]{1,0:T(8,128)}, f32[24,2304]{1,0:T(8,128)}, f32[24,2304]{1,0:T(8,128)}, f32[8,24]{1,0:T(8,128)}, f32[8,24]{1,0:T(8,128)}, /*index=5*/f3...) custom-call(f32[1024,384]{1,0:T(8,128)} %get-tuple-element.36.output, ...), custom_call_target="tpu_custom_call" | custom-call | tf_op jit(solution)/shard_map/update/pallas_call | solution.py:1083

commit v8 on v7

--- a/solution.py
+++ b/solution.py
@@ -381,7 +381,7 @@
     cond_low, mod_one, mod_two, grad_mod, grad_mod_in, triple, mixed, h_one, soft,
     h_all, d_all, gate_all, branch_acc, grad_h_acc, grad_gate_acc, gate_in, share_in,
     up_w, down_w, up_grad, down_grad, gate_grad, attn_share, attn_in, norm_src, norm_box,
-    w_hold, load_sem, gather_send, gather_recv, gather_send_two, gather_recv_two,
+    w_hold, total_hold, load_sem, gather_send, gather_recv, gather_send_two, gather_recv_two,
     scatter_send, scatter_recv, scatter_send_two, scatter_recv_two,
     ada_send, ada_recv, more_send, more_recv, sc_send, sc_recv, mod_send, mod_recv, attn_send, attn_recv, attn_back_send, attn_back_recv,
     core_send, core_recv, token_send, token_recv, norm_send, norm_recv,
@@ -703,7 +703,7 @@
     def finish(e):
         for one, (_, lanes, _) in zip(scatters, streams):
             one.arrive(2, e)
-            total_ref[e, :, lanes] = one.last(e)
+            total_hold[e, :, lanes] = one.last(e)
 
     def collect(k):
         def at(late, act):
@@ -870,9 +870,11 @@
         mod_gather.start(stage + 1, 0)
     for k in left:
         collect(k)
+    stores.append(pltpu.make_async_copy(total_hold, total_ref, load_sem.at[4]))
+    stores[-1].start()
     square = jnp.zeros((1, 1), f32)
     for e in range(wide_experts):
-        square = square + jnp.sum(total_ref[e] * total_ref[e])
+        square = square + jnp.sum(total_hold[e] * total_hold[e])
     mod_gather.arrive(2, 0)
     crosses[3].start()
     def ada_grad(ref, core):
@@ -945,7 +947,7 @@
             jax.ShapeDtypeStruct((8, LANES), f32),
         ),
         in_specs=[hbm, hbm] + [vmem] * 5 + [hbm],
-        out_specs=(hbm, hbm) + (vmem,) * 4,
+        out_specs=(hbm, hbm, vmem, vmem, hbm, vmem),
         scratch_shapes=[
             pltpu.VMEM((wide_experts, count, block, one), bf16),
             pltpu.VMEM((wide_experts, count, block, two), bf16),
@@ -987,7 +989,8 @@
             pltpu.VMEM((2, 8, LANES), f32),
             pltpu.VMEM((depth + 2 * side * side, 8, LANES), f32),
             pltpu.VMEM(w_expert.shape, f32),
-            sems(4),
+            pltpu.VMEM((wide_experts, block, hidden), f32),
+            sems(5),
             *[sems(wide_experts, hops + 1)] * 8,
             *[sems(1, hops)] * 8,
             *[sems(2, hops)] * 4,

time: 254 us -> 253 us (level)
  no operation moved by 1% of the time
where the time goes in v8:
time: 253 us
  Pallas kernels  252 us (100%)
    pallas_call x1, Pallas kernels, block_call(): pl.pallas_call(functools.partial(block_kernel, count, rows, experts, tile...  244 us
    pallas_call x1, Pallas kernels, update_call(): pl.pallas_call(functools.partial(update_kernel, rows, half), out_shape=sh...  8.14 us

profile of v8, /device:TPU:0, one launch (start us, length us, event | category | flops | bytes accessed | tf_op | source)
XLA Modules:
  0.0 253.0 jit_solution(4353766880631691315)
XLA Ops:
  0.6 244.0 %block.1 = (f32[1024,384]{1,0:T(8,128)}, f32[1024,384]{1,0:T(8,128)}, f32[24,2304]{1,0:T(8,128)}, f32[2,48,256]{2,1,0:T(8,128)}, f32[10,48,768]{2,1,0:T(8,128)}, /*index=5*/f32[8,128]{1,0:T(8,128)}) custom-call(f32[1024,384]{1,0:T(8,128)} %tok_ref.1, f32[1024,384]{1,0:T(8,128)} %cot_ref.1, f32[8,384]{1,0:T(8,128)} %cond_ref.1, s32[2,2048]{1,0:T(2,128)} %bitcast.12, ...), custom_call_target="tpu_custom_call" | custom-call | flops 72477573120 | bytes 5898240 | tf_op jit(solution)/shard_map/block/pallas_call | solution.py:939
  244.7 8.1 %update.1 = (f32[24,2304]{1,0:T(8,128)}, f32[24,2304]{1,0:T(8,128)}, f32[24,2304]{1,0:T(8,128)}, f32[8,24]{1,0:T(8,128)}, f32[8,24]{1,0:T(8,128)}, /*index=5*/f3...) custom-call(f32[1024,384]{1,0:T(8,128)} %get-tuple-element.36.output, ...), custom_call_target="tpu_custom_call" | custom-call | tf_op jit(solution)/shard_map/update/pallas_call | solution.py:1086
